TPU v7x, 32 devices: a whole 2x2x4 slice. The times are simulated.
32 devices in a mesh: parts: 2 (over x), expert: 4 (over z), hidden: 4 (over y, core).
Axes of the slice: x: 2, y: 2, z: 4, core: 2. Of those that a mesh axis runs over, the one named last changes fastest.
Arguments:
- tokens: bfloat16 [512, 3072], P(('parts', 'expert', 'hidden')), parts along dimension 0, may hold values from -6 to 6
- grad_out: bfloat16 [512, 3072], P(('parts', 'expert', 'hidden')), parts along dimension 0, may hold values from -6 to 6
- routes: int32 [512, 2], P(('parts', 'expert', 'hidden')), parts along dimension 0, may hold values from 0 to 3, all different within a row; in each aligned block of 16 rows (0 to 15, 16 to 31, ...) at most 12 rows name the same one
- w_router: bfloat16 [3072, 4], replicated, may hold values from -0.109375 to 0.109375
- w_gate: bfloat16 [4, 3072, 8192], P('expert', None, 'hidden'), may hold values from -0.109375 to 0.109375
- w_up: bfloat16 [4, 3072, 8192], P('expert', None, 'hidden'), may hold values from -0.109375 to 0.109375
- w_down: bfloat16 [4, 8192, 3072], P('expert', 'hidden'), may hold values from -0.0625 to 0.0625
Outputs:
- input_grad: bfloat16 [512, 3072], P(('parts', 'expert', 'hidden')), parts along dimension 0
- logit_grad: float32 [512, 2], P(('parts', 'expert', 'hidden')), parts along dimension 0
There are 2 independent parts, one for each index of `parts`. A program takes and returns all parts, laid end to end along the dimension named above; an argument that names none is the same for every part. Nothing has to cross between parts.
Inputs may be any that keep to these rules, and one draw needn't show every extreme that they name: `routes`: the 2 experts of a row differ; the rows of one device name each expert at most 12 times, a bound that some block reaches.
All inputs are finite; a program needn't handle non-finite values.
Results may differ from a plain program's by a relative error of at most 0.005.
Values may be sent and summed in bfloat16 or wider, within the bound.
No kernel may reach another device: no remote copies, remote signals or barrier semaphores. Data moves between devices by JAX's collectives and lax.ppermute only.
A program may use at most 128 MiB of HBM per device.

v0:
```python
import jax
import jax.numpy as jnp
from jax import lax
from jax.sharding import PartitionSpec as P

TOP = 2


def slot_tables(route_rows, experts, capacity):
    tok_count = route_rows.shape[0]
    flat = route_rows.reshape(tok_count * TOP)
    labels = jnp.arange(experts, dtype=jnp.int32)
    onehot = (flat[:, None] == labels).astype(jnp.int32)
    before = jnp.cumsum(onehot, axis=0) - onehot
    place = jnp.sum(before * onehot, axis=1)
    slots = flat * capacity + place
    column = jnp.arange(experts * capacity, dtype=jnp.int32)
    match = slots[None, :] == column[:, None]
    table = jnp.any(match.reshape(experts * capacity, tok_count, TOP), axis=2).astype(jnp.bfloat16)
    return (table, slots)


def shards(tokens, grad_out, routes, w_router, w_gate, w_up, w_down):
    tok_count = tokens.shape[0]
    width = tokens.shape[1]
    experts = w_router.shape[1]
    capacity = 3 * tok_count * TOP // (2 * experts)
    stacked = jnp.stack([tokens, grad_out])
    table, slot_own = slot_tables(routes, experts, capacity)
    outgoing = jnp.einsum("st,xtd->xsd", table, stacked, preferred_element_type=jnp.float32)
    outgoing = outgoing.astype(jnp.bfloat16).reshape(2, experts, capacity, width)
    arrived = lax.all_to_all(outgoing, "expert", split_axis=1, concat_axis=1, tiled=True)
    gathered = lax.all_gather(arrived, "hidden", axis=1, tiled=True)
    rows = gathered.reshape(2, -1, width)
    x_rows = rows[0]
    dy_rows = rows[1]
    gate_local = w_gate[0]
    up_local = w_up[0]
    gate = jnp.dot(x_rows, gate_local, preferred_element_type=jnp.float32)
    up = jnp.dot(x_rows, up_local, preferred_element_type=jnp.float32)
    back = jnp.einsum("rd,fd->rf", dy_rows, w_down[0], preferred_element_type=jnp.float32)
    sig = jax.nn.sigmoid(gate)
    silu = gate * sig
    score = jnp.sum(silu * up * back, axis=1)
    d_gate = (back * up * sig * (1.0 + gate * (1.0 - sig))).astype(jnp.bfloat16)
    d_up = (back * silu).astype(jnp.bfloat16)
    partial_value = jnp.einsum("rf,df->rd", d_gate, gate_local, preferred_element_type=jnp.float32)
    partial_value = partial_value + jnp.einsum(
        "rf,df->rd", d_up, up_local, preferred_element_type=jnp.float32
    )
    summed, sum_scores = (
        lax.psum_scatter(partial_value, "hidden", scatter_dimension=0, tiled=True),
        lax.psum_scatter(score, "hidden", scatter_dimension=0, tiled=True),
    )
    returned, ret_scores = (
        lax.all_to_all(
            summed.reshape(experts, capacity, width),
            "expert",
            split_axis=0,
            concat_axis=0,
            tiled=True,
        ),
        lax.all_to_all(
            sum_scores.reshape(experts, capacity), "expert", split_axis=0, concat_axis=0, tiled=True
        ),
    )
    route_back = returned.reshape(experts * capacity, width)[slot_own].reshape(
        tok_count, TOP, width
    )
    route_score = ret_scores.reshape(-1)[slot_own].reshape(tok_count, TOP)
    logits = jnp.dot(tokens, w_router, preferred_element_type=jnp.float32)
    chosen = jnp.take_along_axis(logits, routes, axis=1)
    prob = jax.nn.sigmoid(chosen - chosen[:, ::-1])
    logit_grad = prob[:, 0:1] * prob[:, 1:2] * (route_score - route_score[:, ::-1])
    labels = jnp.arange(experts, dtype=jnp.int32)
    onehot = (routes[:, :, None] == labels).astype(jnp.float32)
    spread = jnp.einsum("tk,tke->te", logit_grad, onehot)
    router_term = jnp.dot(spread, w_router.astype(jnp.float32).T, precision=lax.Precision.HIGHEST)
    input_grad = (jnp.sum(prob[:, :, None] * route_back, axis=1) + router_term).astype(jnp.bfloat16)
    return (input_grad, logit_grad)


def solution(mesh):
    placed = (
        P(("parts", "expert", "hidden"), None),
        P(("parts", "expert", "hidden"), None),
        P(("parts", "expert", "hidden"), None),
        P(),
        P("expert", None, "hidden"),
        P("expert", None, "hidden"),
        P("expert", "hidden", None),
    )
    return jax.shard_map(
        shards,
        mesh=mesh,
        in_specs=placed,
        out_specs=(P(("parts", "expert", "hidden"), None), P(("parts", "expert", "hidden"), None)),
        check_vma=False,
    )
```

profile of v0, /device:TPU:0, one launch (start us, length us, event | category | flops | bytes accessed | tf_op | source)
XLA Modules:
  0.0 178.4 jit_solution(11156169594830463576)
XLA Ops:
  7.2 0.0 copy-start
  7.2 0.0 all-gather.2.cloned.1.call-start
  7.2 0.7 broadcast_compare_fusion
  7.9 0.7 broadcast_add_fusion
  8.6 0.8 copy.49
  9.3 0.1 copy.47
  9.4 0.1 copy.48
  9.5 0.1 eq.42
  9.6 0.1 fusion.24
  9.7 0.1 reduce_window_sum.11
  9.7 0.2 select_reduce_fusion
  9.9 0.1 reduce_sum.32
  10.0 0.1 copy.54
  10.1 0.1 fusion.25
  10.2 1.3 fusion.13
  11.5 0.6 copy.55
  12.1 22.1 %all_to_all.19 = bf16[2,4,12,3072]{3,0,2,1:T(2,128)(2,1)} all-to-all(bf16[2,4,12,3072]{3,0,2,1:T(2,128)(2,1)S(1)} %bitcast.50), channel_id=1, replica_groups=mesh['parts'=2,'expert'=4,'hidden'=4] {'expert'}, dimensions={1} | all-to-all | bytes 1179648 | tf_op jit(solution)/shard_map/all_to_all | solution.py:32
  34.2 0.0 all-gather.2.cloned.1.call-update
  34.3 0.0 reduce-scatter.2.cloned.1.call-start
  34.3 23.3 %all-gather.2.cloned.1.call-done = bf16[2,16,12,3072]{3,0,2,1:T(2,128)(2,1)} async-done(((bf16[2,4,12,3072]{3,0,2,1:T(2,128)(2,1)}), bf16[2,16,12,3072]{3,0,2,1:T(2,128)(2,1)}) %all-gather.2.cloned.1.call-update) | async-done | bytes 2359312 | tf_op jit(solution)/shard_map/all_gather | solution.py:33
  57.6 11.9 %slice_reduce_fusion.1 = (bf16[16,12,3072]{2,1,0:T(8,128)(2,1)S(1)}, bf16[16,12,3072]{2,1,0:T(8,128)(2,1)S(1)}) fusion(bf16[2,16,12,3072]{3,0,2,1:T(2,128)(2,1)} %all-gather.2.cloned.1.call-done), kind=kLoop, calls=%fused_computation.19 | loop fusion | bytes 4718592 | tf_op jit(solution)/shard_map/slice | solution.py:36
  69.5 1.2 squeeze.15
  70.7 0.3 squeeze.17
  71.0 6.0 %fusion.2 = f32[192,2048]{1,0:T(8,128)S(1)} fusion(bf16[192,3072]{1,0:T(8,128)(2,1)S(1)} %squeeze.17, bf16[1,3072,2048]{2,1,0:T(8,128)(2,1)} %param.11), kind=kOutput, calls=%fused_computation.5 | convolution fusion | flops 2415919104 | bytes 15335424 | tf_op jit(solution)/shard_map/dot_general | solution.py:39
  77.1 6.1 %fusion.6 = f32[192,2048]{1,0:T(8,128)S(1)} fusion(bf16[192,3072]{1,0:T(8,128)(2,1)S(1)} %squeeze.17, bf16[1,3072,2048]{2,1,0:T(8,128)(2,1)} %param.12), kind=kOutput, calls=%fused_computation.9 | convolution fusion | flops 2415919104 | bytes 15335424 | tf_op jit(solution)/shard_map/dot_general | solution.py:40
  83.2 7.6 %multiply_reduce_fusion = (f32[192]{0:T(256)S(1)}, f32[192,2048]{1,0:T(8,128)S(1)}) fusion(f32[192,2048]{1,0:T(8,128)S(1)} %fusion.6, f32[192,2048]{1,0:T(8,128)S(1)} %fusion.2, bf16[192,3072]{1,0:T(8,128)(2,1)S(1)} %copy-done.1, bf16[1,2048,3072]{2,1,0:T(8,128)(2,1)} %param.13), kind=kOutput, calls=%fused_computation.20 | convolution fusion | flops 2418671360 | bytes 18481920 | tf_op jit(solution)/shard_map/rd,fd->rf/dot_general | solution.py:41
  90.8 8.0 %fusion = f32[192,3072]{1,0:T(8,128)S(1)} fusion(bf16[1,3072,2048]{2,1,0:T(8,128)(2,1)} %param.11, f32[192,2048]{1,0:T(8,128)S(1)} %fusion.2, f32[192,2048]{1,0:T(8,128)S(1)} %get-tuple-element.16, f32[192,2048]{1,0:T(8,128)S(1)} %fusion.6), kind=kOutput, calls=%fused_computation.3 | convolution fusion | flops 2419851264 | bytes 19660800 | tf_op jit(solution)/shard_map/rf,df->rd/dot_general | solution.py:47
  98.8 10.3 %fusion.10 = f32[192,3072]{1,0:T(8,128)} fusion(f32[192,3072]{1,0:T(8,128)S(1)} %fusion, bf16[1,3072,2048]{2,1,0:T(8,128)(2,1)} %param.12, f32[192,2048]{1,0:T(8,128)S(1)} %get-tuple-element.16, f32[192,2048]{1,0:T(8,128)S(1)} %fusion.2), kind=kOutput, calls=%fused_computation.13 | convolution fusion | flops 2418868224 | bytes 20447232 | tf_op jit(solution)/shard_map/rf,df->rd/dot_general | solution.py:48
  109.1 0.0 reduce-scatter.2.cloned.1.call-update
  109.1 0.1 copy.50
  109.2 0.1 mul.78
  109.3 0.1 copy.51
  109.4 0.1 reshape.113
  109.5 0.5 copy-done.2
  110.0 0.1 fusion.34
  110.1 0.8 gather_fusion.2
  110.9 0.1 reshape.116
  111.0 0.0 copy-done.3
  111.0 0.6 dynamic-slice
  112.2 5.9 %all-reduce = f32[192]{0:T(256)S(1)} all-reduce(f32[192]{0:T(256)S(1)} %get-tuple-element.15), channel_id=3, replica_groups=mesh['parts'=2,'expert'=4,'hidden'=4] {'hidden'}, use_global_device_ids=true, to_apply=%region_6.7.clone | all-reduce | flops 192 | bytes 1536
  118.1 0.1 dynamic-slice.1
  118.2 0.7 all_to_all.14
  118.9 4.8 %all-to-all-start.2 = ((f32[4,1,12]{2,1,0:T(1,128)}), f32[4,1,12]{2,1,0:T(1,128)S(1)}, u32[]{:S(2)}, u32[]{:S(2)}) async-start(f32[4,1,12]{2,1,0:T(1,128)} %bitcast.11), calls=%async_computation.3 | async-start | bytes 4096 | tf_op jit(solution)/shard_map/all_to_all | solution.py:63
  123.6 0.1 rev.6
  123.7 18.7 %reduce-scatter.2.cloned.1.call-done = f32[48,3072]{1,0:T(8,128)} async-done(((f32[192,3072]{1,0:T(8,128)}), f32[48,3072]{1,0:T(8,128)}) %reduce-scatter.2.cloned.1.call-update) | async-done | bytes 589840 | tf_op jit(solution)/shard_map/reduce_scatter | solution.py:52
  142.4 2.0 %reshape.92 = f32[4,12,3072]{2,1,0:T(8,128)} reshape(f32[48,3072]{1,0:T(8,128)} %reduce-scatter.2.cloned.1.call-done) | data formatting | bytes 1179648 | tf_op jit(solution)/shard_map/reshape | solution.py:57
  144.4 0.0 all-to-all-done.2
  144.4 4.6 %all-to-all-start.1 = ((f32[4,12,3072]{2,1,0:T(8,128)}), f32[4,12,3072]{2,1,0:T(8,128)S(1)}, u32[]{:S(2)}, u32[]{:S(2)}) async-start(f32[4,12,3072]{2,1,0:T(8,128)} %reshape.92), calls=%async_computation.2 | async-start | bytes 1572864 | tf_op jit(solution)/shard_map/all_to_all | solution.py:56
  149.0 0.2 fusion.26
  149.2 0.5 broadcast.103
  149.7 0.7 reduce.9
  150.4 0.1 reshape.95
  150.5 0.7 gather_fusion.1
  151.2 0.1 reshape.96
  151.3 0.1 rev.7
  151.3 0.1 subtract_multiply_fusion
  151.4 0.7 copy.58
  152.1 0.2 fusion.21
  152.3 16.8 %all-to-all-done.1 = f32[4,12,3072]{2,1,0:T(8,128)S(1)} async-done(((f32[4,12,3072]{2,1,0:T(8,128)}), f32[4,12,3072]{2,1,0:T(8,128)S(1)}, u32[]{:S(2)}, u32[]{:S(2)}) %all-to-all-start.1) | async-done | bytes 589856 | tf_op jit(solution)/shard_map/all_to_all | solution.py:56
  169.1 0.1 reshape.93
  169.2 0.7 gather_fusion
  169.9 0.2 reshape.94
  170.1 0.6 multiply_reduce_fusion.1
  170.6 0.9 fusion.14
  (11 shorter events, 0.1 us)
Async XLA Ops:
  7.2 102.3 %copy-start = (bf16[3072,4]{0,1:T(4,128)(2,1)S(1)}, bf16[3072,4]{0,1:T(4,128)(2,1)}, u32[]{:S(2)}) copy-start(bf16[3072,4]{0,1:T(4,128)(2,1)} %param.10) | copy-start | bytes 73732
  7.2 50.4 %all-gather.2.cloned.1.call-start = ((), (), s32[]{:S(2)}) async-start(), calls=%async_computation.4 | async-start | bytes 2949120 | tf_op jit(solution)/shard_map/all_gather | solution.py:33
  34.3 108.1 %reduce-scatter.2.cloned.1.call-start = ((), (), s32[]{:S(2)}) async-start(), calls=%async_computation.5 | async-start | bytes 2949120 | tf_op jit(solution)/shard_map/reduce_scatter | solution.py:52
  77.0 6.1 %copy-start.1 = (bf16[192,3072]{1,0:T(8,128)(2,1)S(1)}, bf16[192,3072]{1,0:T(8,128)(2,1)}, u32[]{:S(2)}) copy-start(bf16[192,3072]{1,0:T(8,128)(2,1)} %squeeze.15) | copy-start | bytes 3538948
  109.1 0.9 copy-start.2
  110.1 0.9 copy-start.3
  118.9 25.5 %all-to-all-start.2 = ((f32[4,1,12]{2,1,0:T(1,128)}), f32[4,1,12]{2,1,0:T(1,128)S(1)}, u32[]{:S(2)}, u32[]{:S(2)}) async-start(f32[4,1,12]{2,1,0:T(1,128)} %bitcast.11), calls=%async_computation.3 | async-start | bytes 4096 | tf_op jit(solution)/shard_map/all_to_all | solution.py:63
  144.4 24.7 %all-to-all-start.1 = ((f32[4,12,3072]{2,1,0:T(8,128)}), f32[4,12,3072]{2,1,0:T(8,128)S(1)}, u32[]{:S(2)}, u32[]{:S(2)}) async-start(f32[4,12,3072]{2,1,0:T(8,128)} %reshape.92), calls=%async_computation.2 | async-start | bytes 1572864 | tf_op jit(solution)/shard_map/all_to_all | solution.py:56
Sparse Core Ops, SparseCore 0:
  34.4 23.1 all-gather.1
  109.2 33.0 reduce-scatter.1
where the time goes:
time: 179 us; the launch traced here: 178 us
  waiting for transfers between devices  58.8 us (33%)
  matrix products  40.5 us (23%)
  blocking collectives  28 us (16%)
  local copies, waits for them, and re-layouts  23.4 us (13%)
  between operations  14.9 us (8%)
  starting transfers between devices  9.43 us (5%)
  other arithmetic  3.29 us (2%)
    all_gather x1, waiting for transfers between devices, shards(): gathered = lax.all_gather(arrived, 'hidden', axis=1, tiled=True)  23.3 us
    all_to_all x1, blocking collectives, shards(): lax.all_to_all(outgoing, 'expert', split_axis=1, concat_axis=1, tiled=True)  22.1 us
    reduce_scatter x1, waiting for transfers between devices, shards(): lax.psum_scatter(partial_value, 'hidden', scatter_dimension=0, tiled=True)  18.7 us
    all_to_all x1, waiting for transfers between devices, shards(): lax.all_to_all(summed.reshape(experts, capacity, width), 'expert', split_...  16.8 us
    slice x1, local copies, waits for them, and re-layouts, shards(): dy_rows = rows[1]  11.9 us
    dot_general x1, matrix products, shards(): jnp.einsum('rf,df->rd', d_up, up_local, preferred_element_type=jnp.float32)  10.3 us
    dot_general x1, matrix products, shards(): jnp.einsum('rf,df->rd', d_gate, gate_local, preferred_element_type=jnp.fl...  7.95 us
    dot_general x1, matrix products, shards(): jnp.einsum('rd,fd->rf', dy_rows, w_down[0], preferred_element_type=jnp.fl...  7.6 us
  transfers between devices with their start and end apart: 4, of which 3 were waited for; matrix products, arithmetic and copies ran while one was open for 4% of the time, Pallas kernels for 0%

commit v1 on v0

v1 whole, which is shorter than its diff:
```python
import functools

import jax
import jax.numpy as jnp
from jax import lax
from jax.experimental import pallas as pl
from jax.experimental.pallas import tpu as pltpu
from jax.sharding import PartitionSpec as P

BF = jnp.bfloat16
F32 = jnp.float32
LANES = 128
ROWS = 256
AHEAD = 3
NT = (((1,), (1,)), ((), ()))
ANY = pl.BlockSpec(memory_space=pl.ANY)
VMEM = pl.BlockSpec(memory_space=pltpu.VMEM)


def dot_nt(a, b):
    return lax.dot_general(a, b, NT, preferred_element_type=F32)


def chunk(extent, wanted):
    size = min(extent, wanted)
    while extent % size:
        size -= LANES
    return size


def fetch(pieces, held, sems):
    copies, at = [], 0
    for i, piece in enumerate(pieces):
        rows = piece.shape[0]
        copies.append(pltpu.make_async_copy(piece, held.at[pl.ds(at, rows)], sems.at[i]))
        at += rows
    for copy in copies:
        copy.start()
    for copy in copies:
        copy.wait()


def load_kernel(n, *refs):
    sources, target, sems = refs[:n], refs[n], refs[n + 1]
    copies = [pltpu.make_async_copy(a, target.at[i], sems.at[i]) for i, a in enumerate(sources)]
    for copy in copies:
        copy.start()
    for copy in copies:
        copy.wait()


def gate_up_kernel(n, *refs):
    pieces, (w_both, both, held, sems) = refs[:n], refs[n:]
    w_gate, w_up, gate, up = w_both.at[0], w_both.at[1], both.at[0], both.at[1]
    fetch(pieces, held, sems)
    rows, ff = gate.shape
    block, step = min(rows, ROWS), chunk(ff, 512)

    @pl.loop(0, rows // block)
    def _(r):
        at = pl.ds(pl.multiple_of(r * block, block), block)

        @pl.loop(0, ff // step)
        def _(f):
            cols = pl.ds(pl.multiple_of(f * step, step), step)
            gate[at, cols] = jnp.dot(held[at, :], w_gate[:, cols], preferred_element_type=F32)
            up[at, cols] = jnp.dot(held[at, :], w_up[:, cols], preferred_element_type=F32)


def split3(score):
    high = score.astype(BF)
    rest = score - high.astype(F32)
    mid = rest.astype(BF)
    low = (rest - mid.astype(F32)).astype(BF)
    lane = lax.broadcasted_iota(jnp.int32, (score.shape[0], LANES), 1)
    spread = [jnp.broadcast_to(t.astype(F32), lane.shape) for t in (high, mid, low)]
    out = jnp.where(lane == 0, spread[0], jnp.where(lane == 1, spread[1], spread[2]))
    return jnp.where(lane < 3, out, 0.0).astype(BF)


def join3(tail):
    return jnp.sum(tail.astype(F32), axis=1, keepdims=True)


def back_kernel(n, *refs):
    pieces = refs[:n]
    w_gate, w_up, w_down, both, keep, send = refs[n : n + 6]
    held, d_gate, d_up, score, v_gate, v_up, v_down, sems, down_sems, sum_sems = refs[n + 6 :]
    gate, up = both.at[0], both.at[1]
    rows, ff = gate.shape
    width = held.shape[1]
    block, step, dstep = min(rows, ROWS), chunk(ff, 512), chunk(width, 512)
    half = rows // 2

    def load_down(f):
        part = pl.ds(pl.multiple_of(f * step, step), step)
        return pltpu.make_async_copy(w_down.at[part], v_down.at[part], down_sems.at[f])

    def load_sum(d, k):
        part = pl.ds(pl.multiple_of(d * dstep, dstep), dstep)
        source, target = ((w_gate, v_gate), (w_up, v_up))[k]
        return pltpu.make_async_copy(source.at[part], target.at[part], sum_sems.at[k, d])

    downs, sums = ff // step, width // dstep

    def start(i):
        @pl.when(i < downs)
        def _():
            load_down(i).start()

        @pl.when((i >= downs) & (i < downs + sums))
        def _():
            load_sum(i - downs, 0).start()
            load_sum(i - downs, 1).start()

    load_down(0).start()
    fetches, at = [], 0
    for i, piece in enumerate(pieces):
        fetches.append(pltpu.make_async_copy(piece, held.at[pl.ds(at, piece.shape[0])], sems.at[i]))
        at += piece.shape[0]
    for copy in fetches:
        copy.start()
    for i in range(1, AHEAD):
        start(i)
    for copy in fetches:
        copy.wait()

    @pl.loop(0, rows // block)
    def _(r):
        at = pl.ds(pl.multiple_of(r * block, block), block)
        score[at, :] = jnp.zeros((block, 1), F32)

        @pl.loop(0, ff // step)
        def _(f):
            cols = pl.ds(pl.multiple_of(f * step, step), step)

            @pl.when(r == 0)
            def _():
                load_down(f).wait()
                start(f + AHEAD)

            back = dot_nt(held[at, :], v_down[cols, :])
            g, u = gate[at, cols], up[at, cols]
            sig = jax.nn.sigmoid(g)
            silu = g * sig
            score[at, :] += jnp.sum(silu * u * back, axis=1, keepdims=True)
            d_gate[at, cols] = (back * u * sig * (1.0 + g * (1.0 - sig))).astype(BF)
            d_up[at, cols] = (back * silu).astype(BF)

        @pl.loop(0, width // dstep)
        def _(d):
            cols = pl.ds(pl.multiple_of(d * dstep, dstep), dstep)

            @pl.when(r == 0)
            def _():
                load_sum(d, 0).wait()
                load_sum(d, 1).wait()
                start(d + downs + AHEAD)

            value = dot_nt(d_gate[at, :], v_gate[cols, :]) + dot_nt(d_up[at, :], v_up[cols, :])
            value = value.astype(BF)
            if rows == block:
                keep[:, cols] = value[:half]
                send[:, cols] = value[half:]
            else:

                @pl.when(r < half // block)
                def _():
                    keep[at, cols] = value

                @pl.when(r >= half // block)
                def _():
                    send[pl.ds(pl.multiple_of(r * block - half, block), block), cols] = value

    keep[:, pl.ds(width, LANES)] = split3(score[pl.ds(0, half), :])
    send[:, pl.ds(width, LANES)] = split3(score[pl.ds(half, half), :])


def add_kernel(mine, theirs, *outs):
    width = mine.shape[1] - LANES
    at = 0
    for out in outs:
        rows = out.shape[0]
        here = pl.ds(at, rows)
        total = mine[here, pl.ds(0, width)].astype(F32) + theirs[here, pl.ds(0, width)].astype(F32)
        out[:, pl.ds(0, width)] = total.astype(BF)
        tail = join3(mine[here, pl.ds(width, LANES)]) + join3(theirs[here, pl.ds(width, LANES)])
        out[:, pl.ds(width, LANES)] = split3(tail)
        at += rows


def route_kernel(tokens, w_router, routes, relative, weight, sign, pair):
    experts = w_router.shape[1]
    logits = jnp.dot(tokens[...], w_router[...], preferred_element_type=F32)
    label = lax.broadcasted_iota(jnp.int32, logits.shape, 1)
    first, second = label == routes[:, 0:1], label == routes[:, 1:2]
    chosen = [jnp.sum(jnp.where(m, logits, 0.0), axis=1, keepdims=True) for m in (first, second)]
    prob = [jax.nn.sigmoid(chosen[0] - chosen[1]), jax.nn.sigmoid(chosen[1] - chosen[0])]
    pair[...] = jnp.where(first, 1.0, 0.0) - jnp.where(second, 1.0, 0.0)
    first, second = label == relative[:, 0:1], label == relative[:, 1:2]
    weight[:, pl.ds(0, experts)] = jnp.where(first, prob[0], 0.0) + jnp.where(second, prob[1], 0.0)
    weight[:, pl.ds(experts, 1)] = prob[0] * prob[1]
    sign[...] = jnp.where(first, 1.0, 0.0) - jnp.where(second, 1.0, 0.0)


def final_kernel(n, *refs):
    blocks, (weight, sign, pair, router, out, logit_grad) = refs[:n], refs[n:]
    width = out.shape[1]
    total, gap = 0.0, 0.0
    for s, block in enumerate(blocks):
        total = total + weight[:, s : s + 1] * block[:, pl.ds(0, width)].astype(F32)
        gap = gap + sign[:, s : s + 1] * join3(block[:, pl.ds(width, LANES)])
    grad = weight[:, n : n + 1] * gap
    for e in range(n):
        total = total + (grad * pair[:, e : e + 1]) * router[e : e + 1, :]
    out[...] = total.astype(BF)
    logit_grad[:, 0:1] = grad
    logit_grad[:, 1:2] = -grad


def call(kernel, args, outs, specs, scratch=(), limit=None, cost=None):
    return pl.pallas_call(
        kernel,
        out_shape=outs,
        in_specs=specs,
        out_specs=[VMEM] * len(outs),
        scratch_shapes=list(scratch),
        compiler_params=pltpu.CompilerParams(vmem_limit_bytes=limit),
        cost_estimate=cost,
    )(*args)


def shards(hidden, tokens, grad_out, routes, w_router, w_gate, w_up, w_down):
    own, width = tokens.shape
    experts = w_router.shape[1]
    ff = w_gate.shape[2]
    shape = jax.ShapeDtypeStruct
    bits = []
    while (1 << len(bits)) < hidden:
        bits.append(1 << len(bits))
    bits = bits[1:] + bits[:1]

    def along(x, shift):
        return lax.ppermute(x, "expert", [(i, (i + shift) % experts) for i in range(experts)])

    def across(x, bit):
        return lax.ppermute(x, "hidden", [(i, i ^ bit) for i in range(hidden)])

    def near(x):
        pieces = [jnp.concatenate([x] + [along(x, s) for s in range(1, experts)])]
        for bit in bits[:-1]:
            pieces = pieces + [across(piece, bit) for piece in pieces]
        return pieces

    def far(pieces):
        return pieces + [across(piece, bits[-1]) for piece in pieces]

    rows = own * experts * hidden
    spare = (4 if rows <= ROWS else 12) << 20
    small = own * hidden * experts * (width + LANES) * 4 + (1 << 20)
    def load(*arrays):
        n = len(arrays)
        (loaded,) = call(
            functools.partial(load_kernel, n),
            arrays,
            [shape((n, *arrays[0].shape), BF)],
            [pl.BlockSpec(memory_space=pltpu.HBM)] * n,
            [pltpu.SemaphoreType.DMA((n,))],
            1 << 20,
            pl.CostEstimate(flops=0, bytes_accessed=2 * sum(a.size for a in arrays), transcendentals=0),
        )
        return pltpu.with_memory_space_constraint(loaded, pltpu.VMEM)

    sources = [pltpu.with_memory_space_constraint(w[0], pltpu.HBM) for w in (w_gate, w_up, w_down)]
    w_both = load(*sources[:2])
    x_pieces, dy_pieces = far(near(tokens)), near(grad_out)
    n = len(x_pieces)
    macs = rows * width * ff
    (both,) = call(
        functools.partial(gate_up_kernel, n),
        x_pieces + [w_both],
        [shape((2, rows, ff), F32)],
        [ANY] * n + [VMEM],
        [pltpu.VMEM((rows, width), BF), pltpu.SemaphoreType.DMA((n,))],
        rows * width * 2 + spare,
        pl.CostEstimate(flops=4 * macs, bytes_accessed=4 * width * ff, transcendentals=0),
    )
    *late, both = lax.optimization_barrier((*dy_pieces[1:], both))
    dy_pieces = [pltpu.with_memory_space_constraint(p, pltpu.HBM) for p in far(dy_pieces[:1] + late)]
    keep, send = call(
        functools.partial(back_kernel, n),
        dy_pieces + sources + [both],
        [shape((rows // 2, width + LANES), BF)] * 2,
        [ANY] * (n + 3) + [VMEM],
        [
            pltpu.VMEM((rows, width), BF),
            pltpu.VMEM((rows, ff), BF),
            pltpu.VMEM((rows, ff), BF),
            pltpu.VMEM((rows, 1), F32),
            pltpu.VMEM((width, ff), BF),
            pltpu.VMEM((width, ff), BF),
            pltpu.VMEM((ff, width), BF),
            pltpu.SemaphoreType.DMA((n,)),
            pltpu.SemaphoreType.DMA((ff // chunk(ff, 512),)),
            pltpu.SemaphoreType.DMA((2, width // chunk(width, 512))),
        ],
        6 * width * ff + rows * (width + LANES) * 4 + rows * (ff * 4 + 4 * LANES) + spare,
        pl.CostEstimate(flops=6 * macs, bytes_accessed=6 * width * ff, transcendentals=0),
    )
    relative = (routes - lax.axis_index("expert")) % experts
    weight, sign, pair = call(
        route_kernel,
        [tokens, w_router, routes, relative],
        [shape((own, experts + 1), F32), shape((own, experts), F32), shape((own, experts), F32)],
        [VMEM] * 4,
        limit=small,
    )
    for bit in bits[:0:-1]:
        arrived = across(send, bit)
        part = keep.shape[0] // 2
        keep, send = call(
            add_kernel, [keep, arrived], [shape((part, width + LANES), BF)] * 2, [VMEM] * 2, limit=small
        )
    arrived = across(send, bits[0])
    blocks = call(
        add_kernel, [keep, arrived], [shape((own, width + LANES), BF)] * experts, [VMEM] * 2, limit=small
    )
    blocks = [blocks[0]] + [along(blocks[s], experts - s) for s in range(1, experts)]
    input_grad, logit_grad = call(
        functools.partial(final_kernel, experts),
        blocks + [weight, sign, pair, w_router.astype(F32).T],
        [shape((own, width), BF), shape((own, 2), F32)],
        [VMEM] * (experts + 4),
        limit=small,
    )
    return (input_grad, logit_grad)


def solution(mesh):
    row = P(("parts", "expert", "hidden"), None)
    placed = (
        row,
        row,
        row,
        P(),
        P("expert", None, "hidden"),
        P("expert", None, "hidden"),
        P("expert", "hidden", None),
    )
    return jax.shard_map(
        functools.partial(shards, mesh.shape["hidden"]),
        mesh=mesh,
        in_specs=placed,
        out_specs=(row, row),
        check_vma=False,
    )
```

time: 179 us -> 89.5 us (0.50)
  matrix products: 40.5 us -> 0 us
  Pallas kernels: 0 us -> 35.1 us
  waiting for transfers between devices: 58.8 us -> 28.8 us
  blocking collectives: 28 us -> 0 us
  local copies, waits for them, and re-layouts: 23.4 us -> 3.76 us
  between operations: 14.9 us -> 0.79 us
  starting transfers between devices: 9.43 us -> 20.8 us
  other arithmetic: 3.29 us -> 0.02 us
    dot_general x9 -> x0, matrix products: 40.5 us -> none  [the longest x1 10.3 us: shards(): jnp.einsum('rf,df->rd', d_up, up_local, preferred_element_type=jnp.float32)]
    pallas_call x0 -> x7, Pallas kernels: none -> 35.1 us  [call(): pl.pallas_call(kernel, out_shape=outs, in_specs=specs, out_specs=[VMEM] *...]
    ppermute x0 -> x17, waiting for transfers between devices: none -> 28.8 us  [the longest x8 17.5 us: across(): return lax.ppermute(x, 'hidden', [(i, i ^ bit) for i in range(hidden)])]
    all_gather x1 -> x0, waiting for transfers between devices: 23.3 us -> none  [shards(): gathered = lax.all_gather(arrived, 'hidden', axis=1, tiled=True)]
    all_to_all x1 -> x0, blocking collectives: 22.1 us -> none  [shards(): lax.all_to_all(outgoing, 'expert', split_axis=1, concat_axis=1, tiled=True)]
    ppermute x0 -> x17, starting transfers between devices: none -> 20.8 us  [the longest x9 17.2 us: along(): lax.ppermute(x, 'expert', [(i, (i + shift) % experts) for i in range(expe...]
    reduce_scatter x1 -> x0, waiting for transfers between devices: 18.7 us -> none  [shards(): lax.psum_scatter(partial_value, 'hidden', scatter_dimension=0, tiled=True)]
    all_to_all x2 -> x0, waiting for transfers between devices: 16.8 us -> none  [the longest x1 16.8 us: shards(): lax.all_to_all(summed.reshape(experts, capacity, width), 'expert', split_...]
  transfers between devices with their start and end apart: 4 -> 17, of which waited for: 3 -> 9; matrix products, arithmetic and copies ran while one was open for 4% -> 3% of each run, Pallas kernels for 0% -> 19%
where the time goes in v1:
time: 89.5 us; the launch traced here: 89.3 us
  Pallas kernels  35.1 us (39%)
  waiting for transfers between devices  28.8 us (32%)
  starting transfers between devices  20.8 us (23%)
  local copies, waits for them, and re-layouts  3.76 us (4%)
    pallas_call x7, Pallas kernels, call(): pl.pallas_call(kernel, out_shape=outs, in_specs=specs, out_specs=[VMEM] *...  35.1 us
    ppermute x8, waiting for transfers between devices, across(): return lax.ppermute(x, 'hidden', [(i, i ^ bit) for i in range(hidden)])  17.5 us
    ppermute x9, starting transfers between devices, along(): lax.ppermute(x, 'expert', [(i, (i + shift) % experts) for i in range(expe...  17.2 us
    ppermute x9, waiting for transfers between devices, along(): lax.ppermute(x, 'expert', [(i, (i + shift) % experts) for i in range(expe...  11.3 us
    ppermute x8, starting transfers between devices, across(): return lax.ppermute(x, 'hidden', [(i, i ^ bit) for i in range(hidden)])  3.58 us
    unnamed x22, local copies, waits for them, and re-layouts  3.1 us
  transfers between devices with their start and end apart: 17, of which 9 were waited for; matrix products, arithmetic and copies ran while one was open for 3% of the time, Pallas kernels for 19%

profile of v1, /device:TPU:0, one launch (start us, length us, event | category | flops | bytes accessed | tf_op | source)
XLA Modules:
  0.0 89.3 jit_solution(3639408540905563417)
XLA Ops:
  0.6 3.1 %collective-permute-start.4 = (bf16[16,3072]{1,0:T(8,128)(2,1)}, bf16[16,3072]{1,0:T(8,128)(2,1)S(1)}, u32[]{:S(2)}, u32[]{:S(2)}) collective-permute-start(bf16[16,3072]{1,0:T(8,128)(2,1)} %tokens.1), channel_id=1, source_target_pairs={{0,4},{4,8},{8,12},{12,0},{1,5},{5,9},{9,13},{13,1},{2,6},{6,10},{... | collective-permute-start | bytes 294920 | tf_op jit(solution)/shard_map/ppermute | solution.py:244
  3.7 2.6 %collective-permute-start.5 = (bf16[16,3072]{1,0:T(8,128)(2,1)}, bf16[16,3072]{1,0:T(8,128)(2,1)S(1)}, u32[]{:S(2)}, u32[]{:S(2)}) collective-permute-start(bf16[16,3072]{1,0:T(8,128)(2,1)} %tokens.1), channel_id=1, source_target_pairs={{0,8},{4,12},{8,0},{12,4},{1,9},{5,13},{9,1},{13,5},{2,10},{6,14},... | collective-permute-start | bytes 294920 | tf_op jit(solution)/shard_map/ppermute | solution.py:244
  6.3 1.3 %collective-permute-start.6 = (bf16[16,3072]{1,0:T(8,128)(2,1)}, bf16[16,3072]{1,0:T(8,128)(2,1)S(1)}, u32[]{:S(2)}, u32[]{:S(2)}) collective-permute-start(bf16[16,3072]{1,0:T(8,128)(2,1)} %tokens.1), channel_id=1, source_target_pairs={{0,12},{4,0},{8,4},{12,8},{1,13},{5,1},{9,5},{13,9},{2,14},{6,2},{... | collective-permute-start | bytes 294920 | tf_op jit(solution)/shard_map/ppermute | solution.py:244
  7.6 0.7 collective-permute-start
  8.3 0.3 collective-permute-start.1
  8.7 0.9 %constant_dynamic-update-slice_fusion.7 = bf16[64,3072]{1,0:T(8,128)(2,1)S(1)} fusion(bf16[16,3072]{1,0:T(8,128)(2,1)} %tokens.1), kind=kLoop, calls=%fused_computation.8 | loop fusion | bytes 196608
  9.6 0.0 collective-permute-done.4
  9.6 3.1 %collective-permute-start.2 = (bf16[16,3072]{1,0:T(8,128)(2,1)}, bf16[16,3072]{1,0:T(8,128)(2,1)S(1)}, u32[]{:S(2)}, u32[]{:S(2)}) collective-permute-start(bf16[16,3072]{1,0:T(8,128)(2,1)} %param.8), channel_id=1, source_target_pairs={{0,12},{4,0},{8,4},{12,8},{1,13},{5,1},{9,5},{13,9},{2,14},{6,2},{... | collective-permute-start | bytes 294920 | tf_op jit(solution)/shard_map/ppermute | solution.py:244
  12.7 3.9 %collective-permute-done.5 = bf16[16,3072]{1,0:T(8,128)(2,1)S(1)} collective-permute-done((bf16[16,3072]{1,0:T(8,128)(2,1)}, bf16[16,3072]{1,0:T(8,128)(2,1)S(1)}, u32[]{:S(2)}, u32[]{:S(2)}) %collective-permute-start.5) | collective-permute-done | bytes 98336 | tf_op jit(solution)/shard_map/ppermute | solution.py:244
  16.6 0.0 collective-permute-done.6
  16.7 1.6 %collective-permute-start.7 = (bf16[64,3072]{1,0:T(8,128)(2,1)S(1)}, bf16[64,3072]{1,0:T(8,128)(2,1)S(1)}, u32[]{:S(2)}, u32[]{:S(2)}) collective-permute-start(bf16[64,3072]{1,0:T(8,128)(2,1)S(1)} %constant_dynamic-update-slice_fusion.4.refs_0_), channel_id=1, source_target_pairs={{0,2},{1,3},{2,0},{3,1},{4,6},{5,7},{6,4},{7,5},{8,10},{9,11},{10,... | collective-permute-start | bytes 1179656 | tf_op jit(solution)/shard_map/ppermute | solution.py:247
  18.2 0.9 %constant_dynamic-update-slice_fusion.3 = bf16[64,3072]{1,0:T(8,128)(2,1)S(1)} fusion(bf16[16,3072]{1,0:T(8,128)(2,1)} %param.8), kind=kLoop, calls=%fused_computation.4 | loop fusion | bytes 196608
  19.1 8.2 %shard_map.86.refs_4_ = bf16[2,3072,2048]{2,1,0:T(8,128)(2,1)S(1)} custom-call(bf16[3072,2048]{1,0:T(8,128)(2,1)} %bitcast.5, bf16[3072,2048]{1,0:T(8,128)(2,1)} %bitcast.7), custom_call_target="tpu_custom_call" | custom-call | bytes 25165824 | tf_op jit(solution)/shard_map/pallas_call | solution.py:222
  27.4 0.1 collective-permute-start.8
  27.4 0.0 collective-permute-done
  27.5 0.0 collective-permute-done.7.refs_1_
  27.5 0.5 collective-permute-start.9
  28.0 0.0 collective-permute-done.1
  28.1 0.0 collective-permute-done.2
  28.1 0.0 copy-start.1
  28.1 0.6 collective-permute-start.3
  28.7 0.0 collective-permute-start.10
  28.7 0.5 collective-permute-done.8.refs_2_
  29.2 0.6 collective-permute-done.9.refs_3_
  29.7 8.0 %shard_map.87.refs_7_ = f32[2,256,2048]{2,1,0:T(8,128)S(1)} custom-call(bf16[64,3072]{1,0:T(8,128)(2,1)S(1)} %constant_dynamic-update-slice_fusion.4.refs_0_, bf16[64,3072]{1,0:T(8,128)(2,1)S(1)} %collective-permute-done.7.refs_1_, bf16[64,3072]{1,0:T(8,128)(2,1)S(1)} %collective-permute-done.8.refs_2_, bf16[64,3072]{1,0:T(8,128)(2,1)S(1)} %collective-permute-done.9.refs_3_, ...), custom_call_target="tpu_custom_call" | custom-call | flops 6442450944 | bytes 25165824 | tf_op jit(solution)/shard_map/pallas_call | solution.py:222
  37.8 0.0 copy-done.1
  37.8 1.4 %collective-permute-done.3.refs_1_ = bf16[64,3072]{1,0:T(8,128)(2,1)S(1)} collective-permute-done((bf16[64,3072]{1,0:T(8,128)(2,1)S(1)}, bf16[64,3072]{1,0:T(8,128)(2,1)S(1)}, u32[]{:S(2)}, u32[]{:S(2)}) %collective-permute-start.3) | collective-permute-done | bytes 393248 | tf_op jit(solution)/shard_map/ppermute | solution.py:247
  39.2 0.0 copy-start.2
  39.2 0.0 collective-permute-start.11
  39.2 0.0 collective-permute-done.10.refs_2_
  39.2 0.0 copy-start.3
  39.2 1.7 %collective-permute-done.11.refs_3_ = bf16[64,3072]{1,0:T(8,128)(2,1)S(1)} collective-permute-done((bf16[64,3072]{1,0:T(8,128)(2,1)S(1)}, bf16[64,3072]{1,0:T(8,128)(2,1)S(1)}, u32[]{:S(2)}, u32[]{:S(2)}) %collective-permute-start.11) | collective-permute-done | bytes 393248 | tf_op jit(solution)/shard_map/ppermute | solution.py:247
  40.9 0.0 copy-done.2
  40.9 0.0 copy-done.3
  40.9 0.0 copy-start.4
  40.9 0.7 copy-done.4
  41.7 0.0 copy-start.6
  41.7 0.0 copy-start.5
  41.7 0.0 copy-start
  41.7 17.0 %shard_map.88 = (bf16[128,3200]{1,0:T(8,128)(2,1)S(1)}, bf16[128,3200]{1,0:T(8,128)(2,1)}) custom-call(bf16[64,3072]{1,0:T(8,128)(2,1)} %copy-done.1, bf16[64,3072]{1,0:T(8,128)(2,1)} %copy-done.2, bf16[64,3072]{1,0:T(8,128)(2,1)} %copy-done.3, bf16[64,3072]{1,0:T(8,128)(2,1)} %copy-done.4, bf16[3072,2048]{1,0:T(8,128)(2,1)} %bitcast.6, ...), custom_call_target="tpu_custom_call" | custom-call | flops 9663676416 | bytes 37748736 | tf_op jit(solution)/shard_map/pallas_call | solution.py:222
  58.7 0.2 collective-permute-start.12
  58.9 0.0 copy-done.6
  58.9 0.1 copy.11.routes
  59.0 2.3 %collective-permute-done.12.theirs = bf16[128,3200]{1,0:T(8,128)(2,1)S(1)} collective-permute-done((bf16[128,3200]{1,0:T(8,128)(2,1)}, bf16[128,3200]{1,0:T(8,128)(2,1)S(1)}, u32[]{:S(2)}, u32[]{:S(2)}) %collective-permute-start.12) | collective-permute-done | bytes 819232 | tf_op jit(solution)/shard_map/ppermute | solution.py:247
  61.3 0.4 shard_map.89
  61.7 0.6 collective-permute-start.13
  62.3 0.0 copy-done.5
  62.3 11.0 %collective-permute-done.13.theirs = bf16[64,3200]{1,0:T(8,128)(2,1)S(1)} collective-permute-done((bf16[64,3200]{1,0:T(8,128)(2,1)S(1)}, bf16[64,3200]{1,0:T(8,128)(2,1)S(1)}, u32[]{:S(2)}, u32[]{:S(2)}) %collective-permute-start.13) | collective-permute-done | bytes 409632 | tf_op jit(solution)/shard_map/ppermute | solution.py:247
  73.3 0.1 shard_map.90
  73.5 5.5 %collective-permute-start.14 = (bf16[16,3200]{1,0:T(8,128)(2,1)S(1)}, bf16[16,3200]{1,0:T(8,128)(2,1)S(1)}, u32[]{:S(2)}, u32[]{:S(2)}) collective-permute-start(bf16[16,3200]{1,0:T(8,128)(2,1)S(1)} %get-tuple-element.22), channel_id=1, source_target_pairs={{0,12},{4,0},{8,4},{12,8},{1,13},{5,1},{9,5},{13,9},{2,14},{6,2},{... | collective-permute-start | bytes 307208 | tf_op jit(solution)/shard_map/ppermute | solution.py:244
  78.9 0.0 collective-permute-start.15
  78.9 0.6 collective-permute-start.16
  79.6 0.4 copy.10.w_router
  80.0 0.0 copy-done
  80.0 0.3 shard_map.91
  80.3 1.9 %collective-permute-done.14.refs_1_ = bf16[16,3200]{1,0:T(8,128)(2,1)S(1)} collective-permute-done((bf16[16,3200]{1,0:T(8,128)(2,1)S(1)}, bf16[16,3200]{1,0:T(8,128)(2,1)S(1)}, u32[]{:S(2)}, u32[]{:S(2)}) %collective-permute-start.14) | collective-permute-done | bytes 102432 | tf_op jit(solution)/shard_map/ppermute | solution.py:244
  82.3 5.4 %collective-permute-done.15.refs_2_ = bf16[16,3200]{1,0:T(8,128)(2,1)S(1)} collective-permute-done((bf16[16,3200]{1,0:T(8,128)(2,1)S(1)}, bf16[16,3200]{1,0:T(8,128)(2,1)S(1)}, u32[]{:S(2)}, u32[]{:S(2)}) %collective-permute-start.15) | collective-permute-done | bytes 102432 | tf_op jit(solution)/shard_map/ppermute | solution.py:244
  87.6 0.0 collective-permute-done.16.refs_3_
  87.6 1.0 %shard_map.92 = (bf16[16,3072]{1,0:T(8,128)(2,1)}, f32[16,2]{1,0:T(8,128)S(1)}) custom-call(bf16[16,3200]{1,0:T(8,128)(2,1)S(1)} %get-tuple-element.21.refs_0_, bf16[16,3200]{1,0:T(8,128)(2,1)S(1)} %collective-permute-done.14.refs_1_, bf16[16,3200]{1,0:T(8,128)(2,1)S(1)} %collective-permute-done.15.refs_2_, ...), custom_call_target="tpu_custom_call" | custom-call | tf_op jit(solution)/shard_map/pallas_call | solution.py:222
  88.7 0.6 copy.12
  (8 shorter events, 0.1 us)
Async XLA Ops:
  0.6 9.0 %collective-permute-start.4 = (bf16[16,3072]{1,0:T(8,128)(2,1)}, bf16[16,3072]{1,0:T(8,128)(2,1)S(1)}, u32[]{:S(2)}, u32[]{:S(2)}) collective-permute-start(bf16[16,3072]{1,0:T(8,128)(2,1)} %tokens.1), channel_id=1, source_target_pairs={{0,4},{4,8},{8,12},{12,0},{1,5},{5,9},{9,13},{13,1},{2,6},{6,10},{... | collective-permute-start | bytes 294920 | tf_op jit(solution)/shard_map/ppermute | solution.py:244
  3.7 12.9 %collective-permute-start.5 = (bf16[16,3072]{1,0:T(8,128)(2,1)}, bf16[16,3072]{1,0:T(8,128)(2,1)S(1)}, u32[]{:S(2)}, u32[]{:S(2)}) collective-permute-start(bf16[16,3072]{1,0:T(8,128)(2,1)} %tokens.1), channel_id=1, source_target_pairs={{0,8},{4,12},{8,0},{12,4},{1,9},{5,13},{9,1},{13,5},{2,10},{6,14},... | collective-permute-start | bytes 294920 | tf_op jit(solution)/shard_map/ppermute | solution.py:244
  6.3 10.4 %collective-permute-start.6 = (bf16[16,3072]{1,0:T(8,128)(2,1)}, bf16[16,3072]{1,0:T(8,128)(2,1)S(1)}, u32[]{:S(2)}, u32[]{:S(2)}) collective-permute-start(bf16[16,3072]{1,0:T(8,128)(2,1)} %tokens.1), channel_id=1, source_target_pairs={{0,12},{4,0},{8,4},{12,8},{1,13},{5,1},{9,5},{13,9},{2,14},{6,2},{... | collective-permute-start | bytes 294920 | tf_op jit(solution)/shard_map/ppermute | solution.py:244
  7.6 19.8 %collective-permute-start = (bf16[16,3072]{1,0:T(8,128)(2,1)}, bf16[16,3072]{1,0:T(8,128)(2,1)S(1)}, u32[]{:S(2)}, u32[]{:S(2)}) collective-permute-start(bf16[16,3072]{1,0:T(8,128)(2,1)} %param.8), channel_id=1, source_target_pairs={{0,4},{4,8},{8,12},{12,0},{1,5},{5,9},{9,13},{13,1},{2,6},{6,10},{... | collective-permute-start | bytes 294920 | tf_op jit(solution)/shard_map/ppermute | solution.py:244
  8.3 19.7 %collective-permute-start.1 = (bf16[16,3072]{1,0:T(8,128)(2,1)}, bf16[16,3072]{1,0:T(8,128)(2,1)S(1)}, u32[]{:S(2)}, u32[]{:S(2)}) collective-permute-start(bf16[16,3072]{1,0:T(8,128)(2,1)} %param.8), channel_id=1, source_target_pairs={{0,8},{4,12},{8,0},{12,4},{1,9},{5,13},{9,1},{13,5},{2,10},{6,14},... | collective-permute-start | bytes 294920 | tf_op jit(solution)/shard_map/ppermute | solution.py:244
  9.6 18.5 %collective-permute-start.2 = (bf16[16,3072]{1,0:T(8,128)(2,1)}, bf16[16,3072]{1,0:T(8,128)(2,1)S(1)}, u32[]{:S(2)}, u32[]{:S(2)}) collective-permute-start(bf16[16,3072]{1,0:T(8,128)(2,1)} %param.8), channel_id=1, source_target_pairs={{0,12},{4,0},{8,4},{12,8},{1,13},{5,1},{9,5},{13,9},{2,14},{6,2},{... | collective-permute-start | bytes 294920 | tf_op jit(solution)/shard_map/ppermute | solution.py:244
  16.7 10.8 %collective-permute-start.7 = (bf16[64,3072]{1,0:T(8,128)(2,1)S(1)}, bf16[64,3072]{1,0:T(8,128)(2,1)S(1)}, u32[]{:S(2)}, u32[]{:S(2)}) collective-permute-start(bf16[64,3072]{1,0:T(8,128)(2,1)S(1)} %constant_dynamic-update-slice_fusion.4.refs_0_), channel_id=1, source_target_pairs={{0,2},{1,3},{2,0},{3,1},{4,6},{5,7},{6,4},{7,5},{8,10},{9,11},{10,... | collective-permute-start | bytes 1179656 | tf_op jit(solution)/shard_map/ppermute | solution.py:247
  27.4 1.8 %collective-permute-start.8 = (bf16[64,3072]{1,0:T(8,128)(2,1)S(1)}, bf16[64,3072]{1,0:T(8,128)(2,1)S(1)}, u32[]{:S(2)}, u32[]{:S(2)}) collective-permute-start(bf16[64,3072]{1,0:T(8,128)(2,1)S(1)} %constant_dynamic-update-slice_fusion.4.refs_0_), channel_id=1, source_target_pairs={{0,1},{1,0},{2,3},{3,2},{4,5},{5,4},{6,7},{7,6},{8,9},{9,8},{10,11... | collective-permute-start | bytes 1179656 | tf_op jit(solution)/shard_map/ppermute | solution.py:247
  27.5 2.2 %collective-permute-start.9 = (bf16[64,3072]{1,0:T(8,128)(2,1)S(1)}, bf16[64,3072]{1,0:T(8,128)(2,1)S(1)}, u32[]{:S(2)}, u32[]{:S(2)}) collective-permute-start(bf16[64,3072]{1,0:T(8,128)(2,1)S(1)} %collective-permute-done.7.refs_1_), channel_id=1, source_target_pairs={{0,1},{1,0},{2,3},{3,2},{4,5},{5,4},{6,7},{7,6},{8,9},{9,8},{10,11... | collective-permute-start | bytes 1179656 | tf_op jit(solution)/shard_map/ppermute | solution.py:247
  28.1 9.7 %copy-start.1 = (bf16[64,3072]{1,0:T(8,128)(2,1)}, bf16[64,3072]{1,0:T(8,128)(2,1)S(1)}, u32[]{:S(2)}) copy-start(bf16[64,3072]{1,0:T(8,128)(2,1)S(1)} %constant_dynamic-update-slice_fusion.refs_0_) | copy-start | bytes 1179652
  28.1 11.1 %collective-permute-start.3 = (bf16[64,3072]{1,0:T(8,128)(2,1)S(1)}, bf16[64,3072]{1,0:T(8,128)(2,1)S(1)}, u32[]{:S(2)}, u32[]{:S(2)}) collective-permute-start(bf16[64,3072]{1,0:T(8,128)(2,1)S(1)} %constant_dynamic-update-slice_fusion.refs_0_), channel_id=1, source_target_pairs={{0,2},{1,3},{2,0},{3,1},{4,6},{5,7},{6,4},{7,5},{8,10},{9,11},{10,... | collective-permute-start | bytes 1179656 | tf_op jit(solution)/shard_map/ppermute | solution.py:247
  28.7 10.5 %collective-permute-start.10 = (bf16[64,3072]{1,0:T(8,128)(2,1)S(1)}, bf16[64,3072]{1,0:T(8,128)(2,1)S(1)}, u32[]{:S(2)}, u32[]{:S(2)}) collective-permute-start(bf16[64,3072]{1,0:T(8,128)(2,1)S(1)} %constant_dynamic-update-slice_fusion.refs_0_), channel_id=1, source_target_pairs={{0,1},{1,0},{2,3},{3,2},{4,5},{5,4},{6,7},{7,6},{8,9},{9,8},{10,11... | collective-permute-start | bytes 1179656 | tf_op jit(solution)/shard_map/ppermute | solution.py:247
  39.2 1.7 %copy-start.2 = (bf16[64,3072]{1,0:T(8,128)(2,1)}, bf16[64,3072]{1,0:T(8,128)(2,1)S(1)}, u32[]{:S(2)}) copy-start(bf16[64,3072]{1,0:T(8,128)(2,1)S(1)} %collective-permute-done.3.refs_1_) | copy-start | bytes 1179652
  39.2 1.7 %collective-permute-start.11 = (bf16[64,3072]{1,0:T(8,128)(2,1)S(1)}, bf16[64,3072]{1,0:T(8,128)(2,1)S(1)}, u32[]{:S(2)}, u32[]{:S(2)}) collective-permute-start(bf16[64,3072]{1,0:T(8,128)(2,1)S(1)} %collective-permute-done.3.refs_1_), channel_id=1, source_target_pairs={{0,1},{1,0},{2,3},{3,2},{4,5},{5,4},{6,7},{7,6},{8,9},{9,8},{10,11... | collective-permute-start | bytes 1179656 | tf_op jit(solution)/shard_map/ppermute | solution.py:247
  39.2 1.7 %copy-start.3 = (bf16[64,3072]{1,0:T(8,128)(2,1)}, bf16[64,3072]{1,0:T(8,128)(2,1)S(1)}, u32[]{:S(2)}) copy-start(bf16[64,3072]{1,0:T(8,128)(2,1)S(1)} %collective-permute-done.10.refs_2_) | copy-start | bytes 1179652
  40.9 0.7 copy-start.4
  41.7 17.3 %copy-start.6 = (s32[16,2]{0,1:T(2,128)S(1)}, s32[16,2]{0,1:T(2,128)}, u32[]{:S(2)}) copy-start(s32[16,2]{0,1:T(2,128)} %param.9) | copy-start | bytes 388
  41.7 20.6 %copy-start.5 = (bf16[3072,4]{0,1:T(4,128)(2,1)S(1)}, bf16[3072,4]{0,1:T(4,128)(2,1)}, u32[]{:S(2)}) copy-start(bf16[3072,4]{0,1:T(4,128)(2,1)} %param.10) | copy-start | bytes 73732
  41.7 38.3 %copy-start = (bf16[16,3072]{1,0:T(8,128)(2,1)S(1)}, bf16[16,3072]{1,0:T(8,128)(2,1)}, u32[]{:S(2)}) copy-start(bf16[16,3072]{1,0:T(8,128)(2,1)} %tokens.1) | copy-start | bytes 294916
  58.7 2.6 %collective-permute-start.12 = (bf16[128,3200]{1,0:T(8,128)(2,1)}, bf16[128,3200]{1,0:T(8,128)(2,1)S(1)}, u32[]{:S(2)}, u32[]{:S(2)}) collective-permute-start(bf16[128,3200]{1,0:T(8,128)(2,1)} %get-tuple-element.18), channel_id=1, source_target_pairs={{0,1},{1,0},{2,3},{3,2},{4,5},{5,4},{6,7},{7,6},{8,9},{9,8},{10,11... | collective-permute-start | bytes 2457608 | tf_op jit(solution)/shard_map/ppermute | solution.py:247
  61.7 11.6 %collective-permute-start.13 = (bf16[64,3200]{1,0:T(8,128)(2,1)S(1)}, bf16[64,3200]{1,0:T(8,128)(2,1)S(1)}, u32[]{:S(2)}, u32[]{:S(2)}) collective-permute-start(bf16[64,3200]{1,0:T(8,128)(2,1)S(1)} %get-tuple-element.20), channel_id=1, source_target_pairs={{0,2},{1,3},{2,0},{3,1},{4,6},{5,7},{6,4},{7,5},{8,10},{9,11},{10,... | collective-permute-start | bytes 1228808 | tf_op jit(solution)/shard_map/ppermute | solution.py:247
  73.5 8.8 %collective-permute-start.14 = (bf16[16,3200]{1,0:T(8,128)(2,1)S(1)}, bf16[16,3200]{1,0:T(8,128)(2,1)S(1)}, u32[]{:S(2)}, u32[]{:S(2)}) collective-permute-start(bf16[16,3200]{1,0:T(8,128)(2,1)S(1)} %get-tuple-element.22), channel_id=1, source_target_pairs={{0,12},{4,0},{8,4},{12,8},{1,13},{5,1},{9,5},{13,9},{2,14},{6,2},{... | collective-permute-start | bytes 307208 | tf_op jit(solution)/shard_map/ppermute | solution.py:244
  78.9 8.7 %collective-permute-start.15 = (bf16[16,3200]{1,0:T(8,128)(2,1)S(1)}, bf16[16,3200]{1,0:T(8,128)(2,1)S(1)}, u32[]{:S(2)}, u32[]{:S(2)}) collective-permute-start(bf16[16,3200]{1,0:T(8,128)(2,1)S(1)} %get-tuple-element.23), channel_id=1, source_target_pairs={{0,8},{4,12},{8,0},{12,4},{1,9},{5,13},{9,1},{13,5},{2,10},{6,14},... | collective-permute-start | bytes 307208 | tf_op jit(solution)/shard_map/ppermute | solution.py:244
  78.9 8.7 %collective-permute-start.16 = (bf16[16,3200]{1,0:T(8,128)(2,1)S(1)}, bf16[16,3200]{1,0:T(8,128)(2,1)S(1)}, u32[]{:S(2)}, u32[]{:S(2)}) collective-permute-start(bf16[16,3200]{1,0:T(8,128)(2,1)S(1)} %get-tuple-element.24), channel_id=1, source_target_pairs={{0,4},{4,8},{8,12},{12,0},{1,5},{5,9},{9,13},{13,1},{2,6},{6,10},{... | collective-permute-start | bytes 307208 | tf_op jit(solution)/shard_map/ppermute | solution.py:244

commit v2 on v1

v2 whole, which is shorter than its diff:
```python
import functools

import jax
import jax.numpy as jnp
from jax import lax
from jax.experimental import pallas as pl
from jax.experimental.pallas import tpu as pltpu
from jax.sharding import PartitionSpec as P

BF = jnp.bfloat16
F32 = jnp.float32
LANES = 128
ROWS = 256
GRANT = 19 << 20
AHEAD = 2
NT = (((1,), (1,)), ((), ()))
ANY = pl.BlockSpec(memory_space=pl.ANY)
VMEM = pl.BlockSpec(memory_space=pltpu.VMEM)


def dot_nt(a, b):
    return lax.dot_general(a, b, NT, preferred_element_type=F32)


def chunk(extent, wanted):
    size = min(extent, wanted)
    while extent % size:
        size -= LANES
    return size


def fetch(pieces, held, sems):
    copies, at = [], 0
    for i, piece in enumerate(pieces):
        rows = piece.shape[0]
        copies.append(pltpu.make_async_copy(piece, held.at[pl.ds(at, rows)], sems.at[i]))
        at += rows
    for copy in copies:
        copy.start()
    for copy in copies:
        copy.wait()


def load_kernel(first, second, target, sems):
    copies = [pltpu.make_async_copy(w, target.at[i], sems.at[i]) for i, w in enumerate((first, second))]
    for copy in copies:
        copy.start()
    for copy in copies:
        copy.wait()


def gate_up_kernel(n, *refs):
    pieces, (weights, both, _, held, sems) = refs[:n], refs[n:]
    fetch(pieces, held, sems)
    rows, ff = both.shape[1:]
    block, step = min(rows, ROWS), chunk(ff, 512)

    @pl.loop(0, rows // block)
    def _(r):
        at = pl.ds(pl.multiple_of(r * block, block), block)

        @pl.loop(0, ff // step)
        def _(f):
            cols = pl.ds(pl.multiple_of(f * step, step), step)
            for k in range(2):
                both[k, at, cols] = jnp.dot(held[at, :], weights[k, :, cols], preferred_element_type=F32)


def split3(score):
    high = score.astype(BF)
    rest = score - high.astype(F32)
    mid = rest.astype(BF)
    low = (rest - mid.astype(F32)).astype(BF)
    lane = lax.broadcasted_iota(jnp.int32, (score.shape[0], LANES), 1)
    spread = [jnp.broadcast_to(t.astype(F32), lane.shape) for t in (high, mid, low)]
    out = jnp.where(lane == 0, spread[0], jnp.where(lane == 1, spread[1], spread[2]))
    return jnp.where(lane < 3, out, 0.0).astype(BF)


def join3(tail):
    return jnp.sum(tail.astype(F32), axis=1, keepdims=True)


def store_halves(r, block, rows, cols, value, keep, send):
    half = rows // 2
    if rows == block:
        keep[:, cols] = value[:half]
        send[:, cols] = value[half:]
    else:

        @pl.when(r < half // block)
        def _():
            keep[pl.ds(pl.multiple_of(r * block, block), block), cols] = value

        @pl.when(r >= half // block)
        def _():
            send[pl.ds(pl.multiple_of(r * block - half, block), block), cols] = value


def sum_columns(start, width, r, block, grads, weights, keep, send):
    rows = grads.shape[1]
    at = pl.ds(pl.multiple_of(r * block, block), block)
    step = chunk(width, 512)

    @pl.loop(0, width // step)
    def _(d):
        source = pl.ds(pl.multiple_of(start + d * step, step), step)
        cols = pl.ds(pl.multiple_of(d * step, step), step)
        value = dot_nt(grads[0, at, :], weights[0, source, :])
        value = value + dot_nt(grads[1, at, :], weights[1, source, :])
        store_halves(r, block, rows, cols, value.astype(BF), keep, send)


def back_kernel(n, *refs):
    pieces = refs[:n]
    weights, w_down, both, keep, send, grads, score, _, held, v_down, sems, down_sems = refs[n:]
    rows, ff = both.shape[1:]
    block, step = min(rows, ROWS), chunk(ff, 512)

    def load_down(f):
        part = pl.ds(pl.multiple_of(f * step, step), step)
        return pltpu.make_async_copy(w_down.at[part], v_down.at[part], down_sems.at[f])

    load_down(0).start()
    fetch(pieces, held, sems)
    for f in range(1, min(AHEAD, ff // step)):
        load_down(f).start()

    @pl.loop(0, rows // block)
    def _(r):
        at = pl.ds(pl.multiple_of(r * block, block), block)
        score[at, :] = jnp.zeros((block, 1), F32)

        @pl.loop(0, ff // step)
        def _(f):
            cols = pl.ds(pl.multiple_of(f * step, step), step)

            @pl.when(r == 0)
            def _():
                load_down(f).wait()

                @pl.when(f + AHEAD < ff // step)
                def _():
                    load_down(f + AHEAD).start()

            back = dot_nt(held[at, :], v_down[cols, :])
            g, u = both[0, at, cols], both[1, at, cols]
            sig = jax.nn.sigmoid(g)
            silu = g * sig
            score[at, :] += jnp.sum(silu * u * back, axis=1, keepdims=True)
            grads[0, at, cols] = (back * u * sig * (1.0 + g * (1.0 - sig))).astype(BF)
            grads[1, at, cols] = (back * silu).astype(BF)

        sum_columns(0, keep.shape[1], r, block, grads, weights, keep, send)


def rest_kernel(start, weights, grads, score, keep, send):
    rows = grads.shape[1]
    width = keep.shape[1] - LANES
    block, half = min(rows, ROWS), rows // 2

    @pl.loop(0, rows // block)
    def _(r):
        sum_columns(start, width, r, block, grads, weights, keep, send)

    keep[:, pl.ds(width, LANES)] = split3(score[pl.ds(0, half), :])
    send[:, pl.ds(width, LANES)] = split3(score[pl.ds(half, half), :])


def add_kernel(tail, mine, theirs, *outs):
    width = mine.shape[1] - (LANES if tail else 0)
    at = 0
    for out in outs:
        rows = out.shape[0]
        here = pl.ds(at, rows)
        total = mine[here, pl.ds(0, width)].astype(F32) + theirs[here, pl.ds(0, width)].astype(F32)
        out[:, pl.ds(0, width)] = total.astype(BF)
        if tail:
            last = pl.ds(width, LANES)
            out[:, last] = split3(join3(mine[here, last]) + join3(theirs[here, last]))
        at += rows


def route_kernel(tokens, w_router, routes, relative, weight, sign, pair):
    experts = w_router.shape[1]
    logits = jnp.dot(tokens[...], w_router[...], preferred_element_type=F32)
    label = lax.broadcasted_iota(jnp.int32, logits.shape, 1)
    first, second = label == routes[:, 0:1], label == routes[:, 1:2]
    chosen = [jnp.sum(jnp.where(m, logits, 0.0), axis=1, keepdims=True) for m in (first, second)]
    prob = [jax.nn.sigmoid(chosen[0] - chosen[1]), jax.nn.sigmoid(chosen[1] - chosen[0])]
    pair[...] = jnp.where(first, 1.0, 0.0) - jnp.where(second, 1.0, 0.0)
    first, second = label == relative[:, 0:1], label == relative[:, 1:2]
    weight[:, pl.ds(0, experts)] = jnp.where(first, prob[0], 0.0) + jnp.where(second, prob[1], 0.0)
    weight[:, pl.ds(experts, 1)] = prob[0] * prob[1]
    sign[...] = jnp.where(first, 1.0, 0.0) - jnp.where(second, 1.0, 0.0)


def final_kernel(n, *refs):
    first, second, (weight, sign, pair, router, out, logit_grad) = refs[:n], refs[n : 2 * n], refs[2 * n :]
    lead = first[0].shape[1]
    gap = 0.0
    for s, block in enumerate(second):
        gap = gap + sign[:, s : s + 1] * join3(block[:, pl.ds(out.shape[1] - lead, LANES)])
    grad = weight[:, n : n + 1] * gap
    logit_grad[:, 0:1] = grad
    logit_grad[:, 1:2] = -grad
    for blocks, cols in ((first, pl.ds(0, lead)), (second, pl.ds(lead, out.shape[1] - lead))):
        total = 0.0
        for s, block in enumerate(blocks):
            total = total + weight[:, s : s + 1] * block[:, pl.ds(0, cols.size)].astype(F32)
        for e in range(n):
            total = total + (grad * pair[:, e : e + 1]) * router[e : e + 1, cols]
        out[:, cols] = total.astype(BF)


def call(kernel, args, outs, specs, scratch=(), limit=None, cost=None, alias={}):
    return pl.pallas_call(
        kernel,
        out_shape=outs,
        in_specs=specs,
        out_specs=[VMEM] * len(outs),
        scratch_shapes=list(scratch),
        compiler_params=pltpu.CompilerParams(vmem_limit_bytes=limit),
        cost_estimate=cost,
        input_output_aliases=alias,
    )(*args)


def shards(hidden, tokens, grad_out, routes, w_router, w_gate, w_up, w_down):
    own, width = tokens.shape
    experts = w_router.shape[1]
    ff = w_gate.shape[2]
    shape = jax.ShapeDtypeStruct
    bits = []
    while (1 << len(bits)) < hidden:
        bits.append(1 << len(bits))
    bits = bits[1:] + bits[:1]

    def along(x, shift):
        return lax.ppermute(x, "expert", [(i, (i + shift) % experts) for i in range(experts)])

    def across(x, bit):
        return lax.ppermute(x, "hidden", [(i, i ^ bit) for i in range(hidden)])

    rows = own * experts * hidden
    macs = rows * width * ff
    lead = width // 2
    rest = width - lead + LANES
    resident_bytes = rows * (2 * width + 8 * LANES) + rows * (ff * 4 + lead * 2 + rest * 2)
    grant = GRANT if rows <= ROWS else resident_bytes + GRANT
    small = min(rows, 2048) * (width + LANES) * 4 + (1 << 20)

    def cost(weights, matmuls):
        return pl.CostEstimate(
            flops=int(2 * matmuls * macs), bytes_accessed=2 * weights * width * ff, transcendentals=0
        )

    def vmem(x):
        return pltpu.with_memory_space_constraint(x, pltpu.VMEM)

    def hbm(x):
        return pltpu.with_memory_space_constraint(x, pltpu.HBM)

    def column(x):
        return jnp.concatenate([x] + [along(x, s) for s in range(1, experts)])

    def spread(pieces, some):
        for bit in some:
            pieces = pieces + [across(piece, bit) for piece in pieces]
        return pieces

    w_gate, w_up, w_down = [hbm(w[0]) for w in (w_gate, w_up, w_down)]
    held = pltpu.VMEM((rows, width), BF)
    pair_of = shape((2, *w_gate.shape), BF)
    (weights,) = call(
        load_kernel, [w_gate, w_up], [pair_of], [ANY] * 2, [pltpu.SemaphoreType.DMA((2,))], grant, cost(2, 0)
    )
    x_column, weights = lax.optimization_barrier((column(tokens), vmem(weights)))
    x_column, grad_out = lax.optimization_barrier((x_column, grad_out))
    x_pieces = spread([x_column], bits)
    dy_pieces = spread([column(grad_out)], bits[:-1])
    n = len(x_pieces)
    both, weights = call(
        functools.partial(gate_up_kernel, n),
        x_pieces + [weights],
        [shape((2, rows, ff), F32), pair_of],
        [ANY] * n + [VMEM],
        [held, pltpu.SemaphoreType.DMA((n,))],
        grant,
        cost(2, 2),
        {n: 1},
    )
    both, weights = vmem(both), vmem(weights)
    *late, both = lax.optimization_barrier((*dy_pieces[1:], both))
    dy_pieces = spread(dy_pieces[:1] + late, bits[-1:])
    keep, send, grads, score, weights = call(
        functools.partial(back_kernel, n),
        dy_pieces + [weights, w_down, both],
        [shape((rows // 2, lead), BF)] * 2 + [shape((2, rows, ff), BF), shape((rows, 1), F32), pair_of],
        [ANY] * n + [VMEM, ANY, VMEM],
        [
            held,
            pltpu.VMEM((ff, width), BF),
            pltpu.SemaphoreType.DMA((n,)),
            pltpu.SemaphoreType.DMA((ff // chunk(ff, 512),)),
        ],
        grant,
        cost(3, 2),
        {n: 4},
    )
    keep_rest, send_rest = call(
        functools.partial(rest_kernel, lead),
        [vmem(weights), vmem(grads), score],
        [shape((rows // 2, rest), BF)] * 2,
        [VMEM] * 3,
        limit=grant,
        cost=cost(1, 1),
    )
    send_rest, routes, w_router, tokens = lax.optimization_barrier((send_rest, routes, w_router, tokens))
    relative = (routes - lax.axis_index("expert")) % experts
    weight, sign, pair = call(
        route_kernel,
        [tokens, w_router, routes, relative],
        [shape((own, experts + 1), F32), shape((own, experts), F32), shape((own, experts), F32)],
        [VMEM] * 4,
        limit=small,
    )

    def collect(keep, send, tail):
        add = functools.partial(add_kernel, tail)
        total = keep.shape[1]
        for bit in bits[:0:-1]:
            arrived = across(send, bit)
            outs = [shape((keep.shape[0] // 2, total), BF)] * 2
            keep, send = call(add, [keep, arrived], outs, [VMEM] * 2, limit=small)
        arrived = across(send, bits[0])
        outs = [shape((own, total), BF)] * experts
        blocks = call(add, [keep, arrived], outs, [VMEM] * 2, limit=small)
        return [blocks[0]] + [along(blocks[s], experts - s) for s in range(1, experts)]

    first, second = collect(keep, send, False), collect(keep_rest, send_rest, True)
    input_grad, logit_grad = call(
        functools.partial(final_kernel, experts),
        first + second + [weight, sign, pair, w_router.astype(F32).T],
        [shape((own, width), BF), shape((own, 2), F32)],
        [VMEM] * (2 * experts + 4),
        limit=small,
    )
    return (input_grad, logit_grad)


def solution(mesh):
    row = P(("parts", "expert", "hidden"), None)
    placed = (
        row,
        row,
        row,
        P(),
        P("expert", None, "hidden"),
        P("expert", None, "hidden"),
        P("expert", "hidden", None),
    )
    return jax.shard_map(
        functools.partial(shards, mesh.shape["hidden"]),
        mesh=mesh,
        in_specs=placed,
        out_specs=(row, row),
        check_vma=False,
    )
```

time: 89.5 us -> 79.2 us (0.88)
  waiting for transfers between devices: 28.8 us -> 18.4 us
  starting transfers between devices: 20.8 us -> 26 us
  local copies, waits for them, and re-layouts: 3.76 us -> 1.19 us
  Pallas kernels: 35.1 us -> 32.6 us
    ppermute x8 -> x10, waiting for transfers between devices: 17.5 us -> 11.2 us  [across(): return lax.ppermute(x, 'hidden', [(i, i ^ bit) for i in range(hidden)])]
    ppermute x9 -> x12, waiting for transfers between devices: 11.3 us -> 7.19 us  [along(): lax.ppermute(x, 'expert', [(i, (i + shift) % experts) for i in range(expe...]
    ppermute x8 -> x10, starting transfers between devices: 3.58 us -> 6.87 us  [across(): return lax.ppermute(x, 'hidden', [(i, i ^ bit) for i in range(hidden)])]
    unnamed x22 -> x11, local copies, waits for them, and re-layouts: 3.1 us -> 0.04 us
    pallas_call x7 -> x10, Pallas kernels: 35.1 us -> 32.6 us  [call(): pl.pallas_call(kernel, out_shape=outs, in_specs=specs, out_specs=[VMEM] *...]
    ppermute x9 -> x12, starting transfers between devices: 17.2 us -> 19.1 us  [along(): lax.ppermute(x, 'expert', [(i, (i + shift) % experts) for i in range(expe...]
  transfers between devices with their start and end apart: 17 -> 22, of which waited for: 9 -> 9; matrix products, arithmetic and copies ran while one was open for 3% -> 1% of each run, Pallas kernels for 19% -> 26%
where the time goes in v2:
time: 79.2 us; the launch traced here: 79.1 us
  Pallas kernels  32.6 us (41%)
  starting transfers between devices  26 us (33%)
  waiting for transfers between devices  18.4 us (23%)
  local copies, waits for them, and re-layouts  1.19 us (2%)
  between operations  0.8 us (1%)
    pallas_call x10, Pallas kernels, call(): pl.pallas_call(kernel, out_shape=outs, in_specs=specs, out_specs=[VMEM] *...  32.6 us
    ppermute x12, starting transfers between devices, along(): lax.ppermute(x, 'expert', [(i, (i + shift) % experts) for i in range(expe...  19.1 us
    ppermute x10, waiting for transfers between devices, across(): return lax.ppermute(x, 'hidden', [(i, i ^ bit) for i in range(hidden)])  11.2 us
    ppermute x12, waiting for transfers between devices, along(): lax.ppermute(x, 'expert', [(i, (i + shift) % experts) for i in range(expe...  7.19 us
    ppermute x10, starting transfers between devices, across(): return lax.ppermute(x, 'hidden', [(i, i ^ bit) for i in range(hidden)])  6.87 us
  transfers between devices with their start and end apart: 22, of which 9 were waited for; matrix products, arithmetic and copies ran while one was open for 1% of the time, Pallas kernels for 26%

profile of v2, /device:TPU:0, one launch (start us, length us, event | category | flops | bytes accessed | tf_op | source)
XLA Modules:
  0.0 79.1 jit_solution(3566342977134455235)
XLA Ops:
  0.6 3.1 %collective-permute-start = (bf16[16,3072]{1,0:T(8,128)(2,1)}, bf16[16,3072]{1,0:T(8,128)(2,1)S(1)}, u32[]{:S(2)}, u32[]{:S(2)}) collective-permute-start(bf16[16,3072]{1,0:T(8,128)(2,1)} %tokens), channel_id=1, source_target_pairs={{0,4},{4,8},{8,12},{12,0},{1,5},{5,9},{9,13},{13,1},{2,6},{6,10},{... | collective-permute-start | bytes 294920 | tf_op jit(solution)/shard_map/ppermute | solution.py:240
  3.7 2.6 %collective-permute-start.1 = (bf16[16,3072]{1,0:T(8,128)(2,1)}, bf16[16,3072]{1,0:T(8,128)(2,1)S(1)}, u32[]{:S(2)}, u32[]{:S(2)}) collective-permute-start(bf16[16,3072]{1,0:T(8,128)(2,1)} %tokens), channel_id=1, source_target_pairs={{0,8},{4,12},{8,0},{12,4},{1,9},{5,13},{9,1},{13,5},{2,10},{6,14},... | collective-permute-start | bytes 294920 | tf_op jit(solution)/shard_map/ppermute | solution.py:240
  6.3 1.3 %collective-permute-start.2 = (bf16[16,3072]{1,0:T(8,128)(2,1)}, bf16[16,3072]{1,0:T(8,128)(2,1)S(1)}, u32[]{:S(2)}, u32[]{:S(2)}) collective-permute-start(bf16[16,3072]{1,0:T(8,128)(2,1)} %tokens), channel_id=1, source_target_pairs={{0,12},{4,0},{8,4},{12,8},{1,13},{5,1},{9,5},{13,9},{2,14},{6,2},{... | collective-permute-start | bytes 294920 | tf_op jit(solution)/shard_map/ppermute | solution.py:240
  7.6 0.0 copy-start
  7.6 0.0 copy-start.2
  7.7 8.2 %shard_map.86.refs_4_ = bf16[2,3072,2048]{2,1,0:T(8,128)(2,1)S(1)} custom-call(bf16[3072,2048]{1,0:T(8,128)(2,1)} %bitcast.5, bf16[3072,2048]{1,0:T(8,128)(2,1)} %bitcast.6), custom_call_target="tpu_custom_call" | custom-call | bytes 25165824 | tf_op jit(solution)/shard_map/pallas_call | solution.py:217
  15.9 0.0 collective-permute-done
  15.9 0.0 collective-permute-done.1
  15.9 0.0 collective-permute-done.2
  15.9 0.0 copy-done
  16.0 0.0 copy-done.2
  16.0 0.7 collective-permute-start.3
  16.7 1.5 %collective-permute-start.7 = (bf16[64,3072]{1,0:T(8,128)(2,1)S(1)}, bf16[64,3072]{1,0:T(8,128)(2,1)S(1)}, u32[]{:S(2)}, u32[]{:S(2)}) collective-permute-start(bf16[64,3072]{1,0:T(8,128)(2,1)S(1)} %pad_maximum_fusion.refs_0_), channel_id=1, source_target_pairs={{0,2},{1,3},{2,0},{3,1},{4,6},{5,7},{6,4},{7,5},{8,10},{9,11},{10,... | collective-permute-start | bytes 1179656 | tf_op jit(solution)/shard_map/ppermute | solution.py:243
  18.2 0.8 collective-permute-start.4
  19.0 2.5 %collective-permute-start.5 = (bf16[16,3072]{1,0:T(8,128)(2,1)S(1)}, bf16[16,3072]{1,0:T(8,128)(2,1)S(1)}, u32[]{:S(2)}, u32[]{:S(2)}) collective-permute-start(bf16[16,3072]{1,0:T(8,128)(2,1)S(1)} %copy-done.2), channel_id=1, source_target_pairs={{0,12},{4,0},{8,4},{12,8},{1,13},{5,1},{9,5},{13,9},{2,14},{6,2},{... | collective-permute-start | bytes 294920 | tf_op jit(solution)/shard_map/ppermute | solution.py:240
  21.5 0.0 collective-permute-start.8
  21.5 2.0 %collective-permute-done.3 = bf16[16,3072]{1,0:T(8,128)(2,1)S(1)} collective-permute-done((bf16[16,3072]{1,0:T(8,128)(2,1)S(1)}, bf16[16,3072]{1,0:T(8,128)(2,1)S(1)}, u32[]{:S(2)}, u32[]{:S(2)}) %collective-permute-start.3) | collective-permute-done | bytes 98336 | tf_op jit(solution)/shard_map/ppermute | solution.py:240
  23.5 3.0 %collective-permute-done.7.refs_1_ = bf16[64,3072]{1,0:T(8,128)(2,1)S(1)} collective-permute-done((bf16[64,3072]{1,0:T(8,128)(2,1)S(1)}, bf16[64,3072]{1,0:T(8,128)(2,1)S(1)}, u32[]{:S(2)}, u32[]{:S(2)}) %collective-permute-start.7) | collective-permute-done | bytes 393248 | tf_op jit(solution)/shard_map/ppermute | solution.py:243
  26.5 0.0 collective-permute-start.9
  26.5 0.0 collective-permute-done.4
  26.5 0.0 collective-permute-done.5
  26.6 1.6 %collective-permute-start.6 = (bf16[64,3072]{1,0:T(8,128)(2,1)S(1)}, bf16[64,3072]{1,0:T(8,128)(2,1)S(1)}, u32[]{:S(2)}, u32[]{:S(2)}) collective-permute-start(bf16[64,3072]{1,0:T(8,128)(2,1)S(1)} %constant_dynamic-update-slice_fusion.refs_0_), channel_id=1, source_target_pairs={{0,2},{1,3},{2,0},{3,1},{4,6},{5,7},{6,4},{7,5},{8,10},{9,11},{10,... | collective-permute-start | bytes 1179656 | tf_op jit(solution)/shard_map/ppermute | solution.py:243
  28.1 0.2 collective-permute-start.10
  28.4 0.0 collective-permute-done.8.refs_2_
  28.4 0.0 collective-permute-done.9.refs_3_
  28.4 8.0 %shard_map.87 = (f32[2,256,2048]{2,1,0:T(8,128)S(1)}, bf16[2,3072,2048]{2,1,0:T(8,128)(2,1)S(1)}) custom-call(bf16[64,3072]{1,0:T(8,128)(2,1)S(1)} %pad_maximum_fusion.refs_0_, bf16[64,3072]{1,0:T(8,128)(2,1)S(1)} %collective-permute-done.7.refs_1_, bf16[64,3072]{1,0:T(8,128)(2,1)S(1)} %collective-permute-done.8.refs_2_, ...), custom_call_target="tpu_custom_call", output_to_operand_aliasing={{1}: (4, {})} | custom-call | flops 6442450944 | bytes 25165824 | tf_op jit(solution)/shard_map/pallas_call | solution.py:217
  36.4 1.7 %collective-permute-done.6.refs_1_ = bf16[64,3072]{1,0:T(8,128)(2,1)S(1)} collective-permute-done((bf16[64,3072]{1,0:T(8,128)(2,1)S(1)}, bf16[64,3072]{1,0:T(8,128)(2,1)S(1)}, u32[]{:S(2)}, u32[]{:S(2)}) %collective-permute-start.6) | collective-permute-done | bytes 393248 | tf_op jit(solution)/shard_map/ppermute | solution.py:243
  38.2 0.0 collective-permute-start.11
  38.2 0.0 collective-permute-done.10.refs_2_
  38.2 1.7 %collective-permute-done.11.refs_3_ = bf16[64,3072]{1,0:T(8,128)(2,1)S(1)} collective-permute-done((bf16[64,3072]{1,0:T(8,128)(2,1)S(1)}, bf16[64,3072]{1,0:T(8,128)(2,1)S(1)}, u32[]{:S(2)}, u32[]{:S(2)}) %collective-permute-start.11) | collective-permute-done | bytes 393248 | tf_op jit(solution)/shard_map/ppermute | solution.py:243
  39.9 10.7 %shard_map.88 = (bf16[128,1536]{1,0:T(8,128)(2,1)S(1)}, bf16[128,1536]{1,0:T(8,128)(2,1)S(1)}, bf16[2,256,2048]{2,1,0:T(8,128)(2,1)S(1)}, f32[256,1]{1,0:T(8,128)S(1)}, bf16[2,3072,2048]{2,1,0:T(8,128)(2,1)S(1)}) custom-call(bf16[64,3072]{1,0:T(8,128)(2,1)S(1)} %constant_dynamic-update-slice_fusion.refs_0_, ...), custom_call_target="tpu_custom_call", output_to_operand_aliasing={{4}: (4, {})} | custom-call | flops 6442450944 | bytes 37748736 | tf_op jit(solution)/shard_map/pallas_call | solution.py:217
  50.6 0.2 collective-permute-start.12
  50.8 0.0 copy-start.1
  50.8 0.0 copy-start.3
  50.8 4.0 %shard_map.91 = (bf16[128,1664]{1,0:T(8,128)(2,1)S(1)}, bf16[128,1664]{1,0:T(8,128)(2,1)S(1)}) custom-call(bf16[2,3072,2048]{2,1,0:T(8,128)(2,1)S(1)} %get-tuple-element.52.weights, bf16[2,256,2048]{2,1,0:T(8,128)(2,1)S(1)} %get-tuple-element.53.grads, f32[256,1]{1,0:T(8,128)S(1)} %get-tuple-element.54.score), custom_call_target="tpu_custom_call" | custom-call | flops 3221225472 | bytes 12582912 | tf_op jit(solution)/shard_map/pallas_call | solution.py:217
  54.7 0.4 collective-permute-start.17
  55.2 0.0 collective-permute-done.12.theirs
  55.2 0.1 shard_map.89
  55.3 1.6 %collective-permute-start.13 = (bf16[64,1536]{1,0:T(8,128)(2,1)S(1)}, bf16[64,1536]{1,0:T(8,128)(2,1)S(1)}, u32[]{:S(2)}, u32[]{:S(2)}) collective-permute-start(bf16[64,1536]{1,0:T(8,128)(2,1)S(1)} %get-tuple-element.47), channel_id=1, source_target_pairs={{0,2},{1,3},{2,0},{3,1},{4,6},{5,7},{6,4},{7,5},{8,10},{9,11},{10,... | collective-permute-start | bytes 589832 | tf_op jit(solution)/shard_map/ppermute | solution.py:243
  56.9 0.0 collective-permute-done.17.theirs
  56.9 0.2 shard_map.92
  57.1 1.3 %collective-permute-start.18 = (bf16[64,1664]{1,0:T(8,128)(2,1)S(1)}, bf16[64,1664]{1,0:T(8,128)(2,1)S(1)}, u32[]{:S(2)}, u32[]{:S(2)}) collective-permute-start(bf16[64,1664]{1,0:T(8,128)(2,1)S(1)} %get-tuple-element.59), channel_id=1, source_target_pairs={{0,2},{1,3},{2,0},{3,1},{4,6},{5,7},{6,4},{7,5},{8,10},{9,11},{10,... | collective-permute-start | bytes 638984 | tf_op jit(solution)/shard_map/ppermute | solution.py:243
  58.4 4.7 %collective-permute-done.13.theirs = bf16[64,1536]{1,0:T(8,128)(2,1)S(1)} collective-permute-done((bf16[64,1536]{1,0:T(8,128)(2,1)S(1)}, bf16[64,1536]{1,0:T(8,128)(2,1)S(1)}, u32[]{:S(2)}, u32[]{:S(2)}) %collective-permute-start.13) | collective-permute-done | bytes 196640 | tf_op jit(solution)/shard_map/ppermute | solution.py:243
  63.1 3.1 %collective-permute-start.14 = (bf16[16,1536]{1,0:T(8,128)(2,1)S(1)}, bf16[16,1536]{1,0:T(8,128)(2,1)S(1)}, u32[]{:S(2)}, u32[]{:S(2)}) collective-permute-start(bf16[16,1536]{1,0:T(8,128)(2,1)S(1)} %get-tuple-element.49), channel_id=1, source_target_pairs={{0,12},{4,0},{8,4},{12,8},{1,13},{5,1},{9,5},{13,9},{2,14},{6,2},{... | collective-permute-start | bytes 147464 | tf_op jit(solution)/shard_map/ppermute | solution.py:240
  66.3 0.0 copy-done.1
  66.3 0.0 copy-done.3
  66.3 0.1 copy.13.routes
  66.4 0.0 collective-permute-start.15
  66.4 0.6 collective-permute-start.16
  67.0 0.0 collective-permute-done.18.theirs
  67.0 0.1 shard_map.93
  67.1 3.3 %collective-permute-start.19 = (bf16[16,1664]{1,0:T(8,128)(2,1)S(1)}, bf16[16,1664]{1,0:T(8,128)(2,1)S(1)}, u32[]{:S(2)}, u32[]{:S(2)}) collective-permute-start(bf16[16,1664]{1,0:T(8,128)(2,1)S(1)} %get-tuple-element.61), channel_id=1, source_target_pairs={{0,12},{4,0},{8,4},{12,8},{1,13},{5,1},{9,5},{13,9},{2,14},{6,2},{... | collective-permute-start | bytes 159752 | tf_op jit(solution)/shard_map/ppermute | solution.py:240
  70.4 1.1 %collective-permute-start.20 = (bf16[16,1664]{1,0:T(8,128)(2,1)S(1)}, bf16[16,1664]{1,0:T(8,128)(2,1)S(1)}, u32[]{:S(2)}, u32[]{:S(2)}) collective-permute-start(bf16[16,1664]{1,0:T(8,128)(2,1)S(1)} %get-tuple-element.62), channel_id=1, source_target_pairs={{0,8},{4,12},{8,0},{12,4},{1,9},{5,13},{9,1},{13,5},{2,10},{6,14},... | collective-permute-start | bytes 159752 | tf_op jit(solution)/shard_map/ppermute | solution.py:240
  71.5 0.0 collective-permute-done.14.refs_1_
  71.5 0.0 collective-permute-start.21
  71.5 0.4 copy.12.w_router
  71.9 0.3 shard_map.94
  72.2 0.3 collective-permute-done.15.refs_2_
  72.6 0.0 collective-permute-done.16.refs_3_
  72.6 0.9 %collective-permute-done.19.refs_5_ = bf16[16,1664]{1,0:T(8,128)(2,1)S(1)} collective-permute-done((bf16[16,1664]{1,0:T(8,128)(2,1)S(1)}, bf16[16,1664]{1,0:T(8,128)(2,1)S(1)}, u32[]{:S(2)}, u32[]{:S(2)}) %collective-permute-start.19) | collective-permute-done | bytes 53280 | tf_op jit(solution)/shard_map/ppermute | solution.py:240
  73.5 2.0 %collective-permute-done.20.refs_6_ = bf16[16,1664]{1,0:T(8,128)(2,1)S(1)} collective-permute-done((bf16[16,1664]{1,0:T(8,128)(2,1)S(1)}, bf16[16,1664]{1,0:T(8,128)(2,1)S(1)}, u32[]{:S(2)}, u32[]{:S(2)}) %collective-permute-start.20) | collective-permute-done | bytes 53280 | tf_op jit(solution)/shard_map/ppermute | solution.py:240
  75.5 2.0 %collective-permute-done.21.refs_7_ = bf16[16,1664]{1,0:T(8,128)(2,1)S(1)} collective-permute-done((bf16[16,1664]{1,0:T(8,128)(2,1)S(1)}, bf16[16,1664]{1,0:T(8,128)(2,1)S(1)}, u32[]{:S(2)}, u32[]{:S(2)}) %collective-permute-start.21) | collective-permute-done | bytes 53280 | tf_op jit(solution)/shard_map/ppermute | solution.py:240
  77.4 1.0 %shard_map.95 = (bf16[16,3072]{1,0:T(8,128)(2,1)}, f32[16,2]{1,0:T(8,128)S(1)}) custom-call(bf16[16,1536]{1,0:T(8,128)(2,1)S(1)} %get-tuple-element.48.refs_0_, bf16[16,1536]{1,0:T(8,128)(2,1)S(1)} %collective-permute-done.14.refs_1_, bf16[16,1536]{1,0:T(8,128)(2,1)S(1)} %collective-permute-done.15.refs_2_, ...), custom_call_target="tpu_custom_call" | custom-call | tf_op jit(solution)/shard_map/pallas_call | solution.py:217
  78.4 0.6 copy.14
  (8 shorter events, 0.1 us)
Async XLA Ops:
  0.6 15.3 %collective-permute-start = (bf16[16,3072]{1,0:T(8,128)(2,1)}, bf16[16,3072]{1,0:T(8,128)(2,1)S(1)}, u32[]{:S(2)}, u32[]{:S(2)}) collective-permute-start(bf16[16,3072]{1,0:T(8,128)(2,1)} %tokens), channel_id=1, source_target_pairs={{0,4},{4,8},{8,12},{12,0},{1,5},{5,9},{9,13},{13,1},{2,6},{6,10},{... | collective-permute-start | bytes 294920 | tf_op jit(solution)/shard_map/ppermute | solution.py:240
  3.7 12.2 %collective-permute-start.1 = (bf16[16,3072]{1,0:T(8,128)(2,1)}, bf16[16,3072]{1,0:T(8,128)(2,1)S(1)}, u32[]{:S(2)}, u32[]{:S(2)}) collective-permute-start(bf16[16,3072]{1,0:T(8,128)(2,1)} %tokens), channel_id=1, source_target_pairs={{0,8},{4,12},{8,0},{12,4},{1,9},{5,13},{9,1},{13,5},{2,10},{6,14},... | collective-permute-start | bytes 294920 | tf_op jit(solution)/shard_map/ppermute | solution.py:240
  6.3 9.6 %collective-permute-start.2 = (bf16[16,3072]{1,0:T(8,128)(2,1)}, bf16[16,3072]{1,0:T(8,128)(2,1)S(1)}, u32[]{:S(2)}, u32[]{:S(2)}) collective-permute-start(bf16[16,3072]{1,0:T(8,128)(2,1)} %tokens), channel_id=1, source_target_pairs={{0,12},{4,0},{8,4},{12,8},{1,13},{5,1},{9,5},{13,9},{2,14},{6,2},{... | collective-permute-start | bytes 294920 | tf_op jit(solution)/shard_map/ppermute | solution.py:240
  7.6 8.3 %copy-start = (bf16[16,3072]{1,0:T(8,128)(2,1)S(1)}, bf16[16,3072]{1,0:T(8,128)(2,1)}, u32[]{:S(2)}) copy-start(bf16[16,3072]{1,0:T(8,128)(2,1)} %tokens) | copy-start | bytes 294916
  7.6 8.3 %copy-start.2 = (bf16[16,3072]{1,0:T(8,128)(2,1)S(1)}, bf16[16,3072]{1,0:T(8,128)(2,1)}, u32[]{:S(2)}) copy-start(bf16[16,3072]{1,0:T(8,128)(2,1)} %param.8) | copy-start | bytes 294916
  16.0 7.5 %collective-permute-start.3 = (bf16[16,3072]{1,0:T(8,128)(2,1)S(1)}, bf16[16,3072]{1,0:T(8,128)(2,1)S(1)}, u32[]{:S(2)}, u32[]{:S(2)}) collective-permute-start(bf16[16,3072]{1,0:T(8,128)(2,1)S(1)} %copy-done.2), channel_id=1, source_target_pairs={{0,4},{4,8},{8,12},{12,0},{1,5},{5,9},{9,13},{13,1},{2,6},{6,10},{... | collective-permute-start | bytes 294920 | tf_op jit(solution)/shard_map/ppermute | solution.py:240
  16.7 9.8 %collective-permute-start.7 = (bf16[64,3072]{1,0:T(8,128)(2,1)S(1)}, bf16[64,3072]{1,0:T(8,128)(2,1)S(1)}, u32[]{:S(2)}, u32[]{:S(2)}) collective-permute-start(bf16[64,3072]{1,0:T(8,128)(2,1)S(1)} %pad_maximum_fusion.refs_0_), channel_id=1, source_target_pairs={{0,2},{1,3},{2,0},{3,1},{4,6},{5,7},{6,4},{7,5},{8,10},{9,11},{10,... | collective-permute-start | bytes 1179656 | tf_op jit(solution)/shard_map/ppermute | solution.py:243
  18.2 8.3 %collective-permute-start.4 = (bf16[16,3072]{1,0:T(8,128)(2,1)S(1)}, bf16[16,3072]{1,0:T(8,128)(2,1)S(1)}, u32[]{:S(2)}, u32[]{:S(2)}) collective-permute-start(bf16[16,3072]{1,0:T(8,128)(2,1)S(1)} %copy-done.2), channel_id=1, source_target_pairs={{0,8},{4,12},{8,0},{12,4},{1,9},{5,13},{9,1},{13,5},{2,10},{6,14},... | collective-permute-start | bytes 294920 | tf_op jit(solution)/shard_map/ppermute | solution.py:240
  19.0 7.6 %collective-permute-start.5 = (bf16[16,3072]{1,0:T(8,128)(2,1)S(1)}, bf16[16,3072]{1,0:T(8,128)(2,1)S(1)}, u32[]{:S(2)}, u32[]{:S(2)}) collective-permute-start(bf16[16,3072]{1,0:T(8,128)(2,1)S(1)} %copy-done.2), channel_id=1, source_target_pairs={{0,12},{4,0},{8,4},{12,8},{1,13},{5,1},{9,5},{13,9},{2,14},{6,2},{... | collective-permute-start | bytes 294920 | tf_op jit(solution)/shard_map/ppermute | solution.py:240
  21.5 6.9 %collective-permute-start.8 = (bf16[64,3072]{1,0:T(8,128)(2,1)S(1)}, bf16[64,3072]{1,0:T(8,128)(2,1)S(1)}, u32[]{:S(2)}, u32[]{:S(2)}) collective-permute-start(bf16[64,3072]{1,0:T(8,128)(2,1)S(1)} %pad_maximum_fusion.refs_0_), channel_id=1, source_target_pairs={{0,1},{1,0},{2,3},{3,2},{4,5},{5,4},{6,7},{7,6},{8,9},{9,8},{10,11... | collective-permute-start | bytes 1179656 | tf_op jit(solution)/shard_map/ppermute | solution.py:243
  26.5 1.9 %collective-permute-start.9 = (bf16[64,3072]{1,0:T(8,128)(2,1)S(1)}, bf16[64,3072]{1,0:T(8,128)(2,1)S(1)}, u32[]{:S(2)}, u32[]{:S(2)}) collective-permute-start(bf16[64,3072]{1,0:T(8,128)(2,1)S(1)} %collective-permute-done.7.refs_1_), channel_id=1, source_target_pairs={{0,1},{1,0},{2,3},{3,2},{4,5},{5,4},{6,7},{7,6},{8,9},{9,8},{10,11... | collective-permute-start | bytes 1179656 | tf_op jit(solution)/shard_map/ppermute | solution.py:243
  26.6 11.6 %collective-permute-start.6 = (bf16[64,3072]{1,0:T(8,128)(2,1)S(1)}, bf16[64,3072]{1,0:T(8,128)(2,1)S(1)}, u32[]{:S(2)}, u32[]{:S(2)}) collective-permute-start(bf16[64,3072]{1,0:T(8,128)(2,1)S(1)} %constant_dynamic-update-slice_fusion.refs_0_), channel_id=1, source_target_pairs={{0,2},{1,3},{2,0},{3,1},{4,6},{5,7},{6,4},{7,5},{8,10},{9,11},{10,... | collective-permute-start | bytes 1179656 | tf_op jit(solution)/shard_map/ppermute | solution.py:243
  28.1 10.0 %collective-permute-start.10 = (bf16[64,3072]{1,0:T(8,128)(2,1)S(1)}, bf16[64,3072]{1,0:T(8,128)(2,1)S(1)}, u32[]{:S(2)}, u32[]{:S(2)}) collective-permute-start(bf16[64,3072]{1,0:T(8,128)(2,1)S(1)} %constant_dynamic-update-slice_fusion.refs_0_), channel_id=1, source_target_pairs={{0,1},{1,0},{2,3},{3,2},{4,5},{5,4},{6,7},{7,6},{8,9},{9,8},{10,11... | collective-permute-start | bytes 1179656 | tf_op jit(solution)/shard_map/ppermute | solution.py:243
  38.2 1.7 %collective-permute-start.11 = (bf16[64,3072]{1,0:T(8,128)(2,1)S(1)}, bf16[64,3072]{1,0:T(8,128)(2,1)S(1)}, u32[]{:S(2)}, u32[]{:S(2)}) collective-permute-start(bf16[64,3072]{1,0:T(8,128)(2,1)S(1)} %collective-permute-done.6.refs_1_), channel_id=1, source_target_pairs={{0,1},{1,0},{2,3},{3,2},{4,5},{5,4},{6,7},{7,6},{8,9},{9,8},{10,11... | collective-permute-start | bytes 1179656 | tf_op jit(solution)/shard_map/ppermute | solution.py:243
  50.6 4.6 %collective-permute-start.12 = (bf16[128,1536]{1,0:T(8,128)(2,1)S(1)}, bf16[128,1536]{1,0:T(8,128)(2,1)S(1)}, u32[]{:S(2)}, u32[]{:S(2)}) collective-permute-start(bf16[128,1536]{1,0:T(8,128)(2,1)S(1)} %get-tuple-element.45), channel_id=1, source_target_pairs={{0,1},{1,0},{2,3},{3,2},{4,5},{5,4},{6,7},{7,6},{8,9},{9,8},{10,11... | collective-permute-start | bytes 1179656 | tf_op jit(solution)/shard_map/ppermute | solution.py:243
  50.8 15.5 %copy-start.1 = (bf16[3072,4]{0,1:T(4,128)(2,1)S(1)}, bf16[3072,4]{0,1:T(4,128)(2,1)}, u32[]{:S(2)}) copy-start(bf16[3072,4]{0,1:T(4,128)(2,1)} %param.10) | copy-start | bytes 73732
  50.8 15.5 %copy-start.3 = (s32[16,2]{0,1:T(2,128)S(1)}, s32[16,2]{0,1:T(2,128)}, u32[]{:S(2)}) copy-start(s32[16,2]{0,1:T(2,128)} %param.9) | copy-start | bytes 388
  54.7 2.1 %collective-permute-start.17 = (bf16[128,1664]{1,0:T(8,128)(2,1)S(1)}, bf16[128,1664]{1,0:T(8,128)(2,1)S(1)}, u32[]{:S(2)}, u32[]{:S(2)}) collective-permute-start(bf16[128,1664]{1,0:T(8,128)(2,1)S(1)} %get-tuple-element.57), channel_id=1, source_target_pairs={{0,1},{1,0},{2,3},{3,2},{4,5},{5,4},{6,7},{7,6},{8,9},{9,8},{10,11... | collective-permute-start | bytes 1277960 | tf_op jit(solution)/shard_map/ppermute | solution.py:243
  55.3 7.8 %collective-permute-start.13 = (bf16[64,1536]{1,0:T(8,128)(2,1)S(1)}, bf16[64,1536]{1,0:T(8,128)(2,1)S(1)}, u32[]{:S(2)}, u32[]{:S(2)}) collective-permute-start(bf16[64,1536]{1,0:T(8,128)(2,1)S(1)} %get-tuple-element.47), channel_id=1, source_target_pairs={{0,2},{1,3},{2,0},{3,1},{4,6},{5,7},{6,4},{7,5},{8,10},{9,11},{10,... | collective-permute-start | bytes 589832 | tf_op jit(solution)/shard_map/ppermute | solution.py:243
  57.1 9.9 %collective-permute-start.18 = (bf16[64,1664]{1,0:T(8,128)(2,1)S(1)}, bf16[64,1664]{1,0:T(8,128)(2,1)S(1)}, u32[]{:S(2)}, u32[]{:S(2)}) collective-permute-start(bf16[64,1664]{1,0:T(8,128)(2,1)S(1)} %get-tuple-element.59), channel_id=1, source_target_pairs={{0,2},{1,3},{2,0},{3,1},{4,6},{5,7},{6,4},{7,5},{8,10},{9,11},{10,... | collective-permute-start | bytes 638984 | tf_op jit(solution)/shard_map/ppermute | solution.py:243
  63.1 8.3 %collective-permute-start.14 = (bf16[16,1536]{1,0:T(8,128)(2,1)S(1)}, bf16[16,1536]{1,0:T(8,128)(2,1)S(1)}, u32[]{:S(2)}, u32[]{:S(2)}) collective-permute-start(bf16[16,1536]{1,0:T(8,128)(2,1)S(1)} %get-tuple-element.49), channel_id=1, source_target_pairs={{0,12},{4,0},{8,4},{12,8},{1,13},{5,1},{9,5},{13,9},{2,14},{6,2},{... | collective-permute-start | bytes 147464 | tf_op jit(solution)/shard_map/ppermute | solution.py:240
  66.4 6.2 %collective-permute-start.15 = (bf16[16,1536]{1,0:T(8,128)(2,1)S(1)}, bf16[16,1536]{1,0:T(8,128)(2,1)S(1)}, u32[]{:S(2)}, u32[]{:S(2)}) collective-permute-start(bf16[16,1536]{1,0:T(8,128)(2,1)S(1)} %get-tuple-element.50), channel_id=1, source_target_pairs={{0,8},{4,12},{8,0},{12,4},{1,9},{5,13},{9,1},{13,5},{2,10},{6,14},... | collective-permute-start | bytes 147464 | tf_op jit(solution)/shard_map/ppermute | solution.py:240
  66.4 6.2 %collective-permute-start.16 = (bf16[16,1536]{1,0:T(8,128)(2,1)S(1)}, bf16[16,1536]{1,0:T(8,128)(2,1)S(1)}, u32[]{:S(2)}, u32[]{:S(2)}) collective-permute-start(bf16[16,1536]{1,0:T(8,128)(2,1)S(1)} %get-tuple-element.51), channel_id=1, source_target_pairs={{0,4},{4,8},{8,12},{12,0},{1,5},{5,9},{9,13},{13,1},{2,6},{6,10},{... | collective-permute-start | bytes 147464 | tf_op jit(solution)/shard_map/ppermute | solution.py:240
  67.1 6.4 %collective-permute-start.19 = (bf16[16,1664]{1,0:T(8,128)(2,1)S(1)}, bf16[16,1664]{1,0:T(8,128)(2,1)S(1)}, u32[]{:S(2)}, u32[]{:S(2)}) collective-permute-start(bf16[16,1664]{1,0:T(8,128)(2,1)S(1)} %get-tuple-element.61), channel_id=1, source_target_pairs={{0,12},{4,0},{8,4},{12,8},{1,13},{5,1},{9,5},{13,9},{2,14},{6,2},{... | collective-permute-start | bytes 159752 | tf_op jit(solution)/shard_map/ppermute | solution.py:240
  70.4 5.0 %collective-permute-start.20 = (bf16[16,1664]{1,0:T(8,128)(2,1)S(1)}, bf16[16,1664]{1,0:T(8,128)(2,1)S(1)}, u32[]{:S(2)}, u32[]{:S(2)}) collective-permute-start(bf16[16,1664]{1,0:T(8,128)(2,1)S(1)} %get-tuple-element.62), channel_id=1, source_target_pairs={{0,8},{4,12},{8,0},{12,4},{1,9},{5,13},{9,1},{13,5},{2,10},{6,14},... | collective-permute-start | bytes 159752 | tf_op jit(solution)/shard_map/ppermute | solution.py:240
  71.5 5.9 %collective-permute-start.21 = (bf16[16,1664]{1,0:T(8,128)(2,1)S(1)}, bf16[16,1664]{1,0:T(8,128)(2,1)S(1)}, u32[]{:S(2)}, u32[]{:S(2)}) collective-permute-start(bf16[16,1664]{1,0:T(8,128)(2,1)S(1)} %get-tuple-element.63), channel_id=1, source_target_pairs={{0,4},{4,8},{8,12},{12,0},{1,5},{5,9},{9,13},{13,1},{2,6},{6,10},{... | collective-permute-start | bytes 159752 | tf_op jit(solution)/shard_map/ppermute | solution.py:240

commit v3 on v2

--- a/solution.py
+++ b/solution.py
@@ -11,7 +11,7 @@
 F32 = jnp.float32
 LANES = 128
 ROWS = 256
-GRANT = 19 << 20
+GRANT = 20 << 20
 AHEAD = 2
 NT = (((1,), (1,)), ((), ()))
 ANY = pl.BlockSpec(memory_space=pl.ANY)
@@ -27,6 +27,15 @@
     while extent % size:
         size -= LANES
     return size
+
+
+def pieces_of(extent):
+    parts, at = [], 0
+    while at < extent:
+        size = min(512 if at < 1024 else 1024, extent - at)
+        parts.append(pl.ds(at, size))
+        at += size
+    return parts
 
 
 def fetch(pieces, held, sems):
@@ -53,7 +62,7 @@
     pieces, (weights, both, _, held, sems) = refs[:n], refs[n:]
     fetch(pieces, held, sems)
     rows, ff = both.shape[1:]
-    block, step = min(rows, ROWS), chunk(ff, 512)
+    block, step = min(rows, ROWS), chunk(ff, 1024)
 
     @pl.loop(0, rows // block)
     def _(r):
@@ -100,7 +109,7 @@
 def sum_columns(start, width, r, block, grads, weights, keep, send):
     rows = grads.shape[1]
     at = pl.ds(pl.multiple_of(r * block, block), block)
-    step = chunk(width, 512)
+    step = chunk(width, 1536)
 
     @pl.loop(0, width // step)
     def _(d):
@@ -115,33 +124,28 @@
     pieces = refs[:n]
     weights, w_down, both, keep, send, grads, score, _, held, v_down, sems, down_sems = refs[n:]
     rows, ff = both.shape[1:]
-    block, step = min(rows, ROWS), chunk(ff, 512)
-
-    def load_down(f):
-        part = pl.ds(pl.multiple_of(f * step, step), step)
-        return pltpu.make_async_copy(w_down.at[part], v_down.at[part], down_sems.at[f])
-
-    load_down(0).start()
+    block = min(rows, ROWS)
+    parts = pieces_of(ff)
+    copies = [
+        pltpu.make_async_copy(w_down.at[part], v_down.at[part], down_sems.at[i]) for i, part in enumerate(parts)
+    ]
+    copies[0].start()
     fetch(pieces, held, sems)
-    for f in range(1, min(AHEAD, ff // step)):
-        load_down(f).start()
+    for copy in copies[1:AHEAD]:
+        copy.start()
 
     @pl.loop(0, rows // block)
     def _(r):
         at = pl.ds(pl.multiple_of(r * block, block), block)
         score[at, :] = jnp.zeros((block, 1), F32)
 
-        @pl.loop(0, ff // step)
-        def _(f):
-            cols = pl.ds(pl.multiple_of(f * step, step), step)
+        for f, cols in enumerate(parts):
 
             @pl.when(r == 0)
             def _():
-                load_down(f).wait()
-
-                @pl.when(f + AHEAD < ff // step)
-                def _():
-                    load_down(f + AHEAD).start()
+                copies[f].wait()
+                if f + AHEAD < len(copies):
+                    copies[f + AHEAD].start()
 
             back = dot_nt(held[at, :], v_down[cols, :])
             g, u = both[0, at, cols], both[1, at, cols]
@@ -182,8 +186,8 @@
 
 
 def route_kernel(tokens, w_router, routes, relative, weight, sign, pair):
-    experts = w_router.shape[1]
-    logits = jnp.dot(tokens[...], w_router[...], preferred_element_type=F32)
+    experts = w_router.shape[0]
+    logits = dot_nt(tokens[...], w_router[...])
     label = lax.broadcasted_iota(jnp.int32, logits.shape, 1)
     first, second = label == routes[:, 0:1], label == routes[:, 1:2]
     chosen = [jnp.sum(jnp.where(m, logits, 0.0), axis=1, keepdims=True) for m in (first, second)]
@@ -202,8 +206,9 @@
     for s, block in enumerate(second):
         gap = gap + sign[:, s : s + 1] * join3(block[:, pl.ds(out.shape[1] - lead, LANES)])
     grad = weight[:, n : n + 1] * gap
-    logit_grad[:, 0:1] = grad
-    logit_grad[:, 1:2] = -grad
+    turned = jnp.broadcast_to(grad, (grad.shape[0], LANES)).T
+    logit_grad[0:1, :] = turned[0:1, :]
+    logit_grad[1:2, :] = -turned[0:1, :]
     for blocks, cols in ((first, pl.ds(0, lead)), (second, pl.ds(lead, out.shape[1] - lead))):
         total = 0.0
         for s, block in enumerate(blocks):
@@ -237,7 +242,7 @@
     bits = bits[1:] + bits[:1]
 
     def along(x, shift):
-        return lax.ppermute(x, "expert", [(i, (i + shift) % experts) for i in range(experts)])
+        return lax.ppermute(x, "expert", [(i, i ^ shift) for i in range(experts)])
 
     def across(x, bit):
         return lax.ppermute(x, "hidden", [(i, i ^ bit) for i in range(hidden)])
@@ -247,7 +252,7 @@
     lead = width // 2
     rest = width - lead + LANES
     resident_bytes = rows * (2 * width + 8 * LANES) + rows * (ff * 4 + lead * 2 + rest * 2)
-    grant = GRANT if rows <= ROWS else resident_bytes + GRANT
+    grant = GRANT if rows <= ROWS else resident_bytes + (14 << 20)
     small = min(rows, 2048) * (width + LANES) * 4 + (1 << 20)
 
     def cost(weights, matmuls):
@@ -302,7 +307,7 @@
             held,
             pltpu.VMEM((ff, width), BF),
             pltpu.SemaphoreType.DMA((n,)),
-            pltpu.SemaphoreType.DMA((ff // chunk(ff, 512),)),
+            pltpu.SemaphoreType.DMA((len(pieces_of(ff)),)),
         ],
         grant,
         cost(3, 2),
@@ -317,10 +322,10 @@
         cost=cost(1, 1),
     )
     send_rest, routes, w_router, tokens = lax.optimization_barrier((send_rest, routes, w_router, tokens))
-    relative = (routes - lax.axis_index("expert")) % experts
+    relative = routes ^ lax.axis_index("expert")
     weight, sign, pair = call(
         route_kernel,
-        [tokens, w_router, routes, relative],
+        [tokens, w_router.T, routes, relative],
         [shape((own, experts + 1), F32), shape((own, experts), F32), shape((own, experts), F32)],
         [VMEM] * 4,
         limit=small,
@@ -336,17 +341,17 @@
         arrived = across(send, bits[0])
         outs = [shape((own, total), BF)] * experts
         blocks = call(add, [keep, arrived], outs, [VMEM] * 2, limit=small)
-        return [blocks[0]] + [along(blocks[s], experts - s) for s in range(1, experts)]
+        return [blocks[0]] + [along(blocks[s], s) for s in range(1, experts)]
 
     first, second = collect(keep, send, False), collect(keep_rest, send_rest, True)
     input_grad, logit_grad = call(
         functools.partial(final_kernel, experts),
         first + second + [weight, sign, pair, w_router.astype(F32).T],
-        [shape((own, width), BF), shape((own, 2), F32)],
+        [shape((own, width), BF), shape((2, own), F32)],
         [VMEM] * (2 * experts + 4),
         limit=small,
     )
-    return (input_grad, logit_grad)
+    return (input_grad, logit_grad.T)
 
 
 def solution(mesh):

time: 79.2 us -> 76.7 us (0.968)
  Pallas kernels: 32.6 us -> 31.2 us
  local copies, waits for them, and re-layouts: 1.19 us -> 0.13 us
    ppermute x10, waiting for transfers between devices: 11.2 us -> 12.6 us  [across(): return lax.ppermute(x, 'hidden', [(i, i ^ bit) for i in range(hidden)])]
    pallas_call x10, Pallas kernels: 32.6 us -> 31.2 us  [call(): pl.pallas_call(kernel, out_shape=outs, in_specs=specs, out_specs=[VMEM] *...]
    ppermute x10, starting transfers between devices: 6.87 us -> 5.64 us  [across(): return lax.ppermute(x, 'hidden', [(i, i ^ bit) for i in range(hidden)])]
    ppermute x12, waiting for transfers between devices: 7.19 us -> 6.31 us  [along(): return lax.ppermute(x, 'expert', [(i, i ^ shift) for i in range(experts)])]
  transfers between devices with their start and end apart: 22 -> 22, of which waited for: 9 -> 8; matrix products, arithmetic and copies ran while one was open for 1% -> 0% of each run, Pallas kernels for 26% -> 26%
where the time goes in v3:
time: 76.7 us; the launch traced here: 76.6 us
  Pallas kernels  31.2 us (41%)
  starting transfers between devices  25.4 us (33%)
  waiting for transfers between devices  18.9 us (25%)
  between operations  0.8 us (1%)
    pallas_call x10, Pallas kernels, call(): pl.pallas_call(kernel, out_shape=outs, in_specs=specs, out_specs=[VMEM] *...  31.2 us
    ppermute x12, starting transfers between devices, along(): return lax.ppermute(x, 'expert', [(i, i ^ shift) for i in range(experts)])  19.8 us
    ppermute x10, waiting for transfers between devices, across(): return lax.ppermute(x, 'hidden', [(i, i ^ bit) for i in range(hidden)])  12.6 us
    ppermute x12, waiting for transfers between devices, along(): return lax.ppermute(x, 'expert', [(i, i ^ shift) for i in range(experts)])  6.31 us
    ppermute x10, starting transfers between devices, across(): return lax.ppermute(x, 'hidden', [(i, i ^ bit) for i in range(hidden)])  5.64 us
  transfers between devices with their start and end apart: 22, of which 8 were waited for; matrix products, arithmetic and copies ran while one was open for 0% of the time, Pallas kernels for 26%

profile of v3, /device:TPU:0, one launch (start us, length us, event | category | flops | bytes accessed | tf_op | source)
XLA Modules:
  0.0 76.6 jit_solution(4452359864225402587)
XLA Ops:
  0.6 3.1 %collective-permute-start = (bf16[16,3072]{1,0:T(8,128)(2,1)}, bf16[16,3072]{1,0:T(8,128)(2,1)S(1)}, u32[]{:S(2)}, u32[]{:S(2)}) collective-permute-start(bf16[16,3072]{1,0:T(8,128)(2,1)} %tokens), channel_id=1, source_target_pairs={{0,4},{4,0},{8,12},{12,8},{1,5},{5,1},{9,13},{13,9},{2,6},{6,2},{1... | collective-permute-start | bytes 294920 | tf_op jit(solution)/shard_map/ppermute | solution.py:245
  3.7 2.6 %collective-permute-start.1 = (bf16[16,3072]{1,0:T(8,128)(2,1)}, bf16[16,3072]{1,0:T(8,128)(2,1)S(1)}, u32[]{:S(2)}, u32[]{:S(2)}) collective-permute-start(bf16[16,3072]{1,0:T(8,128)(2,1)} %tokens), channel_id=1, source_target_pairs={{0,8},{4,12},{8,0},{12,4},{1,9},{5,13},{9,1},{13,5},{2,10},{6,14},... | collective-permute-start | bytes 294920 | tf_op jit(solution)/shard_map/ppermute | solution.py:245
  6.3 0.0 collective-permute-start.2
  6.3 0.0 copy-start
  6.3 0.0 copy-start.2
  6.3 8.2 %shard_map.86.refs_4_ = bf16[2,3072,2048]{2,1,0:T(8,128)(2,1)S(1)} custom-call(bf16[3072,2048]{1,0:T(8,128)(2,1)} %bitcast.7, bf16[3072,2048]{1,0:T(8,128)(2,1)} %bitcast.8), custom_call_target="tpu_custom_call" | custom-call | bytes 25165824 | tf_op jit(solution)/shard_map/pallas_call | solution.py:222
  14.5 0.0 collective-permute-done
  14.6 0.0 collective-permute-done.1
  14.6 0.0 collective-permute-done.2
  14.6 0.0 copy-done
  14.6 0.0 copy-done.2
  14.6 1.5 %collective-permute-start.3 = (bf16[16,3072]{1,0:T(8,128)(2,1)S(1)}, bf16[16,3072]{1,0:T(8,128)(2,1)S(1)}, u32[]{:S(2)}, u32[]{:S(2)}) collective-permute-start(bf16[16,3072]{1,0:T(8,128)(2,1)S(1)} %copy-done.2), channel_id=1, source_target_pairs={{0,4},{4,0},{8,12},{12,8},{1,5},{5,1},{9,13},{13,9},{2,6},{6,2},{1... | collective-permute-start | bytes 294920 | tf_op jit(solution)/shard_map/ppermute | solution.py:245
  16.1 1.5 %collective-permute-start.7 = (bf16[64,3072]{1,0:T(8,128)(2,1)S(1)}, bf16[64,3072]{1,0:T(8,128)(2,1)S(1)}, u32[]{:S(2)}, u32[]{:S(2)}) collective-permute-start(bf16[64,3072]{1,0:T(8,128)(2,1)S(1)} %pad_maximum_fusion.refs_0_), channel_id=1, source_target_pairs={{0,2},{1,3},{2,0},{3,1},{4,6},{5,7},{6,4},{7,5},{8,10},{9,11},{10,... | collective-permute-start | bytes 1179656 | tf_op jit(solution)/shard_map/ppermute | solution.py:248
  17.6 3.0 %collective-permute-start.4 = (bf16[16,3072]{1,0:T(8,128)(2,1)S(1)}, bf16[16,3072]{1,0:T(8,128)(2,1)S(1)}, u32[]{:S(2)}, u32[]{:S(2)}) collective-permute-start(bf16[16,3072]{1,0:T(8,128)(2,1)S(1)} %copy-done.2), channel_id=1, source_target_pairs={{0,8},{4,12},{8,0},{12,4},{1,9},{5,13},{9,1},{13,5},{2,10},{6,14},... | collective-permute-start | bytes 294920 | tf_op jit(solution)/shard_map/ppermute | solution.py:245
  20.7 0.2 collective-permute-start.5
  20.9 0.0 collective-permute-start.8
  20.9 0.0 collective-permute-done.3
  20.9 4.6 %collective-permute-done.7.refs_1_ = bf16[64,3072]{1,0:T(8,128)(2,1)S(1)} collective-permute-done((bf16[64,3072]{1,0:T(8,128)(2,1)S(1)}, bf16[64,3072]{1,0:T(8,128)(2,1)S(1)}, u32[]{:S(2)}, u32[]{:S(2)}) %collective-permute-start.7) | collective-permute-done | bytes 393248 | tf_op jit(solution)/shard_map/ppermute | solution.py:248
  25.5 0.0 collective-permute-start.9
  25.5 1.8 %collective-permute-done.4 = bf16[16,3072]{1,0:T(8,128)(2,1)S(1)} collective-permute-done((bf16[16,3072]{1,0:T(8,128)(2,1)S(1)}, bf16[16,3072]{1,0:T(8,128)(2,1)S(1)}, u32[]{:S(2)}, u32[]{:S(2)}) %collective-permute-start.4) | collective-permute-done | bytes 98336 | tf_op jit(solution)/shard_map/ppermute | solution.py:245
  27.3 0.0 collective-permute-done.5
  27.4 0.6 collective-permute-start.6
  27.9 0.0 collective-permute-start.10
  27.9 0.0 collective-permute-done.8.refs_2_
  27.9 0.0 collective-permute-done.9.refs_3_
  28.0 7.6 %shard_map.87 = (f32[2,256,2048]{2,1,0:T(8,128)S(1)}, bf16[2,3072,2048]{2,1,0:T(8,128)(2,1)S(1)}) custom-call(bf16[64,3072]{1,0:T(8,128)(2,1)S(1)} %pad_maximum_fusion.refs_0_, bf16[64,3072]{1,0:T(8,128)(2,1)S(1)} %collective-permute-done.7.refs_1_, bf16[64,3072]{1,0:T(8,128)(2,1)S(1)} %collective-permute-done.8.refs_2_, ...), custom_call_target="tpu_custom_call", output_to_operand_aliasing={{1}: (4, {})} | custom-call | flops 6442450944 | bytes 25165824 | tf_op jit(solution)/shard_map/pallas_call | solution.py:222
  35.6 1.6 %collective-permute-done.6.refs_1_ = bf16[64,3072]{1,0:T(8,128)(2,1)S(1)} collective-permute-done((bf16[64,3072]{1,0:T(8,128)(2,1)S(1)}, bf16[64,3072]{1,0:T(8,128)(2,1)S(1)}, u32[]{:S(2)}, u32[]{:S(2)}) %collective-permute-start.6) | collective-permute-done | bytes 393248 | tf_op jit(solution)/shard_map/ppermute | solution.py:248
  37.2 0.0 collective-permute-start.11
  37.2 0.0 collective-permute-done.10.refs_2_
  37.2 1.7 %collective-permute-done.11.refs_3_ = bf16[64,3072]{1,0:T(8,128)(2,1)S(1)} collective-permute-done((bf16[64,3072]{1,0:T(8,128)(2,1)S(1)}, bf16[64,3072]{1,0:T(8,128)(2,1)S(1)}, u32[]{:S(2)}, u32[]{:S(2)}) %collective-permute-start.11) | collective-permute-done | bytes 393248 | tf_op jit(solution)/shard_map/ppermute | solution.py:248
  38.9 10.2 %shard_map.88 = (bf16[128,1536]{1,0:T(8,128)(2,1)S(1)}, bf16[128,1536]{1,0:T(8,128)(2,1)S(1)}, bf16[2,256,2048]{2,1,0:T(8,128)(2,1)S(1)}, f32[256,1]{1,0:T(8,128)S(1)}, bf16[2,3072,2048]{2,1,0:T(8,128)(2,1)S(1)}) custom-call(bf16[64,3072]{1,0:T(8,128)(2,1)S(1)} %constant_dynamic-update-slice_fusion.refs_0_, ...), custom_call_target="tpu_custom_call", output_to_operand_aliasing={{4}: (4, {})} | custom-call | flops 6442450944 | bytes 37748736 | tf_op jit(solution)/shard_map/pallas_call | solution.py:222
  49.1 0.2 collective-permute-start.12
  49.3 0.0 copy-start.1
  49.3 0.0 copy-start.3
  49.3 3.4 %shard_map.91 = (bf16[128,1664]{1,0:T(8,128)(2,1)S(1)}, bf16[128,1664]{1,0:T(8,128)(2,1)S(1)}) custom-call(bf16[2,3072,2048]{2,1,0:T(8,128)(2,1)S(1)} %get-tuple-element.54.weights, bf16[2,256,2048]{2,1,0:T(8,128)(2,1)S(1)} %get-tuple-element.55.grads, f32[256,1]{1,0:T(8,128)S(1)} %get-tuple-element.56.score), custom_call_target="tpu_custom_call" | custom-call | flops 3221225472 | bytes 12582912 | tf_op jit(solution)/shard_map/pallas_call | solution.py:222
  52.8 0.4 collective-permute-start.17
  53.2 0.0 collective-permute-done.12.theirs
  53.2 0.1 shard_map.89
  53.3 1.6 %collective-permute-start.13 = (bf16[64,1536]{1,0:T(8,128)(2,1)S(1)}, bf16[64,1536]{1,0:T(8,128)(2,1)S(1)}, u32[]{:S(2)}, u32[]{:S(2)}) collective-permute-start(bf16[64,1536]{1,0:T(8,128)(2,1)S(1)} %get-tuple-element.49), channel_id=1, source_target_pairs={{0,2},{1,3},{2,0},{3,1},{4,6},{5,7},{6,4},{7,5},{8,10},{9,11},{10,... | collective-permute-start | bytes 589832 | tf_op jit(solution)/shard_map/ppermute | solution.py:248
  54.9 0.0 collective-permute-done.17.theirs
  54.9 0.2 shard_map.92
  55.1 1.3 %collective-permute-start.18 = (bf16[64,1664]{1,0:T(8,128)(2,1)S(1)}, bf16[64,1664]{1,0:T(8,128)(2,1)S(1)}, u32[]{:S(2)}, u32[]{:S(2)}) collective-permute-start(bf16[64,1664]{1,0:T(8,128)(2,1)S(1)} %get-tuple-element.61), channel_id=1, source_target_pairs={{0,2},{1,3},{2,0},{3,1},{4,6},{5,7},{6,4},{7,5},{8,10},{9,11},{10,... | collective-permute-start | bytes 638984 | tf_op jit(solution)/shard_map/ppermute | solution.py:248
  56.4 4.7 %collective-permute-done.13.theirs = bf16[64,1536]{1,0:T(8,128)(2,1)S(1)} collective-permute-done((bf16[64,1536]{1,0:T(8,128)(2,1)S(1)}, bf16[64,1536]{1,0:T(8,128)(2,1)S(1)}, u32[]{:S(2)}, u32[]{:S(2)}) %collective-permute-start.13) | collective-permute-done | bytes 196640 | tf_op jit(solution)/shard_map/ppermute | solution.py:248
  61.2 1.3 %collective-permute-start.14 = (bf16[16,1536]{1,0:T(8,128)(2,1)S(1)}, bf16[16,1536]{1,0:T(8,128)(2,1)S(1)}, u32[]{:S(2)}, u32[]{:S(2)}) collective-permute-start(bf16[16,1536]{1,0:T(8,128)(2,1)S(1)} %get-tuple-element.51), channel_id=1, source_target_pairs={{0,4},{4,0},{8,12},{12,8},{1,5},{5,1},{9,13},{13,9},{2,6},{6,2},{1... | collective-permute-start | bytes 147464 | tf_op jit(solution)/shard_map/ppermute | solution.py:245
  62.5 0.0 copy-done.1
  62.5 0.0 copy-done.3
  62.5 0.1 copy.15.routes
  62.6 2.4 %collective-permute-start.15 = (bf16[16,1536]{1,0:T(8,128)(2,1)S(1)}, bf16[16,1536]{1,0:T(8,128)(2,1)S(1)}, u32[]{:S(2)}, u32[]{:S(2)}) collective-permute-start(bf16[16,1536]{1,0:T(8,128)(2,1)S(1)} %get-tuple-element.52), channel_id=1, source_target_pairs={{0,8},{4,12},{8,0},{12,4},{1,9},{5,13},{9,1},{13,5},{2,10},{6,14},... | collective-permute-start | bytes 147464 | tf_op jit(solution)/shard_map/ppermute | solution.py:245
  65.0 1.2 %collective-permute-start.16 = (bf16[16,1536]{1,0:T(8,128)(2,1)S(1)}, bf16[16,1536]{1,0:T(8,128)(2,1)S(1)}, u32[]{:S(2)}, u32[]{:S(2)}) collective-permute-start(bf16[16,1536]{1,0:T(8,128)(2,1)S(1)} %get-tuple-element.53), channel_id=1, source_target_pairs={{0,12},{4,8},{8,4},{12,0},{1,13},{5,9},{9,5},{13,1},{2,14},{6,10},... | collective-permute-start | bytes 147464 | tf_op jit(solution)/shard_map/ppermute | solution.py:245
  66.2 0.0 collective-permute-done.18.theirs
  66.2 0.1 shard_map.93
  66.3 0.6 collective-permute-start.19
  66.9 2.7 %collective-permute-start.20 = (bf16[16,1664]{1,0:T(8,128)(2,1)S(1)}, bf16[16,1664]{1,0:T(8,128)(2,1)S(1)}, u32[]{:S(2)}, u32[]{:S(2)}) collective-permute-start(bf16[16,1664]{1,0:T(8,128)(2,1)S(1)} %get-tuple-element.64), channel_id=1, source_target_pairs={{0,8},{4,12},{8,0},{12,4},{1,9},{5,13},{9,1},{13,5},{2,10},{6,14},... | collective-permute-start | bytes 159752 | tf_op jit(solution)/shard_map/ppermute | solution.py:245
  69.6 0.0 collective-permute-done.14.refs_1_
  69.6 1.2 %collective-permute-start.21 = (bf16[16,1664]{1,0:T(8,128)(2,1)S(1)}, bf16[16,1664]{1,0:T(8,128)(2,1)S(1)}, u32[]{:S(2)}, u32[]{:S(2)}) collective-permute-start(bf16[16,1664]{1,0:T(8,128)(2,1)S(1)} %get-tuple-element.65), channel_id=1, source_target_pairs={{0,12},{4,8},{8,4},{12,0},{1,13},{5,9},{9,5},{13,1},{2,14},{6,10},... | collective-permute-start | bytes 159752 | tf_op jit(solution)/shard_map/ppermute | solution.py:245
  70.8 0.2 shard_map.94
  71.0 0.0 collective-permute-done.15.refs_2_
  71.0 0.4 collective-permute-done.16.refs_3_
  71.4 0.0 collective-permute-done.19.refs_5_
  71.4 2.3 %collective-permute-done.20.refs_6_ = bf16[16,1664]{1,0:T(8,128)(2,1)S(1)} collective-permute-done((bf16[16,1664]{1,0:T(8,128)(2,1)S(1)}, bf16[16,1664]{1,0:T(8,128)(2,1)S(1)}, u32[]{:S(2)}, u32[]{:S(2)}) %collective-permute-start.20) | collective-permute-done | bytes 53280 | tf_op jit(solution)/shard_map/ppermute | solution.py:245
  73.6 1.9 %collective-permute-done.21.refs_7_ = bf16[16,1664]{1,0:T(8,128)(2,1)S(1)} collective-permute-done((bf16[16,1664]{1,0:T(8,128)(2,1)S(1)}, bf16[16,1664]{1,0:T(8,128)(2,1)S(1)}, u32[]{:S(2)}, u32[]{:S(2)}) %collective-permute-start.21) | collective-permute-done | bytes 53280 | tf_op jit(solution)/shard_map/ppermute | solution.py:245
  75.5 1.1 %shard_map.95 = (bf16[16,3072]{1,0:T(8,128)(2,1)}, f32[2,16]{1,0:T(2,128)}) custom-call(bf16[16,1536]{1,0:T(8,128)(2,1)S(1)} %get-tuple-element.50.refs_0_, bf16[16,1536]{1,0:T(8,128)(2,1)S(1)} %collective-permute-done.14.refs_1_, bf16[16,1536]{1,0:T(8,128)(2,1)S(1)} %collective-permute-done.15.refs_2_, ...), custom_call_target="tpu_custom_call" | custom-call | tf_op jit(solution)/shard_map/pallas_call | solution.py:222
  (8 shorter events, 0.1 us)
Async XLA Ops:
  0.6 13.9 %collective-permute-start = (bf16[16,3072]{1,0:T(8,128)(2,1)}, bf16[16,3072]{1,0:T(8,128)(2,1)S(1)}, u32[]{:S(2)}, u32[]{:S(2)}) collective-permute-start(bf16[16,3072]{1,0:T(8,128)(2,1)} %tokens), channel_id=1, source_target_pairs={{0,4},{4,0},{8,12},{12,8},{1,5},{5,1},{9,13},{13,9},{2,6},{6,2},{1... | collective-permute-start | bytes 294920 | tf_op jit(solution)/shard_map/ppermute | solution.py:245
  3.7 10.8 %collective-permute-start.1 = (bf16[16,3072]{1,0:T(8,128)(2,1)}, bf16[16,3072]{1,0:T(8,128)(2,1)S(1)}, u32[]{:S(2)}, u32[]{:S(2)}) collective-permute-start(bf16[16,3072]{1,0:T(8,128)(2,1)} %tokens), channel_id=1, source_target_pairs={{0,8},{4,12},{8,0},{12,4},{1,9},{5,13},{9,1},{13,5},{2,10},{6,14},... | collective-permute-start | bytes 294920 | tf_op jit(solution)/shard_map/ppermute | solution.py:245
  6.3 8.3 %collective-permute-start.2 = (bf16[16,3072]{1,0:T(8,128)(2,1)}, bf16[16,3072]{1,0:T(8,128)(2,1)S(1)}, u32[]{:S(2)}, u32[]{:S(2)}) collective-permute-start(bf16[16,3072]{1,0:T(8,128)(2,1)} %tokens), channel_id=1, source_target_pairs={{0,12},{4,8},{8,4},{12,0},{1,13},{5,9},{9,5},{13,1},{2,14},{6,10},... | collective-permute-start | bytes 294920 | tf_op jit(solution)/shard_map/ppermute | solution.py:245
  6.3 8.3 %copy-start = (bf16[16,3072]{1,0:T(8,128)(2,1)S(1)}, bf16[16,3072]{1,0:T(8,128)(2,1)}, u32[]{:S(2)}) copy-start(bf16[16,3072]{1,0:T(8,128)(2,1)} %tokens) | copy-start | bytes 294916
  6.3 8.3 %copy-start.2 = (bf16[16,3072]{1,0:T(8,128)(2,1)S(1)}, bf16[16,3072]{1,0:T(8,128)(2,1)}, u32[]{:S(2)}) copy-start(bf16[16,3072]{1,0:T(8,128)(2,1)} %param.8) | copy-start | bytes 294916
  14.6 6.3 %collective-permute-start.3 = (bf16[16,3072]{1,0:T(8,128)(2,1)S(1)}, bf16[16,3072]{1,0:T(8,128)(2,1)S(1)}, u32[]{:S(2)}, u32[]{:S(2)}) collective-permute-start(bf16[16,3072]{1,0:T(8,128)(2,1)S(1)} %copy-done.2), channel_id=1, source_target_pairs={{0,4},{4,0},{8,12},{12,8},{1,5},{5,1},{9,13},{13,9},{2,6},{6,2},{1... | collective-permute-start | bytes 294920 | tf_op jit(solution)/shard_map/ppermute | solution.py:245
  16.1 9.4 %collective-permute-start.7 = (bf16[64,3072]{1,0:T(8,128)(2,1)S(1)}, bf16[64,3072]{1,0:T(8,128)(2,1)S(1)}, u32[]{:S(2)}, u32[]{:S(2)}) collective-permute-start(bf16[64,3072]{1,0:T(8,128)(2,1)S(1)} %pad_maximum_fusion.refs_0_), channel_id=1, source_target_pairs={{0,2},{1,3},{2,0},{3,1},{4,6},{5,7},{6,4},{7,5},{8,10},{9,11},{10,... | collective-permute-start | bytes 1179656 | tf_op jit(solution)/shard_map/ppermute | solution.py:248
  17.6 9.7 %collective-permute-start.4 = (bf16[16,3072]{1,0:T(8,128)(2,1)S(1)}, bf16[16,3072]{1,0:T(8,128)(2,1)S(1)}, u32[]{:S(2)}, u32[]{:S(2)}) collective-permute-start(bf16[16,3072]{1,0:T(8,128)(2,1)S(1)} %copy-done.2), channel_id=1, source_target_pairs={{0,8},{4,12},{8,0},{12,4},{1,9},{5,13},{9,1},{13,5},{2,10},{6,14},... | collective-permute-start | bytes 294920 | tf_op jit(solution)/shard_map/ppermute | solution.py:245
  20.7 6.7 %collective-permute-start.5 = (bf16[16,3072]{1,0:T(8,128)(2,1)S(1)}, bf16[16,3072]{1,0:T(8,128)(2,1)S(1)}, u32[]{:S(2)}, u32[]{:S(2)}) collective-permute-start(bf16[16,3072]{1,0:T(8,128)(2,1)S(1)} %copy-done.2), channel_id=1, source_target_pairs={{0,12},{4,8},{8,4},{12,0},{1,13},{5,9},{9,5},{13,1},{2,14},{6,10},... | collective-permute-start | bytes 294920 | tf_op jit(solution)/shard_map/ppermute | solution.py:245
  20.9 7.1 %collective-permute-start.8 = (bf16[64,3072]{1,0:T(8,128)(2,1)S(1)}, bf16[64,3072]{1,0:T(8,128)(2,1)S(1)}, u32[]{:S(2)}, u32[]{:S(2)}) collective-permute-start(bf16[64,3072]{1,0:T(8,128)(2,1)S(1)} %pad_maximum_fusion.refs_0_), channel_id=1, source_target_pairs={{0,1},{1,0},{2,3},{3,2},{4,5},{5,4},{6,7},{7,6},{8,9},{9,8},{10,11... | collective-permute-start | bytes 1179656 | tf_op jit(solution)/shard_map/ppermute | solution.py:248
  25.5 2.4 %collective-permute-start.9 = (bf16[64,3072]{1,0:T(8,128)(2,1)S(1)}, bf16[64,3072]{1,0:T(8,128)(2,1)S(1)}, u32[]{:S(2)}, u32[]{:S(2)}) collective-permute-start(bf16[64,3072]{1,0:T(8,128)(2,1)S(1)} %collective-permute-done.7.refs_1_), channel_id=1, source_target_pairs={{0,1},{1,0},{2,3},{3,2},{4,5},{5,4},{6,7},{7,6},{8,9},{9,8},{10,11... | collective-permute-start | bytes 1179656 | tf_op jit(solution)/shard_map/ppermute | solution.py:248
  27.4 9.8 %collective-permute-start.6 = (bf16[64,3072]{1,0:T(8,128)(2,1)S(1)}, bf16[64,3072]{1,0:T(8,128)(2,1)S(1)}, u32[]{:S(2)}, u32[]{:S(2)}) collective-permute-start(bf16[64,3072]{1,0:T(8,128)(2,1)S(1)} %constant_dynamic-update-slice_fusion.refs_0_), channel_id=1, source_target_pairs={{0,2},{1,3},{2,0},{3,1},{4,6},{5,7},{6,4},{7,5},{8,10},{9,11},{10,... | collective-permute-start | bytes 1179656 | tf_op jit(solution)/shard_map/ppermute | solution.py:248
  27.9 9.2 %collective-permute-start.10 = (bf16[64,3072]{1,0:T(8,128)(2,1)S(1)}, bf16[64,3072]{1,0:T(8,128)(2,1)S(1)}, u32[]{:S(2)}, u32[]{:S(2)}) collective-permute-start(bf16[64,3072]{1,0:T(8,128)(2,1)S(1)} %constant_dynamic-update-slice_fusion.refs_0_), channel_id=1, source_target_pairs={{0,1},{1,0},{2,3},{3,2},{4,5},{5,4},{6,7},{7,6},{8,9},{9,8},{10,11... | collective-permute-start | bytes 1179656 | tf_op jit(solution)/shard_map/ppermute | solution.py:248
  37.2 1.7 %collective-permute-start.11 = (bf16[64,3072]{1,0:T(8,128)(2,1)S(1)}, bf16[64,3072]{1,0:T(8,128)(2,1)S(1)}, u32[]{:S(2)}, u32[]{:S(2)}) collective-permute-start(bf16[64,3072]{1,0:T(8,128)(2,1)S(1)} %collective-permute-done.6.refs_1_), channel_id=1, source_target_pairs={{0,1},{1,0},{2,3},{3,2},{4,5},{5,4},{6,7},{7,6},{8,9},{9,8},{10,11... | collective-permute-start | bytes 1179656 | tf_op jit(solution)/shard_map/ppermute | solution.py:248
  49.1 4.1 %collective-permute-start.12 = (bf16[128,1536]{1,0:T(8,128)(2,1)S(1)}, bf16[128,1536]{1,0:T(8,128)(2,1)S(1)}, u32[]{:S(2)}, u32[]{:S(2)}) collective-permute-start(bf16[128,1536]{1,0:T(8,128)(2,1)S(1)} %get-tuple-element.47), channel_id=1, source_target_pairs={{0,1},{1,0},{2,3},{3,2},{4,5},{5,4},{6,7},{7,6},{8,9},{9,8},{10,11... | collective-permute-start | bytes 1179656 | tf_op jit(solution)/shard_map/ppermute | solution.py:248
  49.3 13.1 %copy-start.1 = (bf16[3072,4]{0,1:T(4,128)(2,1)S(1)}, bf16[3072,4]{0,1:T(4,128)(2,1)}, u32[]{:S(2)}) copy-start(bf16[3072,4]{0,1:T(4,128)(2,1)} %param.10) | copy-start | bytes 73732
  49.3 13.1 %copy-start.3 = (s32[16,2]{0,1:T(2,128)S(1)}, s32[16,2]{0,1:T(2,128)}, u32[]{:S(2)}) copy-start(s32[16,2]{0,1:T(2,128)} %param.9) | copy-start | bytes 388
  52.8 2.1 %collective-permute-start.17 = (bf16[128,1664]{1,0:T(8,128)(2,1)S(1)}, bf16[128,1664]{1,0:T(8,128)(2,1)S(1)}, u32[]{:S(2)}, u32[]{:S(2)}) collective-permute-start(bf16[128,1664]{1,0:T(8,128)(2,1)S(1)} %get-tuple-element.59), channel_id=1, source_target_pairs={{0,1},{1,0},{2,3},{3,2},{4,5},{5,4},{6,7},{7,6},{8,9},{9,8},{10,11... | collective-permute-start | bytes 1277960 | tf_op jit(solution)/shard_map/ppermute | solution.py:248
  53.3 7.8 %collective-permute-start.13 = (bf16[64,1536]{1,0:T(8,128)(2,1)S(1)}, bf16[64,1536]{1,0:T(8,128)(2,1)S(1)}, u32[]{:S(2)}, u32[]{:S(2)}) collective-permute-start(bf16[64,1536]{1,0:T(8,128)(2,1)S(1)} %get-tuple-element.49), channel_id=1, source_target_pairs={{0,2},{1,3},{2,0},{3,1},{4,6},{5,7},{6,4},{7,5},{8,10},{9,11},{10,... | collective-permute-start | bytes 589832 | tf_op jit(solution)/shard_map/ppermute | solution.py:248
  55.1 11.1 %collective-permute-start.18 = (bf16[64,1664]{1,0:T(8,128)(2,1)S(1)}, bf16[64,1664]{1,0:T(8,128)(2,1)S(1)}, u32[]{:S(2)}, u32[]{:S(2)}) collective-permute-start(bf16[64,1664]{1,0:T(8,128)(2,1)S(1)} %get-tuple-element.61), channel_id=1, source_target_pairs={{0,2},{1,3},{2,0},{3,1},{4,6},{5,7},{6,4},{7,5},{8,10},{9,11},{10,... | collective-permute-start | bytes 638984 | tf_op jit(solution)/shard_map/ppermute | solution.py:248
  61.2 8.4 %collective-permute-start.14 = (bf16[16,1536]{1,0:T(8,128)(2,1)S(1)}, bf16[16,1536]{1,0:T(8,128)(2,1)S(1)}, u32[]{:S(2)}, u32[]{:S(2)}) collective-permute-start(bf16[16,1536]{1,0:T(8,128)(2,1)S(1)} %get-tuple-element.51), channel_id=1, source_target_pairs={{0,4},{4,0},{8,12},{12,8},{1,5},{5,1},{9,13},{13,9},{2,6},{6,2},{1... | collective-permute-start | bytes 147464 | tf_op jit(solution)/shard_map/ppermute | solution.py:245
  62.6 8.4 %collective-permute-start.15 = (bf16[16,1536]{1,0:T(8,128)(2,1)S(1)}, bf16[16,1536]{1,0:T(8,128)(2,1)S(1)}, u32[]{:S(2)}, u32[]{:S(2)}) collective-permute-start(bf16[16,1536]{1,0:T(8,128)(2,1)S(1)} %get-tuple-element.52), channel_id=1, source_target_pairs={{0,8},{4,12},{8,0},{12,4},{1,9},{5,13},{9,1},{13,5},{2,10},{6,14},... | collective-permute-start | bytes 147464 | tf_op jit(solution)/shard_map/ppermute | solution.py:245
  65.0 6.4 %collective-permute-start.16 = (bf16[16,1536]{1,0:T(8,128)(2,1)S(1)}, bf16[16,1536]{1,0:T(8,128)(2,1)S(1)}, u32[]{:S(2)}, u32[]{:S(2)}) collective-permute-start(bf16[16,1536]{1,0:T(8,128)(2,1)S(1)} %get-tuple-element.53), channel_id=1, source_target_pairs={{0,12},{4,8},{8,4},{12,0},{1,13},{5,9},{9,5},{13,1},{2,14},{6,10},... | collective-permute-start | bytes 147464 | tf_op jit(solution)/shard_map/ppermute | solution.py:245
  66.3 5.1 %collective-permute-start.19 = (bf16[16,1664]{1,0:T(8,128)(2,1)S(1)}, bf16[16,1664]{1,0:T(8,128)(2,1)S(1)}, u32[]{:S(2)}, u32[]{:S(2)}) collective-permute-start(bf16[16,1664]{1,0:T(8,128)(2,1)S(1)} %get-tuple-element.63), channel_id=1, source_target_pairs={{0,4},{4,0},{8,12},{12,8},{1,5},{5,1},{9,13},{13,9},{2,6},{6,2},{1... | collective-permute-start | bytes 159752 | tf_op jit(solution)/shard_map/ppermute | solution.py:245
  66.9 6.8 %collective-permute-start.20 = (bf16[16,1664]{1,0:T(8,128)(2,1)S(1)}, bf16[16,1664]{1,0:T(8,128)(2,1)S(1)}, u32[]{:S(2)}, u32[]{:S(2)}) collective-permute-start(bf16[16,1664]{1,0:T(8,128)(2,1)S(1)} %get-tuple-element.64), channel_id=1, source_target_pairs={{0,8},{4,12},{8,0},{12,4},{1,9},{5,13},{9,1},{13,5},{2,10},{6,14},... | collective-permute-start | bytes 159752 | tf_op jit(solution)/shard_map/ppermute | solution.py:245
  69.6 5.9 %collective-permute-start.21 = (bf16[16,1664]{1,0:T(8,128)(2,1)S(1)}, bf16[16,1664]{1,0:T(8,128)(2,1)S(1)}, u32[]{:S(2)}, u32[]{:S(2)}) collective-permute-start(bf16[16,1664]{1,0:T(8,128)(2,1)S(1)} %get-tuple-element.65), channel_id=1, source_target_pairs={{0,12},{4,8},{8,4},{12,0},{1,13},{5,9},{9,5},{13,1},{2,14},{6,10},... | collective-permute-start | bytes 159752 | tf_op jit(solution)/shard_map/ppermute | solution.py:245

commit v4 on v3

--- a/solution.py
+++ b/solution.py
@@ -11,8 +11,7 @@
 F32 = jnp.float32
 LANES = 128
 ROWS = 256
-GRANT = 20 << 20
-AHEAD = 2
+GRANT = 15 << 20
 NT = (((1,), (1,)), ((), ()))
 ANY = pl.BlockSpec(memory_space=pl.ANY)
 VMEM = pl.BlockSpec(memory_space=pltpu.VMEM)
@@ -27,15 +26,6 @@
     while extent % size:
         size -= LANES
     return size
-
-
-def pieces_of(extent):
-    parts, at = [], 0
-    while at < extent:
-        size = min(512 if at < 1024 else 1024, extent - at)
-        parts.append(pl.ds(at, size))
-        at += size
-    return parts
 
 
 def fetch(pieces, held, sems):
@@ -50,16 +40,16 @@
         copy.wait()
 
 
-def load_kernel(first, second, target, sems):
-    copies = [pltpu.make_async_copy(w, target.at[i], sems.at[i]) for i, w in enumerate((first, second))]
-    for copy in copies:
-        copy.start()
-    for copy in copies:
-        copy.wait()
+def load_kernel(k, source, *refs):
+    copy = pltpu.make_async_copy(source, refs[-2].at[k], refs[-1])
+    copy.start()
+    copy.wait()
 
 
 def gate_up_kernel(n, *refs):
-    pieces, (weights, both, _, held, sems) = refs[:n], refs[n:]
+    pieces, (weights, w_down, both, _, near_down, held, sems) = refs[:n], refs[n:]
+    copy = pltpu.make_async_copy(w_down.at[pl.ds(0, near_down.shape[0])], near_down, sems.at[n])
+    copy.start()
     fetch(pieces, held, sems)
     rows, ff = both.shape[1:]
     block, step = min(rows, ROWS), chunk(ff, 1024)
@@ -73,6 +63,8 @@
             cols = pl.ds(pl.multiple_of(f * step, step), step)
             for k in range(2):
                 both[k, at, cols] = jnp.dot(held[at, :], weights[k, :, cols], preferred_element_type=F32)
+
+    copy.wait()
 
 
 def split3(score):
@@ -122,32 +114,30 @@
 
 def back_kernel(n, *refs):
     pieces = refs[:n]
-    weights, w_down, both, keep, send, grads, score, _, held, v_down, sems, down_sems = refs[n:]
+    weights, w_down, near_down, both, keep, send, grads, score, _, held, v_down, sem, sems = refs[n:]
     rows, ff = both.shape[1:]
     block = min(rows, ROWS)
-    parts = pieces_of(ff)
-    copies = [
-        pltpu.make_async_copy(w_down.at[part], v_down.at[part], down_sems.at[i]) for i, part in enumerate(parts)
-    ]
-    copies[0].start()
+    near = near_down.shape[0]
+    step = chunk(near, 1024)
+    copy = pltpu.make_async_copy(w_down.at[pl.ds(near, ff - near)], v_down, sem)
+    copy.start()
     fetch(pieces, held, sems)
-    for copy in copies[1:AHEAD]:
-        copy.start()
 
     @pl.loop(0, rows // block)
     def _(r):
         at = pl.ds(pl.multiple_of(r * block, block), block)
         score[at, :] = jnp.zeros((block, 1), F32)
 
-        for f, cols in enumerate(parts):
-
-            @pl.when(r == 0)
-            def _():
-                copies[f].wait()
-                if f + AHEAD < len(copies):
-                    copies[f + AHEAD].start()
-
-            back = dot_nt(held[at, :], v_down[cols, :])
+        for f in range(ff // step):
+            cols = pl.ds(f * step, step)
+            if f * step == near:
+
+                @pl.when(r == 0)
+                def _():
+                    copy.wait()
+
+            down = near_down[cols, :] if f * step < near else v_down[pl.ds(f * step - near, step), :]
+            back = dot_nt(held[at, :], down)
             g, u = both[0, at, cols], both[1, at, cols]
             sig = jax.nn.sigmoid(g)
             silu = g * sig
@@ -277,37 +267,46 @@
     w_gate, w_up, w_down = [hbm(w[0]) for w in (w_gate, w_up, w_down)]
     held = pltpu.VMEM((rows, width), BF)
     pair_of = shape((2, *w_gate.shape), BF)
-    (weights,) = call(
-        load_kernel, [w_gate, w_up], [pair_of], [ANY] * 2, [pltpu.SemaphoreType.DMA((2,))], grant, cost(2, 0)
-    )
-    x_column, weights = lax.optimization_barrier((column(tokens), vmem(weights)))
-    x_column, grad_out = lax.optimization_barrier((x_column, grad_out))
-    x_pieces = spread([x_column], bits)
-    dy_pieces = spread([column(grad_out)], bits[:-1])
+    def load(k, *args):
+        specs = [ANY, VMEM][: len(args)]
+        alias = {1: 0} if k else {}
+        sem = [pltpu.SemaphoreType.DMA]
+        (out,) = call(functools.partial(load_kernel, k), args, [pair_of], specs, sem, grant, cost(0, 0), alias)
+        return vmem(out)
+
+    x_column, weights = lax.optimization_barrier((column(tokens), load(0, w_gate)))
+    x_pieces = spread([x_column], bits[:-1])
+    x_pieces[-1], weights = lax.optimization_barrier((x_pieces[-1], load(1, w_up, weights)))
+    x_pieces = spread(x_pieces, bits[-1:])
+    dy_pieces = spread([column(grad_out)], [bit ^ bits[-1] for bit in bits[:-1]])
     n = len(x_pieces)
-    both, weights = call(
+    both, weights, near_down = call(
         functools.partial(gate_up_kernel, n),
-        x_pieces + [weights],
-        [shape((2, rows, ff), F32), pair_of],
-        [ANY] * n + [VMEM],
-        [held, pltpu.SemaphoreType.DMA((n,))],
+        x_pieces + [weights, w_down],
+        [shape((2, rows, ff), F32), pair_of, shape((ff // 2, width), BF)],
+        [ANY] * n + [VMEM, ANY],
+        [held, pltpu.SemaphoreType.DMA((n + 1,))],
         grant,
         cost(2, 2),
         {n: 1},
     )
-    both, weights = vmem(both), vmem(weights)
+    both, weights, near_down = vmem(both), vmem(weights), vmem(near_down)
     *late, both = lax.optimization_barrier((*dy_pieces[1:], both))
     dy_pieces = spread(dy_pieces[:1] + late, bits[-1:])
+    half = len(dy_pieces) // 2
+    turned = [bin(i).count("1") % 2 for i in range(half)]
+    order = [i + half * turned[i] for i in range(half)] + [i + half - half * turned[i] for i in range(half)]
+    dy_pieces = [dy_pieces[i] for i in order]
     keep, send, grads, score, weights = call(
         functools.partial(back_kernel, n),
-        dy_pieces + [weights, w_down, both],
+        dy_pieces + [weights, w_down, near_down, both],
         [shape((rows // 2, lead), BF)] * 2 + [shape((2, rows, ff), BF), shape((rows, 1), F32), pair_of],
-        [ANY] * n + [VMEM, ANY, VMEM],
+        [ANY] * n + [VMEM, ANY, VMEM, VMEM],
         [
             held,
-            pltpu.VMEM((ff, width), BF),
+            pltpu.VMEM((ff - ff // 2, width), BF),
+            pltpu.SemaphoreType.DMA,
             pltpu.SemaphoreType.DMA((n,)),
-            pltpu.SemaphoreType.DMA((len(pieces_of(ff)),)),
         ],
         grant,
         cost(3, 2),

time: 76.7 us -> 75.4 us (0.983)
  waiting for transfers between devices: 18.9 us -> 14.5 us
  starting transfers between devices: 25.4 us -> 29.2 us
    ppermute x10, waiting for transfers between devices: 12.6 us -> 10.4 us  [across(): return lax.ppermute(x, 'hidden', [(i, i ^ bit) for i in range(hidden)])]
    ppermute x12, waiting for transfers between devices: 6.31 us -> 4.17 us  [along(): return lax.ppermute(x, 'expert', [(i, i ^ shift) for i in range(experts)])]
    ppermute x10, starting transfers between devices: 5.64 us -> 7.77 us  [across(): return lax.ppermute(x, 'hidden', [(i, i ^ bit) for i in range(hidden)])]
    ppermute x12, starting transfers between devices: 19.8 us -> 21.4 us  [along(): return lax.ppermute(x, 'expert', [(i, i ^ shift) for i in range(experts)])]
    pallas_call x10 -> x11, Pallas kernels: 31.2 us -> 30.5 us  [call(): pl.pallas_call(kernel, out_shape=outs, in_specs=specs, out_specs=[VMEM] *...]
  transfers between devices with their start and end apart: 22 -> 22, of which waited for: 8 -> 7; matrix products, arithmetic and copies ran while one was open for 0% -> 0% of each run, Pallas kernels for 26% -> 28%
where the time goes in v4:
time: 75.4 us; the launch traced here: 75.2 us
  Pallas kernels  30.5 us (40%)
  starting transfers between devices  29.2 us (39%)
  waiting for transfers between devices  14.5 us (19%)
  between operations  0.84 us (1%)
    pallas_call x11, Pallas kernels, call(): pl.pallas_call(kernel, out_shape=outs, in_specs=specs, out_specs=[VMEM] *...  30.5 us
    ppermute x12, starting transfers between devices, along(): return lax.ppermute(x, 'expert', [(i, i ^ shift) for i in range(experts)])  21.4 us
    ppermute x10, waiting for transfers between devices, across(): return lax.ppermute(x, 'hidden', [(i, i ^ bit) for i in range(hidden)])  10.4 us
    ppermute x10, starting transfers between devices, across(): return lax.ppermute(x, 'hidden', [(i, i ^ bit) for i in range(hidden)])  7.77 us
    ppermute x12, waiting for transfers between devices, along(): return lax.ppermute(x, 'expert', [(i, i ^ shift) for i in range(experts)])  4.17 us
  transfers between devices with their start and end apart: 22, of which 7 were waited for; matrix products, arithmetic and copies ran while one was open for 0% of the time, Pallas kernels for 28%

profile of v4, /device:TPU:0, one launch (start us, length us, event | category | flops | bytes accessed | tf_op | source)
XLA Modules:
  0.0 75.2 jit_solution(8730546919304404295)
XLA Ops:
  0.6 3.1 %collective-permute-start.4 = (bf16[16,3072]{1,0:T(8,128)(2,1)}, bf16[16,3072]{1,0:T(8,128)(2,1)S(1)}, u32[]{:S(2)}, u32[]{:S(2)}) collective-permute-start(bf16[16,3072]{1,0:T(8,128)(2,1)} %tokens), channel_id=1, source_target_pairs={{0,4},{4,0},{8,12},{12,8},{1,5},{5,1},{9,13},{13,9},{2,6},{6,2},{1... | collective-permute-start | bytes 294920 | tf_op jit(solution)/shard_map/ppermute | solution.py:235
  3.7 2.6 %collective-permute-start.5 = (bf16[16,3072]{1,0:T(8,128)(2,1)}, bf16[16,3072]{1,0:T(8,128)(2,1)S(1)}, u32[]{:S(2)}, u32[]{:S(2)}) collective-permute-start(bf16[16,3072]{1,0:T(8,128)(2,1)} %tokens), channel_id=1, source_target_pairs={{0,8},{4,12},{8,0},{12,4},{1,9},{5,13},{9,1},{13,5},{2,10},{6,14},... | collective-permute-start | bytes 294920 | tf_op jit(solution)/shard_map/ppermute | solution.py:235
  6.3 0.0 collective-permute-start.6
  6.3 0.9 %collective-permute-start = (bf16[16,3072]{1,0:T(8,128)(2,1)}, bf16[16,3072]{1,0:T(8,128)(2,1)S(1)}, u32[]{:S(2)}, u32[]{:S(2)}) collective-permute-start(bf16[16,3072]{1,0:T(8,128)(2,1)} %param.8), channel_id=1, source_target_pairs={{0,4},{4,0},{8,12},{12,8},{1,5},{5,1},{9,13},{13,9},{2,6},{6,2},{1... | collective-permute-start | bytes 294920 | tf_op jit(solution)/shard_map/ppermute | solution.py:235
  7.2 3.5 %collective-permute-start.1 = (bf16[16,3072]{1,0:T(8,128)(2,1)}, bf16[16,3072]{1,0:T(8,128)(2,1)S(1)}, u32[]{:S(2)}, u32[]{:S(2)}) collective-permute-start(bf16[16,3072]{1,0:T(8,128)(2,1)} %param.8), channel_id=1, source_target_pairs={{0,8},{4,12},{8,0},{12,4},{1,9},{5,13},{9,1},{13,5},{2,10},{6,14},... | collective-permute-start | bytes 294920 | tf_op jit(solution)/shard_map/ppermute | solution.py:235
  10.7 0.0 copy-start.2
  10.7 0.0 copy-start
  10.7 4.6 %shard_map.86.refs_0_ = bf16[2,3072,2048]{2,1,0:T(8,128)(2,1)S(1)} custom-call(bf16[3072,2048]{1,0:T(8,128)(2,1)} %bitcast.9), custom_call_target="tpu_custom_call" | custom-call | tf_op jit(solution)/shard_map/pallas_call | solution.py:212
  15.3 0.0 collective-permute-done.4
  15.3 0.0 copy-done.2
  15.4 0.1 collective-permute-start.2
  15.4 0.0 collective-permute-done.5
  15.4 0.0 collective-permute-done.6
  15.5 0.0 copy-done
  15.5 1.8 %collective-permute-start.7 = (bf16[64,3072]{1,0:T(8,128)(2,1)S(1)}, bf16[64,3072]{1,0:T(8,128)(2,1)S(1)}, u32[]{:S(2)}, u32[]{:S(2)}) collective-permute-start(bf16[64,3072]{1,0:T(8,128)(2,1)S(1)} %pad_maximum_fusion.refs_0_), channel_id=1, source_target_pairs={{0,2},{1,3},{2,0},{3,1},{4,6},{5,7},{6,4},{7,5},{8,10},{9,11},{10,... | collective-permute-start | bytes 1179656 | tf_op jit(solution)/shard_map/ppermute | solution.py:238
  17.3 0.1 collective-permute-start.8
  17.4 0.0 collective-permute-done
  17.4 4.6 %shard_map.87.refs_4_ = bf16[2,3072,2048]{2,1,0:T(8,128)(2,1)S(1)} custom-call(bf16[3072,2048]{1,0:T(8,128)(2,1)} %bitcast.10, bf16[2,3072,2048]{2,1,0:T(8,128)(2,1)S(1)} %shard_map.86.refs_0_), custom_call_target="tpu_custom_call", output_to_operand_aliasing={{}: (1, {})} | custom-call | tf_op jit(solution)/shard_map/pallas_call | solution.py:212
  22.0 3.0 %collective-permute-done.7.refs_1_ = bf16[64,3072]{1,0:T(8,128)(2,1)S(1)} collective-permute-done((bf16[64,3072]{1,0:T(8,128)(2,1)S(1)}, bf16[64,3072]{1,0:T(8,128)(2,1)S(1)}, u32[]{:S(2)}, u32[]{:S(2)}) %collective-permute-start.7) | collective-permute-done | bytes 393248 | tf_op jit(solution)/shard_map/ppermute | solution.py:238
  25.0 0.0 collective-permute-start.9
  25.0 0.0 collective-permute-done.1
  25.0 0.0 collective-permute-done.2
  25.1 1.7 %collective-permute-start.3 = (bf16[64,3072]{1,0:T(8,128)(2,1)S(1)}, bf16[64,3072]{1,0:T(8,128)(2,1)S(1)}, u32[]{:S(2)}, u32[]{:S(2)}) collective-permute-start(bf16[64,3072]{1,0:T(8,128)(2,1)S(1)} %constant_dynamic-update-slice_fusion.refs_0_), channel_id=1, source_target_pairs={{0,3},{1,2},{2,1},{3,0},{4,7},{5,6},{6,5},{7,4},{8,11},{9,10},{10,... | collective-permute-start | bytes 1179656 | tf_op jit(solution)/shard_map/ppermute | solution.py:238
  26.8 0.0 collective-permute-start.11
  26.8 0.0 collective-permute-done.8.refs_2_
  26.8 0.0 collective-permute-done.9.refs_3_
  26.8 7.6 %shard_map.88 = (f32[2,256,2048]{2,1,0:T(8,128)S(1)}, bf16[2,3072,2048]{2,1,0:T(8,128)(2,1)S(1)}, bf16[1024,3072]{1,0:T(8,128)(2,1)S(1)}) custom-call(bf16[64,3072]{1,0:T(8,128)(2,1)S(1)} %pad_maximum_fusion.refs_0_, bf16[64,3072]{1,0:T(8,128)(2,1)S(1)} %collective-permute-done.7.refs_1_, ...), custom_call_target="tpu_custom_call", output_to_operand_aliasing={{1}: (4, {})} | custom-call | flops 6442450944 | bytes 25165824 | tf_op jit(solution)/shard_map/pallas_call | solution.py:212
  34.4 1.5 %collective-permute-done.3.refs_3_ = bf16[64,3072]{1,0:T(8,128)(2,1)S(1)} collective-permute-done((bf16[64,3072]{1,0:T(8,128)(2,1)S(1)}, bf16[64,3072]{1,0:T(8,128)(2,1)S(1)}, u32[]{:S(2)}, u32[]{:S(2)}) %collective-permute-start.3) | collective-permute-done | bytes 393248 | tf_op jit(solution)/shard_map/ppermute | solution.py:238
  35.9 0.5 collective-permute-start.10
  36.4 0.0 collective-permute-done.11.refs_2_
  36.4 1.3 %collective-permute-done.10.refs_1_ = bf16[64,3072]{1,0:T(8,128)(2,1)S(1)} collective-permute-done((bf16[64,3072]{1,0:T(8,128)(2,1)S(1)}, bf16[64,3072]{1,0:T(8,128)(2,1)S(1)}, u32[]{:S(2)}, u32[]{:S(2)}) %collective-permute-start.10) | collective-permute-done | bytes 393248 | tf_op jit(solution)/shard_map/ppermute | solution.py:238
  37.7 8.5 %shard_map.89 = (bf16[128,1536]{1,0:T(8,128)(2,1)S(1)}, bf16[128,1536]{1,0:T(8,128)(2,1)S(1)}, bf16[2,256,2048]{2,1,0:T(8,128)(2,1)S(1)}, f32[256,1]{1,0:T(8,128)S(1)}, bf16[2,3072,2048]{2,1,0:T(8,128)(2,1)S(1)}) custom-call(bf16[64,3072]{1,0:T(8,128)(2,1)S(1)} %constant_dynamic-update-slice_fusion.refs_0_, ...), custom_call_target="tpu_custom_call", output_to_operand_aliasing={{4}: (4, {})} | custom-call | flops 6442450944 | bytes 37748736 | tf_op jit(solution)/shard_map/pallas_call | solution.py:212
  46.2 0.4 collective-permute-start.12
  46.7 0.0 copy-start.1
  46.7 0.0 copy-start.3
  46.7 3.4 %shard_map.92 = (bf16[128,1664]{1,0:T(8,128)(2,1)S(1)}, bf16[128,1664]{1,0:T(8,128)(2,1)S(1)}) custom-call(bf16[2,3072,2048]{2,1,0:T(8,128)(2,1)S(1)} %get-tuple-element.56.weights, bf16[2,256,2048]{2,1,0:T(8,128)(2,1)S(1)} %get-tuple-element.57.grads, f32[256,1]{1,0:T(8,128)S(1)} %get-tuple-element.58.score), custom_call_target="tpu_custom_call" | custom-call | flops 3221225472 | bytes 12582912 | tf_op jit(solution)/shard_map/pallas_call | solution.py:212
  50.1 0.2 collective-permute-start.17
  50.3 0.0 collective-permute-done.12.theirs
  50.3 0.1 shard_map.90
  50.4 1.6 %collective-permute-start.13 = (bf16[64,1536]{1,0:T(8,128)(2,1)S(1)}, bf16[64,1536]{1,0:T(8,128)(2,1)S(1)}, u32[]{:S(2)}, u32[]{:S(2)}) collective-permute-start(bf16[64,1536]{1,0:T(8,128)(2,1)S(1)} %get-tuple-element.51), channel_id=1, source_target_pairs={{0,2},{1,3},{2,0},{3,1},{4,6},{5,7},{6,4},{7,5},{8,10},{9,11},{10,... | collective-permute-start | bytes 589832 | tf_op jit(solution)/shard_map/ppermute | solution.py:238
  52.0 0.0 collective-permute-done.17.theirs
  52.0 0.2 shard_map.93
  52.2 1.5 %collective-permute-start.18 = (bf16[64,1664]{1,0:T(8,128)(2,1)S(1)}, bf16[64,1664]{1,0:T(8,128)(2,1)S(1)}, u32[]{:S(2)}, u32[]{:S(2)}) collective-permute-start(bf16[64,1664]{1,0:T(8,128)(2,1)S(1)} %get-tuple-element.63), channel_id=1, source_target_pairs={{0,2},{1,3},{2,0},{3,1},{4,6},{5,7},{6,4},{7,5},{8,10},{9,11},{10,... | collective-permute-start | bytes 638984 | tf_op jit(solution)/shard_map/ppermute | solution.py:238
  53.7 4.5 %collective-permute-done.13.theirs = bf16[64,1536]{1,0:T(8,128)(2,1)S(1)} collective-permute-done((bf16[64,1536]{1,0:T(8,128)(2,1)S(1)}, bf16[64,1536]{1,0:T(8,128)(2,1)S(1)}, u32[]{:S(2)}, u32[]{:S(2)}) %collective-permute-start.13) | collective-permute-done | bytes 196640 | tf_op jit(solution)/shard_map/ppermute | solution.py:238
  58.3 3.5 %collective-permute-start.14 = (bf16[16,1536]{1,0:T(8,128)(2,1)S(1)}, bf16[16,1536]{1,0:T(8,128)(2,1)S(1)}, u32[]{:S(2)}, u32[]{:S(2)}) collective-permute-start(bf16[16,1536]{1,0:T(8,128)(2,1)S(1)} %get-tuple-element.53), channel_id=1, source_target_pairs={{0,4},{4,0},{8,12},{12,8},{1,5},{5,1},{9,13},{13,9},{2,6},{6,2},{1... | collective-permute-start | bytes 147464 | tf_op jit(solution)/shard_map/ppermute | solution.py:235
  61.7 0.0 copy-done.1
  61.8 0.0 copy-done.3
  61.8 0.1 copy.16.routes
  61.8 1.8 %collective-permute-start.15 = (bf16[16,1536]{1,0:T(8,128)(2,1)S(1)}, bf16[16,1536]{1,0:T(8,128)(2,1)S(1)}, u32[]{:S(2)}, u32[]{:S(2)}) collective-permute-start(bf16[16,1536]{1,0:T(8,128)(2,1)S(1)} %get-tuple-element.54), channel_id=1, source_target_pairs={{0,8},{4,12},{8,0},{12,4},{1,9},{5,13},{9,1},{13,5},{2,10},{6,14},... | collective-permute-start | bytes 147464 | tf_op jit(solution)/shard_map/ppermute | solution.py:235
  63.7 1.5 %collective-permute-start.16 = (bf16[16,1536]{1,0:T(8,128)(2,1)S(1)}, bf16[16,1536]{1,0:T(8,128)(2,1)S(1)}, u32[]{:S(2)}, u32[]{:S(2)}) collective-permute-start(bf16[16,1536]{1,0:T(8,128)(2,1)S(1)} %get-tuple-element.55), channel_id=1, source_target_pairs={{0,12},{4,8},{8,4},{12,0},{1,13},{5,9},{9,5},{13,1},{2,14},{6,10},... | collective-permute-start | bytes 147464 | tf_op jit(solution)/shard_map/ppermute | solution.py:235
  65.2 0.0 collective-permute-done.18.theirs
  65.2 0.1 shard_map.94
  65.3 0.6 collective-permute-start.19
  65.9 2.4 %collective-permute-start.20 = (bf16[16,1664]{1,0:T(8,128)(2,1)S(1)}, bf16[16,1664]{1,0:T(8,128)(2,1)S(1)}, u32[]{:S(2)}, u32[]{:S(2)}) collective-permute-start(bf16[16,1664]{1,0:T(8,128)(2,1)S(1)} %get-tuple-element.66), channel_id=1, source_target_pairs={{0,8},{4,12},{8,0},{12,4},{1,9},{5,13},{9,1},{13,5},{2,10},{6,14},... | collective-permute-start | bytes 159752 | tf_op jit(solution)/shard_map/ppermute | solution.py:235
  68.2 0.0 collective-permute-done.14.refs_1_
  68.2 1.5 %collective-permute-start.21 = (bf16[16,1664]{1,0:T(8,128)(2,1)S(1)}, bf16[16,1664]{1,0:T(8,128)(2,1)S(1)}, u32[]{:S(2)}, u32[]{:S(2)}) collective-permute-start(bf16[16,1664]{1,0:T(8,128)(2,1)S(1)} %get-tuple-element.67), channel_id=1, source_target_pairs={{0,12},{4,8},{8,4},{12,0},{1,13},{5,9},{9,5},{13,1},{2,14},{6,10},... | collective-permute-start | bytes 159752 | tf_op jit(solution)/shard_map/ppermute | solution.py:235
  69.8 0.2 shard_map.95
  70.0 0.0 collective-permute-done.15.refs_2_
  70.0 0.0 collective-permute-done.16.refs_3_
  70.0 0.3 collective-permute-done.19.refs_5_
  70.4 2.6 %collective-permute-done.20.refs_6_ = bf16[16,1664]{1,0:T(8,128)(2,1)S(1)} collective-permute-done((bf16[16,1664]{1,0:T(8,128)(2,1)S(1)}, bf16[16,1664]{1,0:T(8,128)(2,1)S(1)}, u32[]{:S(2)}, u32[]{:S(2)}) %collective-permute-start.20) | collective-permute-done | bytes 53280 | tf_op jit(solution)/shard_map/ppermute | solution.py:235
  73.0 1.2 %collective-permute-done.21.refs_7_ = bf16[16,1664]{1,0:T(8,128)(2,1)S(1)} collective-permute-done((bf16[16,1664]{1,0:T(8,128)(2,1)S(1)}, bf16[16,1664]{1,0:T(8,128)(2,1)S(1)}, u32[]{:S(2)}, u32[]{:S(2)}) %collective-permute-start.21) | collective-permute-done | bytes 53280 | tf_op jit(solution)/shard_map/ppermute | solution.py:235
  74.2 1.1 %shard_map.96 = (bf16[16,3072]{1,0:T(8,128)(2,1)}, f32[2,16]{1,0:T(2,128)}) custom-call(bf16[16,1536]{1,0:T(8,128)(2,1)S(1)} %get-tuple-element.52.refs_0_, bf16[16,1536]{1,0:T(8,128)(2,1)S(1)} %collective-permute-done.14.refs_1_, bf16[16,1536]{1,0:T(8,128)(2,1)S(1)} %collective-permute-done.15.refs_2_, ...), custom_call_target="tpu_custom_call" | custom-call | tf_op jit(solution)/shard_map/pallas_call | solution.py:212
  (8 shorter events, 0.1 us)
Async XLA Ops:
  0.6 14.7 %collective-permute-start.4 = (bf16[16,3072]{1,0:T(8,128)(2,1)}, bf16[16,3072]{1,0:T(8,128)(2,1)S(1)}, u32[]{:S(2)}, u32[]{:S(2)}) collective-permute-start(bf16[16,3072]{1,0:T(8,128)(2,1)} %tokens), channel_id=1, source_target_pairs={{0,4},{4,0},{8,12},{12,8},{1,5},{5,1},{9,13},{13,9},{2,6},{6,2},{1... | collective-permute-start | bytes 294920 | tf_op jit(solution)/shard_map/ppermute | solution.py:235
  3.7 11.7 %collective-permute-start.5 = (bf16[16,3072]{1,0:T(8,128)(2,1)}, bf16[16,3072]{1,0:T(8,128)(2,1)S(1)}, u32[]{:S(2)}, u32[]{:S(2)}) collective-permute-start(bf16[16,3072]{1,0:T(8,128)(2,1)} %tokens), channel_id=1, source_target_pairs={{0,8},{4,12},{8,0},{12,4},{1,9},{5,13},{9,1},{13,5},{2,10},{6,14},... | collective-permute-start | bytes 294920 | tf_op jit(solution)/shard_map/ppermute | solution.py:235
  6.3 9.1 %collective-permute-start.6 = (bf16[16,3072]{1,0:T(8,128)(2,1)}, bf16[16,3072]{1,0:T(8,128)(2,1)S(1)}, u32[]{:S(2)}, u32[]{:S(2)}) collective-permute-start(bf16[16,3072]{1,0:T(8,128)(2,1)} %tokens), channel_id=1, source_target_pairs={{0,12},{4,8},{8,4},{12,0},{1,13},{5,9},{9,5},{13,1},{2,14},{6,10},... | collective-permute-start | bytes 294920 | tf_op jit(solution)/shard_map/ppermute | solution.py:235
  6.3 11.0 %collective-permute-start = (bf16[16,3072]{1,0:T(8,128)(2,1)}, bf16[16,3072]{1,0:T(8,128)(2,1)S(1)}, u32[]{:S(2)}, u32[]{:S(2)}) collective-permute-start(bf16[16,3072]{1,0:T(8,128)(2,1)} %param.8), channel_id=1, source_target_pairs={{0,4},{4,0},{8,12},{12,8},{1,5},{5,1},{9,13},{13,9},{2,6},{6,2},{1... | collective-permute-start | bytes 294920 | tf_op jit(solution)/shard_map/ppermute | solution.py:235
  7.2 17.8 %collective-permute-start.1 = (bf16[16,3072]{1,0:T(8,128)(2,1)}, bf16[16,3072]{1,0:T(8,128)(2,1)S(1)}, u32[]{:S(2)}, u32[]{:S(2)}) collective-permute-start(bf16[16,3072]{1,0:T(8,128)(2,1)} %param.8), channel_id=1, source_target_pairs={{0,8},{4,12},{8,0},{12,4},{1,9},{5,13},{9,1},{13,5},{2,10},{6,14},... | collective-permute-start | bytes 294920 | tf_op jit(solution)/shard_map/ppermute | solution.py:235
  10.7 4.6 %copy-start.2 = (bf16[16,3072]{1,0:T(8,128)(2,1)S(1)}, bf16[16,3072]{1,0:T(8,128)(2,1)}, u32[]{:S(2)}) copy-start(bf16[16,3072]{1,0:T(8,128)(2,1)} %param.8) | copy-start | bytes 294916
  10.7 4.8 %copy-start = (bf16[16,3072]{1,0:T(8,128)(2,1)S(1)}, bf16[16,3072]{1,0:T(8,128)(2,1)}, u32[]{:S(2)}) copy-start(bf16[16,3072]{1,0:T(8,128)(2,1)} %tokens) | copy-start | bytes 294916
  15.4 9.7 %collective-permute-start.2 = (bf16[16,3072]{1,0:T(8,128)(2,1)S(1)}, bf16[16,3072]{1,0:T(8,128)(2,1)S(1)}, u32[]{:S(2)}, u32[]{:S(2)}) collective-permute-start(bf16[16,3072]{1,0:T(8,128)(2,1)S(1)} %copy-done.2), channel_id=1, source_target_pairs={{0,12},{4,8},{8,4},{12,0},{1,13},{5,9},{9,5},{13,1},{2,14},{6,10},... | collective-permute-start | bytes 294920 | tf_op jit(solution)/shard_map/ppermute | solution.py:235
  15.5 9.5 %collective-permute-start.7 = (bf16[64,3072]{1,0:T(8,128)(2,1)S(1)}, bf16[64,3072]{1,0:T(8,128)(2,1)S(1)}, u32[]{:S(2)}, u32[]{:S(2)}) collective-permute-start(bf16[64,3072]{1,0:T(8,128)(2,1)S(1)} %pad_maximum_fusion.refs_0_), channel_id=1, source_target_pairs={{0,2},{1,3},{2,0},{3,1},{4,6},{5,7},{6,4},{7,5},{8,10},{9,11},{10,... | collective-permute-start | bytes 1179656 | tf_op jit(solution)/shard_map/ppermute | solution.py:238
  17.3 9.5 %collective-permute-start.8 = (bf16[64,3072]{1,0:T(8,128)(2,1)S(1)}, bf16[64,3072]{1,0:T(8,128)(2,1)S(1)}, u32[]{:S(2)}, u32[]{:S(2)}) collective-permute-start(bf16[64,3072]{1,0:T(8,128)(2,1)S(1)} %pad_maximum_fusion.refs_0_), channel_id=1, source_target_pairs={{0,1},{1,0},{2,3},{3,2},{4,5},{5,4},{6,7},{7,6},{8,9},{9,8},{10,11... | collective-permute-start | bytes 1179656 | tf_op jit(solution)/shard_map/ppermute | solution.py:238
  25.0 1.8 %collective-permute-start.9 = (bf16[64,3072]{1,0:T(8,128)(2,1)S(1)}, bf16[64,3072]{1,0:T(8,128)(2,1)S(1)}, u32[]{:S(2)}, u32[]{:S(2)}) collective-permute-start(bf16[64,3072]{1,0:T(8,128)(2,1)S(1)} %collective-permute-done.7.refs_1_), channel_id=1, source_target_pairs={{0,1},{1,0},{2,3},{3,2},{4,5},{5,4},{6,7},{7,6},{8,9},{9,8},{10,11... | collective-permute-start | bytes 1179656 | tf_op jit(solution)/shard_map/ppermute | solution.py:238
  25.1 10.8 %collective-permute-start.3 = (bf16[64,3072]{1,0:T(8,128)(2,1)S(1)}, bf16[64,3072]{1,0:T(8,128)(2,1)S(1)}, u32[]{:S(2)}, u32[]{:S(2)}) collective-permute-start(bf16[64,3072]{1,0:T(8,128)(2,1)S(1)} %constant_dynamic-update-slice_fusion.refs_0_), channel_id=1, source_target_pairs={{0,3},{1,2},{2,1},{3,0},{4,7},{5,6},{6,5},{7,4},{8,11},{9,10},{10,... | collective-permute-start | bytes 1179656 | tf_op jit(solution)/shard_map/ppermute | solution.py:238
  26.8 9.6 %collective-permute-start.11 = (bf16[64,3072]{1,0:T(8,128)(2,1)S(1)}, bf16[64,3072]{1,0:T(8,128)(2,1)S(1)}, u32[]{:S(2)}, u32[]{:S(2)}) collective-permute-start(bf16[64,3072]{1,0:T(8,128)(2,1)S(1)} %constant_dynamic-update-slice_fusion.refs_0_), channel_id=1, source_target_pairs={{0,1},{1,0},{2,3},{3,2},{4,5},{5,4},{6,7},{7,6},{8,9},{9,8},{10,11... | collective-permute-start | bytes 1179656 | tf_op jit(solution)/shard_map/ppermute | solution.py:238
  35.9 1.8 %collective-permute-start.10 = (bf16[64,3072]{1,0:T(8,128)(2,1)S(1)}, bf16[64,3072]{1,0:T(8,128)(2,1)S(1)}, u32[]{:S(2)}, u32[]{:S(2)}) collective-permute-start(bf16[64,3072]{1,0:T(8,128)(2,1)S(1)} %collective-permute-done.3.refs_3_), channel_id=1, source_target_pairs={{0,1},{1,0},{2,3},{3,2},{4,5},{5,4},{6,7},{7,6},{8,9},{9,8},{10,11... | collective-permute-start | bytes 1179656 | tf_op jit(solution)/shard_map/ppermute | solution.py:238
  46.2 4.1 %collective-permute-start.12 = (bf16[128,1536]{1,0:T(8,128)(2,1)S(1)}, bf16[128,1536]{1,0:T(8,128)(2,1)S(1)}, u32[]{:S(2)}, u32[]{:S(2)}) collective-permute-start(bf16[128,1536]{1,0:T(8,128)(2,1)S(1)} %get-tuple-element.49), channel_id=1, source_target_pairs={{0,1},{1,0},{2,3},{3,2},{4,5},{5,4},{6,7},{7,6},{8,9},{9,8},{10,11... | collective-permute-start | bytes 1179656 | tf_op jit(solution)/shard_map/ppermute | solution.py:238
  46.7 15.1 %copy-start.1 = (bf16[3072,4]{0,1:T(4,128)(2,1)S(1)}, bf16[3072,4]{0,1:T(4,128)(2,1)}, u32[]{:S(2)}) copy-start(bf16[3072,4]{0,1:T(4,128)(2,1)} %param.10) | copy-start | bytes 73732
  46.7 15.1 %copy-start.3 = (s32[16,2]{0,1:T(2,128)S(1)}, s32[16,2]{0,1:T(2,128)}, u32[]{:S(2)}) copy-start(s32[16,2]{0,1:T(2,128)} %param.9) | copy-start | bytes 388
  50.1 1.9 %collective-permute-start.17 = (bf16[128,1664]{1,0:T(8,128)(2,1)S(1)}, bf16[128,1664]{1,0:T(8,128)(2,1)S(1)}, u32[]{:S(2)}, u32[]{:S(2)}) collective-permute-start(bf16[128,1664]{1,0:T(8,128)(2,1)S(1)} %get-tuple-element.61), channel_id=1, source_target_pairs={{0,1},{1,0},{2,3},{3,2},{4,5},{5,4},{6,7},{7,6},{8,9},{9,8},{10,11... | collective-permute-start | bytes 1277960 | tf_op jit(solution)/shard_map/ppermute | solution.py:238
  50.4 7.8 %collective-permute-start.13 = (bf16[64,1536]{1,0:T(8,128)(2,1)S(1)}, bf16[64,1536]{1,0:T(8,128)(2,1)S(1)}, u32[]{:S(2)}, u32[]{:S(2)}) collective-permute-start(bf16[64,1536]{1,0:T(8,128)(2,1)S(1)} %get-tuple-element.51), channel_id=1, source_target_pairs={{0,2},{1,3},{2,0},{3,1},{4,6},{5,7},{6,4},{7,5},{8,10},{9,11},{10,... | collective-permute-start | bytes 589832 | tf_op jit(solution)/shard_map/ppermute | solution.py:238
  52.2 13.0 %collective-permute-start.18 = (bf16[64,1664]{1,0:T(8,128)(2,1)S(1)}, bf16[64,1664]{1,0:T(8,128)(2,1)S(1)}, u32[]{:S(2)}, u32[]{:S(2)}) collective-permute-start(bf16[64,1664]{1,0:T(8,128)(2,1)S(1)} %get-tuple-element.63), channel_id=1, source_target_pairs={{0,2},{1,3},{2,0},{3,1},{4,6},{5,7},{6,4},{7,5},{8,10},{9,11},{10,... | collective-permute-start | bytes 638984 | tf_op jit(solution)/shard_map/ppermute | solution.py:238
  58.3 10.0 %collective-permute-start.14 = (bf16[16,1536]{1,0:T(8,128)(2,1)S(1)}, bf16[16,1536]{1,0:T(8,128)(2,1)S(1)}, u32[]{:S(2)}, u32[]{:S(2)}) collective-permute-start(bf16[16,1536]{1,0:T(8,128)(2,1)S(1)} %get-tuple-element.53), channel_id=1, source_target_pairs={{0,4},{4,0},{8,12},{12,8},{1,5},{5,1},{9,13},{13,9},{2,6},{6,2},{1... | collective-permute-start | bytes 147464 | tf_op jit(solution)/shard_map/ppermute | solution.py:235
  61.8 8.2 %collective-permute-start.15 = (bf16[16,1536]{1,0:T(8,128)(2,1)S(1)}, bf16[16,1536]{1,0:T(8,128)(2,1)S(1)}, u32[]{:S(2)}, u32[]{:S(2)}) collective-permute-start(bf16[16,1536]{1,0:T(8,128)(2,1)S(1)} %get-tuple-element.54), channel_id=1, source_target_pairs={{0,8},{4,12},{8,0},{12,4},{1,9},{5,13},{9,1},{13,5},{2,10},{6,14},... | collective-permute-start | bytes 147464 | tf_op jit(solution)/shard_map/ppermute | solution.py:235
  63.7 6.3 %collective-permute-start.16 = (bf16[16,1536]{1,0:T(8,128)(2,1)S(1)}, bf16[16,1536]{1,0:T(8,128)(2,1)S(1)}, u32[]{:S(2)}, u32[]{:S(2)}) collective-permute-start(bf16[16,1536]{1,0:T(8,128)(2,1)S(1)} %get-tuple-element.55), channel_id=1, source_target_pairs={{0,12},{4,8},{8,4},{12,0},{1,13},{5,9},{9,5},{13,1},{2,14},{6,10},... | collective-permute-start | bytes 147464 | tf_op jit(solution)/shard_map/ppermute | solution.py:235
  65.3 5.1 %collective-permute-start.19 = (bf16[16,1664]{1,0:T(8,128)(2,1)S(1)}, bf16[16,1664]{1,0:T(8,128)(2,1)S(1)}, u32[]{:S(2)}, u32[]{:S(2)}) collective-permute-start(bf16[16,1664]{1,0:T(8,128)(2,1)S(1)} %get-tuple-element.65), channel_id=1, source_target_pairs={{0,4},{4,0},{8,12},{12,8},{1,5},{5,1},{9,13},{13,9},{2,6},{6,2},{1... | collective-permute-start | bytes 159752 | tf_op jit(solution)/shard_map/ppermute | solution.py:235
  65.9 7.1 %collective-permute-start.20 = (bf16[16,1664]{1,0:T(8,128)(2,1)S(1)}, bf16[16,1664]{1,0:T(8,128)(2,1)S(1)}, u32[]{:S(2)}, u32[]{:S(2)}) collective-permute-start(bf16[16,1664]{1,0:T(8,128)(2,1)S(1)} %get-tuple-element.66), channel_id=1, source_target_pairs={{0,8},{4,12},{8,0},{12,4},{1,9},{5,13},{9,1},{13,5},{2,10},{6,14},... | collective-permute-start | bytes 159752 | tf_op jit(solution)/shard_map/ppermute | solution.py:235
  68.2 5.9 %collective-permute-start.21 = (bf16[16,1664]{1,0:T(8,128)(2,1)S(1)}, bf16[16,1664]{1,0:T(8,128)(2,1)S(1)}, u32[]{:S(2)}, u32[]{:S(2)}) collective-permute-start(bf16[16,1664]{1,0:T(8,128)(2,1)S(1)} %get-tuple-element.67), channel_id=1, source_target_pairs={{0,12},{4,8},{8,4},{12,0},{1,13},{5,9},{9,5},{13,1},{2,14},{6,10},... | collective-permute-start | bytes 159752 | tf_op jit(solution)/shard_map/ppermute | solution.py:235

commit v5 on v4

--- a/solution.py
+++ b/solution.py
@@ -86,7 +86,7 @@
     half = rows // 2
     if rows == block:
         keep[:, cols] = value[:half]
-        send[:, cols] = value[half:]
+        send[:, cols] = value[half:].astype(BF)
     else:
 
         @pl.when(r < half // block)
@@ -95,7 +95,7 @@
 
         @pl.when(r >= half // block)
         def _():
-            send[pl.ds(pl.multiple_of(r * block - half, block), block), cols] = value
+            send[pl.ds(pl.multiple_of(r * block - half, block), block), cols] = value.astype(BF)
 
 
 def sum_columns(start, width, r, block, grads, weights, keep, send):
@@ -109,7 +109,7 @@
         cols = pl.ds(pl.multiple_of(d * step, step), step)
         value = dot_nt(grads[0, at, :], weights[0, source, :])
         value = value + dot_nt(grads[1, at, :], weights[1, source, :])
-        store_halves(r, block, rows, cols, value.astype(BF), keep, send)
+        store_halves(r, block, rows, cols, value, keep, send)
 
 
 def back_kernel(n, *refs):
@@ -157,7 +157,7 @@
     def _(r):
         sum_columns(start, width, r, block, grads, weights, keep, send)
 
-    keep[:, pl.ds(width, LANES)] = split3(score[pl.ds(0, half), :])
+    keep[:, pl.ds(width, LANES)] = split3(score[pl.ds(0, half), :]).astype(F32)
     send[:, pl.ds(width, LANES)] = split3(score[pl.ds(half, half), :])
 
 
@@ -167,11 +167,11 @@
     for out in outs:
         rows = out.shape[0]
         here = pl.ds(at, rows)
-        total = mine[here, pl.ds(0, width)].astype(F32) + theirs[here, pl.ds(0, width)].astype(F32)
-        out[:, pl.ds(0, width)] = total.astype(BF)
+        total = mine[here, pl.ds(0, width)] + theirs[here, pl.ds(0, width)].astype(F32)
+        out[:, pl.ds(0, width)] = total.astype(out.dtype)
         if tail:
             last = pl.ds(width, LANES)
-            out[:, last] = split3(join3(mine[here, last]) + join3(theirs[here, last]))
+            out[:, last] = split3(join3(mine[here, last]) + join3(theirs[here, last])).astype(out.dtype)
         at += rows
 
 
@@ -241,8 +241,8 @@
     macs = rows * width * ff
     lead = width // 2
     rest = width - lead + LANES
-    resident_bytes = rows * (2 * width + 8 * LANES) + rows * (ff * 4 + lead * 2 + rest * 2)
-    grant = GRANT if rows <= ROWS else resident_bytes + (14 << 20)
+    resident_bytes = rows * (2 * width + 8 * LANES) + rows * (ff * 4 + lead * 3 + rest * 3)
+    grant = GRANT if rows <= ROWS else resident_bytes + (8 << 20)
     small = min(rows, 2048) * (width + LANES) * 4 + (1 << 20)
 
     def cost(weights, matmuls):
@@ -300,7 +300,8 @@
     keep, send, grads, score, weights = call(
         functools.partial(back_kernel, n),
         dy_pieces + [weights, w_down, near_down, both],
-        [shape((rows // 2, lead), BF)] * 2 + [shape((2, rows, ff), BF), shape((rows, 1), F32), pair_of],
+        [shape((rows // 2, lead), F32), shape((rows // 2, lead), BF)]
+        + [shape((2, rows, ff), BF), shape((rows, 1), F32), pair_of],
         [ANY] * n + [VMEM, ANY, VMEM, VMEM],
         [
             held,
@@ -315,7 +316,7 @@
     keep_rest, send_rest = call(
         functools.partial(rest_kernel, lead),
         [vmem(weights), vmem(grads), score],
-        [shape((rows // 2, rest), BF)] * 2,
+        [shape((rows // 2, rest), F32), shape((rows // 2, rest), BF)],
         [VMEM] * 3,
         limit=grant,
         cost=cost(1, 1),
@@ -335,10 +336,10 @@
         total = keep.shape[1]
         for bit in bits[:0:-1]:
             arrived = across(send, bit)
-            outs = [shape((keep.shape[0] // 2, total), BF)] * 2
+            outs = [shape((keep.shape[0] // 2, total), kind) for kind in (F32, BF)]
             keep, send = call(add, [keep, arrived], outs, [VMEM] * 2, limit=small)
         arrived = across(send, bits[0])
-        outs = [shape((own, total), BF)] * experts
+        outs = [shape((own, total), F32)] + [shape((own, total), BF)] * (experts - 1)
         blocks = call(add, [keep, arrived], outs, [VMEM] * 2, limit=small)
         return [blocks[0]] + [along(blocks[s], s) for s in range(1, experts)]
 

time: 75.4 us -> 75.4 us (level)
  no operation moved by 1% of the time
where the time goes in v5:
time: 75.4 us; the launch traced here: 75.2 us
  Pallas kernels  30.4 us (40%)
  starting transfers between devices  29.2 us (39%)
  waiting for transfers between devices  14.6 us (19%)
  between operations  0.85 us (1%)
    pallas_call x11, Pallas kernels, call(): pl.pallas_call(kernel, out_shape=outs, in_specs=specs, out_specs=[VMEM] *...  30.4 us
    ppermute x12, starting transfers between devices, along(): return lax.ppermute(x, 'expert', [(i, i ^ shift) for i in range(experts)])  21.4 us
    ppermute x10, waiting for transfers between devices, across(): return lax.ppermute(x, 'hidden', [(i, i ^ bit) for i in range(hidden)])  10.4 us
    ppermute x10, starting transfers between devices, across(): return lax.ppermute(x, 'hidden', [(i, i ^ bit) for i in range(hidden)])  7.79 us
    ppermute x12, waiting for transfers between devices, along(): return lax.ppermute(x, 'expert', [(i, i ^ shift) for i in range(experts)])  4.17 us
  transfers between devices with their start and end apart: 22, of which 7 were waited for; matrix products, arithmetic and copies ran while one was open for 0% of the time, Pallas kernels for 28%

profile of v5, /device:TPU:0, one launch (start us, length us, event | category | flops | bytes accessed | tf_op | source)
XLA Modules:
  0.0 75.2 jit_solution(2528361093922810569)
XLA Ops:
  0.6 3.1 %collective-permute-start.4 = (bf16[16,3072]{1,0:T(8,128)(2,1)}, bf16[16,3072]{1,0:T(8,128)(2,1)S(1)}, u32[]{:S(2)}, u32[]{:S(2)}) collective-permute-start(bf16[16,3072]{1,0:T(8,128)(2,1)} %tokens), channel_id=1, source_target_pairs={{0,4},{4,0},{8,12},{12,8},{1,5},{5,1},{9,13},{13,9},{2,6},{6,2},{1... | collective-permute-start | bytes 294920 | tf_op jit(solution)/shard_map/ppermute | solution.py:235
  3.7 2.6 %collective-permute-start.5 = (bf16[16,3072]{1,0:T(8,128)(2,1)}, bf16[16,3072]{1,0:T(8,128)(2,1)S(1)}, u32[]{:S(2)}, u32[]{:S(2)}) collective-permute-start(bf16[16,3072]{1,0:T(8,128)(2,1)} %tokens), channel_id=1, source_target_pairs={{0,8},{4,12},{8,0},{12,4},{1,9},{5,13},{9,1},{13,5},{2,10},{6,14},... | collective-permute-start | bytes 294920 | tf_op jit(solution)/shard_map/ppermute | solution.py:235
  6.3 0.0 collective-permute-start.6
  6.3 0.9 %collective-permute-start = (bf16[16,3072]{1,0:T(8,128)(2,1)}, bf16[16,3072]{1,0:T(8,128)(2,1)S(1)}, u32[]{:S(2)}, u32[]{:S(2)}) collective-permute-start(bf16[16,3072]{1,0:T(8,128)(2,1)} %param.8), channel_id=1, source_target_pairs={{0,4},{4,0},{8,12},{12,8},{1,5},{5,1},{9,13},{13,9},{2,6},{6,2},{1... | collective-permute-start | bytes 294920 | tf_op jit(solution)/shard_map/ppermute | solution.py:235
  7.2 3.5 %collective-permute-start.1 = (bf16[16,3072]{1,0:T(8,128)(2,1)}, bf16[16,3072]{1,0:T(8,128)(2,1)S(1)}, u32[]{:S(2)}, u32[]{:S(2)}) collective-permute-start(bf16[16,3072]{1,0:T(8,128)(2,1)} %param.8), channel_id=1, source_target_pairs={{0,8},{4,12},{8,0},{12,4},{1,9},{5,13},{9,1},{13,5},{2,10},{6,14},... | collective-permute-start | bytes 294920 | tf_op jit(solution)/shard_map/ppermute | solution.py:235
  10.7 0.0 copy-start.2
  10.7 0.0 copy-start
  10.7 4.6 %shard_map.86.refs_0_ = bf16[2,3072,2048]{2,1,0:T(8,128)(2,1)S(1)} custom-call(bf16[3072,2048]{1,0:T(8,128)(2,1)} %bitcast.9), custom_call_target="tpu_custom_call" | custom-call | tf_op jit(solution)/shard_map/pallas_call | solution.py:212
  15.3 0.0 collective-permute-done.4
  15.3 0.0 copy-done.2
  15.4 0.1 collective-permute-start.2
  15.4 0.0 collective-permute-done.5
  15.4 0.0 collective-permute-done.6
  15.5 0.0 copy-done
  15.5 1.8 %collective-permute-start.7 = (bf16[64,3072]{1,0:T(8,128)(2,1)S(1)}, bf16[64,3072]{1,0:T(8,128)(2,1)S(1)}, u32[]{:S(2)}, u32[]{:S(2)}) collective-permute-start(bf16[64,3072]{1,0:T(8,128)(2,1)S(1)} %pad_maximum_fusion.refs_0_), channel_id=1, source_target_pairs={{0,2},{1,3},{2,0},{3,1},{4,6},{5,7},{6,4},{7,5},{8,10},{9,11},{10,... | collective-permute-start | bytes 1179656 | tf_op jit(solution)/shard_map/ppermute | solution.py:238
  17.3 0.1 collective-permute-start.8
  17.4 0.0 collective-permute-done
  17.4 4.6 %shard_map.87.refs_4_ = bf16[2,3072,2048]{2,1,0:T(8,128)(2,1)S(1)} custom-call(bf16[3072,2048]{1,0:T(8,128)(2,1)} %bitcast.10, bf16[2,3072,2048]{2,1,0:T(8,128)(2,1)S(1)} %shard_map.86.refs_0_), custom_call_target="tpu_custom_call", output_to_operand_aliasing={{}: (1, {})} | custom-call | tf_op jit(solution)/shard_map/pallas_call | solution.py:212
  22.0 3.0 %collective-permute-done.7.refs_1_ = bf16[64,3072]{1,0:T(8,128)(2,1)S(1)} collective-permute-done((bf16[64,3072]{1,0:T(8,128)(2,1)S(1)}, bf16[64,3072]{1,0:T(8,128)(2,1)S(1)}, u32[]{:S(2)}, u32[]{:S(2)}) %collective-permute-start.7) | collective-permute-done | bytes 393248 | tf_op jit(solution)/shard_map/ppermute | solution.py:238
  25.0 0.0 collective-permute-start.9
  25.0 0.0 collective-permute-done.1
  25.0 0.0 collective-permute-done.2
  25.1 1.7 %collective-permute-start.3 = (bf16[64,3072]{1,0:T(8,128)(2,1)S(1)}, bf16[64,3072]{1,0:T(8,128)(2,1)S(1)}, u32[]{:S(2)}, u32[]{:S(2)}) collective-permute-start(bf16[64,3072]{1,0:T(8,128)(2,1)S(1)} %constant_dynamic-update-slice_fusion.refs_0_), channel_id=1, source_target_pairs={{0,3},{1,2},{2,1},{3,0},{4,7},{5,6},{6,5},{7,4},{8,11},{9,10},{10,... | collective-permute-start | bytes 1179656 | tf_op jit(solution)/shard_map/ppermute | solution.py:238
  26.8 0.0 collective-permute-start.11
  26.8 0.0 collective-permute-done.8.refs_2_
  26.8 0.0 collective-permute-done.9.refs_3_
  26.8 7.6 %shard_map.88 = (f32[2,256,2048]{2,1,0:T(8,128)S(1)}, bf16[2,3072,2048]{2,1,0:T(8,128)(2,1)S(1)}, bf16[1024,3072]{1,0:T(8,128)(2,1)S(1)}) custom-call(bf16[64,3072]{1,0:T(8,128)(2,1)S(1)} %pad_maximum_fusion.refs_0_, bf16[64,3072]{1,0:T(8,128)(2,1)S(1)} %collective-permute-done.7.refs_1_, ...), custom_call_target="tpu_custom_call", output_to_operand_aliasing={{1}: (4, {})} | custom-call | flops 6442450944 | bytes 25165824 | tf_op jit(solution)/shard_map/pallas_call | solution.py:212
  34.4 1.5 %collective-permute-done.3.refs_3_ = bf16[64,3072]{1,0:T(8,128)(2,1)S(1)} collective-permute-done((bf16[64,3072]{1,0:T(8,128)(2,1)S(1)}, bf16[64,3072]{1,0:T(8,128)(2,1)S(1)}, u32[]{:S(2)}, u32[]{:S(2)}) %collective-permute-start.3) | collective-permute-done | bytes 393248 | tf_op jit(solution)/shard_map/ppermute | solution.py:238
  35.9 0.5 collective-permute-start.10
  36.4 0.0 collective-permute-done.11.refs_2_
  36.4 1.3 %collective-permute-done.10.refs_1_ = bf16[64,3072]{1,0:T(8,128)(2,1)S(1)} collective-permute-done((bf16[64,3072]{1,0:T(8,128)(2,1)S(1)}, bf16[64,3072]{1,0:T(8,128)(2,1)S(1)}, u32[]{:S(2)}, u32[]{:S(2)}) %collective-permute-start.10) | collective-permute-done | bytes 393248 | tf_op jit(solution)/shard_map/ppermute | solution.py:238
  37.7 8.5 %shard_map.89 = (f32[128,1536]{1,0:T(8,128)S(1)}, bf16[128,1536]{1,0:T(8,128)(2,1)S(1)}, bf16[2,256,2048]{2,1,0:T(8,128)(2,1)S(1)}, f32[256,1]{1,0:T(8,128)S(1)}, bf16[2,3072,2048]{2,1,0:T(8,128)(2,1)S(1)}) custom-call(bf16[64,3072]{1,0:T(8,128)(2,1)S(1)} %constant_dynamic-update-slice_fusion.refs_0_, ...), custom_call_target="tpu_custom_call", output_to_operand_aliasing={{4}: (4, {})} | custom-call | flops 6442450944 | bytes 37748736 | tf_op jit(solution)/shard_map/pallas_call | solution.py:212
  46.2 0.4 collective-permute-start.12
  46.7 0.0 copy-start.1
  46.7 0.0 copy-start.3
  46.7 3.4 %shard_map.92 = (f32[128,1664]{1,0:T(8,128)S(1)}, bf16[128,1664]{1,0:T(8,128)(2,1)S(1)}) custom-call(bf16[2,3072,2048]{2,1,0:T(8,128)(2,1)S(1)} %get-tuple-element.56.weights, bf16[2,256,2048]{2,1,0:T(8,128)(2,1)S(1)} %get-tuple-element.57.grads, f32[256,1]{1,0:T(8,128)S(1)} %get-tuple-element.58.score), custom_call_target="tpu_custom_call" | custom-call | flops 3221225472 | bytes 12582912 | tf_op jit(solution)/shard_map/pallas_call | solution.py:212
  50.1 0.2 collective-permute-start.17
  50.3 0.0 collective-permute-done.12.theirs
  50.3 0.1 shard_map.90
  50.4 1.6 %collective-permute-start.13 = (bf16[64,1536]{1,0:T(8,128)(2,1)S(1)}, bf16[64,1536]{1,0:T(8,128)(2,1)S(1)}, u32[]{:S(2)}, u32[]{:S(2)}) collective-permute-start(bf16[64,1536]{1,0:T(8,128)(2,1)S(1)} %get-tuple-element.51), channel_id=1, source_target_pairs={{0,2},{1,3},{2,0},{3,1},{4,6},{5,7},{6,4},{7,5},{8,10},{9,11},{10,... | collective-permute-start | bytes 589832 | tf_op jit(solution)/shard_map/ppermute | solution.py:238
  52.0 0.0 collective-permute-done.17.theirs
  52.0 0.1 shard_map.93
  52.1 1.5 %collective-permute-start.18 = (bf16[64,1664]{1,0:T(8,128)(2,1)S(1)}, bf16[64,1664]{1,0:T(8,128)(2,1)S(1)}, u32[]{:S(2)}, u32[]{:S(2)}) collective-permute-start(bf16[64,1664]{1,0:T(8,128)(2,1)S(1)} %get-tuple-element.63), channel_id=1, source_target_pairs={{0,2},{1,3},{2,0},{3,1},{4,6},{5,7},{6,4},{7,5},{8,10},{9,11},{10,... | collective-permute-start | bytes 638984 | tf_op jit(solution)/shard_map/ppermute | solution.py:238
  53.7 4.5 %collective-permute-done.13.theirs = bf16[64,1536]{1,0:T(8,128)(2,1)S(1)} collective-permute-done((bf16[64,1536]{1,0:T(8,128)(2,1)S(1)}, bf16[64,1536]{1,0:T(8,128)(2,1)S(1)}, u32[]{:S(2)}, u32[]{:S(2)}) %collective-permute-start.13) | collective-permute-done | bytes 196640 | tf_op jit(solution)/shard_map/ppermute | solution.py:238
  58.2 3.5 %collective-permute-start.14 = (bf16[16,1536]{1,0:T(8,128)(2,1)S(1)}, bf16[16,1536]{1,0:T(8,128)(2,1)S(1)}, u32[]{:S(2)}, u32[]{:S(2)}) collective-permute-start(bf16[16,1536]{1,0:T(8,128)(2,1)S(1)} %get-tuple-element.53), channel_id=1, source_target_pairs={{0,4},{4,0},{8,12},{12,8},{1,5},{5,1},{9,13},{13,9},{2,6},{6,2},{1... | collective-permute-start | bytes 147464 | tf_op jit(solution)/shard_map/ppermute | solution.py:235
  61.7 0.0 copy-done.1
  61.7 0.0 copy-done.3
  61.7 0.1 copy.16.routes
  61.8 1.8 %collective-permute-start.15 = (bf16[16,1536]{1,0:T(8,128)(2,1)S(1)}, bf16[16,1536]{1,0:T(8,128)(2,1)S(1)}, u32[]{:S(2)}, u32[]{:S(2)}) collective-permute-start(bf16[16,1536]{1,0:T(8,128)(2,1)S(1)} %get-tuple-element.54), channel_id=1, source_target_pairs={{0,8},{4,12},{8,0},{12,4},{1,9},{5,13},{9,1},{13,5},{2,10},{6,14},... | collective-permute-start | bytes 147464 | tf_op jit(solution)/shard_map/ppermute | solution.py:235
  63.6 1.5 %collective-permute-start.16 = (bf16[16,1536]{1,0:T(8,128)(2,1)S(1)}, bf16[16,1536]{1,0:T(8,128)(2,1)S(1)}, u32[]{:S(2)}, u32[]{:S(2)}) collective-permute-start(bf16[16,1536]{1,0:T(8,128)(2,1)S(1)} %get-tuple-element.55), channel_id=1, source_target_pairs={{0,12},{4,8},{8,4},{12,0},{1,13},{5,9},{9,5},{13,1},{2,14},{6,10},... | collective-permute-start | bytes 147464 | tf_op jit(solution)/shard_map/ppermute | solution.py:235
  65.2 0.0 collective-permute-done.18.theirs
  65.2 0.1 shard_map.94
  65.3 0.6 collective-permute-start.19
  65.8 2.4 %collective-permute-start.20 = (bf16[16,1664]{1,0:T(8,128)(2,1)S(1)}, bf16[16,1664]{1,0:T(8,128)(2,1)S(1)}, u32[]{:S(2)}, u32[]{:S(2)}) collective-permute-start(bf16[16,1664]{1,0:T(8,128)(2,1)S(1)} %get-tuple-element.66), channel_id=1, source_target_pairs={{0,8},{4,12},{8,0},{12,4},{1,9},{5,13},{9,1},{13,5},{2,10},{6,14},... | collective-permute-start | bytes 159752 | tf_op jit(solution)/shard_map/ppermute | solution.py:235
  68.2 0.0 collective-permute-done.14.refs_1_
  68.2 1.5 %collective-permute-start.21 = (bf16[16,1664]{1,0:T(8,128)(2,1)S(1)}, bf16[16,1664]{1,0:T(8,128)(2,1)S(1)}, u32[]{:S(2)}, u32[]{:S(2)}) collective-permute-start(bf16[16,1664]{1,0:T(8,128)(2,1)S(1)} %get-tuple-element.67), channel_id=1, source_target_pairs={{0,12},{4,8},{8,4},{12,0},{1,13},{5,9},{9,5},{13,1},{2,14},{6,10},... | collective-permute-start | bytes 159752 | tf_op jit(solution)/shard_map/ppermute | solution.py:235
  69.7 0.2 shard_map.95
  70.0 0.0 collective-permute-done.15.refs_2_
  70.0 0.0 collective-permute-done.16.refs_3_
  70.0 0.3 collective-permute-done.19.refs_5_
  70.3 2.6 %collective-permute-done.20.refs_6_ = bf16[16,1664]{1,0:T(8,128)(2,1)S(1)} collective-permute-done((bf16[16,1664]{1,0:T(8,128)(2,1)S(1)}, bf16[16,1664]{1,0:T(8,128)(2,1)S(1)}, u32[]{:S(2)}, u32[]{:S(2)}) %collective-permute-start.20) | collective-permute-done | bytes 53280 | tf_op jit(solution)/shard_map/ppermute | solution.py:235
  73.0 1.2 %collective-permute-done.21.refs_7_ = bf16[16,1664]{1,0:T(8,128)(2,1)S(1)} collective-permute-done((bf16[16,1664]{1,0:T(8,128)(2,1)S(1)}, bf16[16,1664]{1,0:T(8,128)(2,1)S(1)}, u32[]{:S(2)}, u32[]{:S(2)}) %collective-permute-start.21) | collective-permute-done | bytes 53280 | tf_op jit(solution)/shard_map/ppermute | solution.py:235
  74.2 1.1 %shard_map.96 = (bf16[16,3072]{1,0:T(8,128)(2,1)}, f32[2,16]{1,0:T(2,128)}) custom-call(f32[16,1536]{1,0:T(8,128)S(1)} %get-tuple-element.52.refs_0_, bf16[16,1536]{1,0:T(8,128)(2,1)S(1)} %collective-permute-done.14.refs_1_, bf16[16,1536]{1,0:T(8,128)(2,1)S(1)} %collective-permute-done.15.refs_2_, bf16[16,1536]{1,0:T(8,128)(2,1)S(1)} %collective-permute-done.16.refs_3_, ...), custom_call_target="tpu_custom_call" | custom-call | tf_op jit(solution)/shard_map/pallas_call | solution.py:212
  (8 shorter events, 0.1 us)
Async XLA Ops:
  0.6 14.7 %collective-permute-start.4 = (bf16[16,3072]{1,0:T(8,128)(2,1)}, bf16[16,3072]{1,0:T(8,128)(2,1)S(1)}, u32[]{:S(2)}, u32[]{:S(2)}) collective-permute-start(bf16[16,3072]{1,0:T(8,128)(2,1)} %tokens), channel_id=1, source_target_pairs={{0,4},{4,0},{8,12},{12,8},{1,5},{5,1},{9,13},{13,9},{2,6},{6,2},{1... | collective-permute-start | bytes 294920 | tf_op jit(solution)/shard_map/ppermute | solution.py:235
  3.7 11.7 %collective-permute-start.5 = (bf16[16,3072]{1,0:T(8,128)(2,1)}, bf16[16,3072]{1,0:T(8,128)(2,1)S(1)}, u32[]{:S(2)}, u32[]{:S(2)}) collective-permute-start(bf16[16,3072]{1,0:T(8,128)(2,1)} %tokens), channel_id=1, source_target_pairs={{0,8},{4,12},{8,0},{12,4},{1,9},{5,13},{9,1},{13,5},{2,10},{6,14},... | collective-permute-start | bytes 294920 | tf_op jit(solution)/shard_map/ppermute | solution.py:235
  6.3 9.1 %collective-permute-start.6 = (bf16[16,3072]{1,0:T(8,128)(2,1)}, bf16[16,3072]{1,0:T(8,128)(2,1)S(1)}, u32[]{:S(2)}, u32[]{:S(2)}) collective-permute-start(bf16[16,3072]{1,0:T(8,128)(2,1)} %tokens), channel_id=1, source_target_pairs={{0,12},{4,8},{8,4},{12,0},{1,13},{5,9},{9,5},{13,1},{2,14},{6,10},... | collective-permute-start | bytes 294920 | tf_op jit(solution)/shard_map/ppermute | solution.py:235
  6.3 11.0 %collective-permute-start = (bf16[16,3072]{1,0:T(8,128)(2,1)}, bf16[16,3072]{1,0:T(8,128)(2,1)S(1)}, u32[]{:S(2)}, u32[]{:S(2)}) collective-permute-start(bf16[16,3072]{1,0:T(8,128)(2,1)} %param.8), channel_id=1, source_target_pairs={{0,4},{4,0},{8,12},{12,8},{1,5},{5,1},{9,13},{13,9},{2,6},{6,2},{1... | collective-permute-start | bytes 294920 | tf_op jit(solution)/shard_map/ppermute | solution.py:235
  7.2 17.8 %collective-permute-start.1 = (bf16[16,3072]{1,0:T(8,128)(2,1)}, bf16[16,3072]{1,0:T(8,128)(2,1)S(1)}, u32[]{:S(2)}, u32[]{:S(2)}) collective-permute-start(bf16[16,3072]{1,0:T(8,128)(2,1)} %param.8), channel_id=1, source_target_pairs={{0,8},{4,12},{8,0},{12,4},{1,9},{5,13},{9,1},{13,5},{2,10},{6,14},... | collective-permute-start | bytes 294920 | tf_op jit(solution)/shard_map/ppermute | solution.py:235
  10.7 4.6 %copy-start.2 = (bf16[16,3072]{1,0:T(8,128)(2,1)S(1)}, bf16[16,3072]{1,0:T(8,128)(2,1)}, u32[]{:S(2)}) copy-start(bf16[16,3072]{1,0:T(8,128)(2,1)} %param.8) | copy-start | bytes 294916
  10.7 4.8 %copy-start = (bf16[16,3072]{1,0:T(8,128)(2,1)S(1)}, bf16[16,3072]{1,0:T(8,128)(2,1)}, u32[]{:S(2)}) copy-start(bf16[16,3072]{1,0:T(8,128)(2,1)} %tokens) | copy-start | bytes 294916
  15.4 9.7 %collective-permute-start.2 = (bf16[16,3072]{1,0:T(8,128)(2,1)S(1)}, bf16[16,3072]{1,0:T(8,128)(2,1)S(1)}, u32[]{:S(2)}, u32[]{:S(2)}) collective-permute-start(bf16[16,3072]{1,0:T(8,128)(2,1)S(1)} %copy-done.2), channel_id=1, source_target_pairs={{0,12},{4,8},{8,4},{12,0},{1,13},{5,9},{9,5},{13,1},{2,14},{6,10},... | collective-permute-start | bytes 294920 | tf_op jit(solution)/shard_map/ppermute | solution.py:235
  15.5 9.5 %collective-permute-start.7 = (bf16[64,3072]{1,0:T(8,128)(2,1)S(1)}, bf16[64,3072]{1,0:T(8,128)(2,1)S(1)}, u32[]{:S(2)}, u32[]{:S(2)}) collective-permute-start(bf16[64,3072]{1,0:T(8,128)(2,1)S(1)} %pad_maximum_fusion.refs_0_), channel_id=1, source_target_pairs={{0,2},{1,3},{2,0},{3,1},{4,6},{5,7},{6,4},{7,5},{8,10},{9,11},{10,... | collective-permute-start | bytes 1179656 | tf_op jit(solution)/shard_map/ppermute | solution.py:238
  17.3 9.5 %collective-permute-start.8 = (bf16[64,3072]{1,0:T(8,128)(2,1)S(1)}, bf16[64,3072]{1,0:T(8,128)(2,1)S(1)}, u32[]{:S(2)}, u32[]{:S(2)}) collective-permute-start(bf16[64,3072]{1,0:T(8,128)(2,1)S(1)} %pad_maximum_fusion.refs_0_), channel_id=1, source_target_pairs={{0,1},{1,0},{2,3},{3,2},{4,5},{5,4},{6,7},{7,6},{8,9},{9,8},{10,11... | collective-permute-start | bytes 1179656 | tf_op jit(solution)/shard_map/ppermute | solution.py:238
  25.0 1.8 %collective-permute-start.9 = (bf16[64,3072]{1,0:T(8,128)(2,1)S(1)}, bf16[64,3072]{1,0:T(8,128)(2,1)S(1)}, u32[]{:S(2)}, u32[]{:S(2)}) collective-permute-start(bf16[64,3072]{1,0:T(8,128)(2,1)S(1)} %collective-permute-done.7.refs_1_), channel_id=1, source_target_pairs={{0,1},{1,0},{2,3},{3,2},{4,5},{5,4},{6,7},{7,6},{8,9},{9,8},{10,11... | collective-permute-start | bytes 1179656 | tf_op jit(solution)/shard_map/ppermute | solution.py:238
  25.1 10.8 %collective-permute-start.3 = (bf16[64,3072]{1,0:T(8,128)(2,1)S(1)}, bf16[64,3072]{1,0:T(8,128)(2,1)S(1)}, u32[]{:S(2)}, u32[]{:S(2)}) collective-permute-start(bf16[64,3072]{1,0:T(8,128)(2,1)S(1)} %constant_dynamic-update-slice_fusion.refs_0_), channel_id=1, source_target_pairs={{0,3},{1,2},{2,1},{3,0},{4,7},{5,6},{6,5},{7,4},{8,11},{9,10},{10,... | collective-permute-start | bytes 1179656 | tf_op jit(solution)/shard_map/ppermute | solution.py:238
  26.8 9.6 %collective-permute-start.11 = (bf16[64,3072]{1,0:T(8,128)(2,1)S(1)}, bf16[64,3072]{1,0:T(8,128)(2,1)S(1)}, u32[]{:S(2)}, u32[]{:S(2)}) collective-permute-start(bf16[64,3072]{1,0:T(8,128)(2,1)S(1)} %constant_dynamic-update-slice_fusion.refs_0_), channel_id=1, source_target_pairs={{0,1},{1,0},{2,3},{3,2},{4,5},{5,4},{6,7},{7,6},{8,9},{9,8},{10,11... | collective-permute-start | bytes 1179656 | tf_op jit(solution)/shard_map/ppermute | solution.py:238
  35.9 1.8 %collective-permute-start.10 = (bf16[64,3072]{1,0:T(8,128)(2,1)S(1)}, bf16[64,3072]{1,0:T(8,128)(2,1)S(1)}, u32[]{:S(2)}, u32[]{:S(2)}) collective-permute-start(bf16[64,3072]{1,0:T(8,128)(2,1)S(1)} %collective-permute-done.3.refs_3_), channel_id=1, source_target_pairs={{0,1},{1,0},{2,3},{3,2},{4,5},{5,4},{6,7},{7,6},{8,9},{9,8},{10,11... | collective-permute-start | bytes 1179656 | tf_op jit(solution)/shard_map/ppermute | solution.py:238
  46.2 4.1 %collective-permute-start.12 = (bf16[128,1536]{1,0:T(8,128)(2,1)S(1)}, bf16[128,1536]{1,0:T(8,128)(2,1)S(1)}, u32[]{:S(2)}, u32[]{:S(2)}) collective-permute-start(bf16[128,1536]{1,0:T(8,128)(2,1)S(1)} %get-tuple-element.49), channel_id=1, source_target_pairs={{0,1},{1,0},{2,3},{3,2},{4,5},{5,4},{6,7},{7,6},{8,9},{9,8},{10,11... | collective-permute-start | bytes 1179656 | tf_op jit(solution)/shard_map/ppermute | solution.py:238
  46.7 15.0 %copy-start.1 = (bf16[3072,4]{0,1:T(4,128)(2,1)S(1)}, bf16[3072,4]{0,1:T(4,128)(2,1)}, u32[]{:S(2)}) copy-start(bf16[3072,4]{0,1:T(4,128)(2,1)} %param.10) | copy-start | bytes 73732
  46.7 15.0 %copy-start.3 = (s32[16,2]{0,1:T(2,128)S(1)}, s32[16,2]{0,1:T(2,128)}, u32[]{:S(2)}) copy-start(s32[16,2]{0,1:T(2,128)} %param.9) | copy-start | bytes 388
  50.1 1.9 %collective-permute-start.17 = (bf16[128,1664]{1,0:T(8,128)(2,1)S(1)}, bf16[128,1664]{1,0:T(8,128)(2,1)S(1)}, u32[]{:S(2)}, u32[]{:S(2)}) collective-permute-start(bf16[128,1664]{1,0:T(8,128)(2,1)S(1)} %get-tuple-element.61), channel_id=1, source_target_pairs={{0,1},{1,0},{2,3},{3,2},{4,5},{5,4},{6,7},{7,6},{8,9},{9,8},{10,11... | collective-permute-start | bytes 1277960 | tf_op jit(solution)/shard_map/ppermute | solution.py:238
  50.4 7.8 %collective-permute-start.13 = (bf16[64,1536]{1,0:T(8,128)(2,1)S(1)}, bf16[64,1536]{1,0:T(8,128)(2,1)S(1)}, u32[]{:S(2)}, u32[]{:S(2)}) collective-permute-start(bf16[64,1536]{1,0:T(8,128)(2,1)S(1)} %get-tuple-element.51), channel_id=1, source_target_pairs={{0,2},{1,3},{2,0},{3,1},{4,6},{5,7},{6,4},{7,5},{8,10},{9,11},{10,... | collective-permute-start | bytes 589832 | tf_op jit(solution)/shard_map/ppermute | solution.py:238
  52.1 13.0 %collective-permute-start.18 = (bf16[64,1664]{1,0:T(8,128)(2,1)S(1)}, bf16[64,1664]{1,0:T(8,128)(2,1)S(1)}, u32[]{:S(2)}, u32[]{:S(2)}) collective-permute-start(bf16[64,1664]{1,0:T(8,128)(2,1)S(1)} %get-tuple-element.63), channel_id=1, source_target_pairs={{0,2},{1,3},{2,0},{3,1},{4,6},{5,7},{6,4},{7,5},{8,10},{9,11},{10,... | collective-permute-start | bytes 638984 | tf_op jit(solution)/shard_map/ppermute | solution.py:238
  58.2 10.0 %collective-permute-start.14 = (bf16[16,1536]{1,0:T(8,128)(2,1)S(1)}, bf16[16,1536]{1,0:T(8,128)(2,1)S(1)}, u32[]{:S(2)}, u32[]{:S(2)}) collective-permute-start(bf16[16,1536]{1,0:T(8,128)(2,1)S(1)} %get-tuple-element.53), channel_id=1, source_target_pairs={{0,4},{4,0},{8,12},{12,8},{1,5},{5,1},{9,13},{13,9},{2,6},{6,2},{1... | collective-permute-start | bytes 147464 | tf_op jit(solution)/shard_map/ppermute | solution.py:235
  61.8 8.2 %collective-permute-start.15 = (bf16[16,1536]{1,0:T(8,128)(2,1)S(1)}, bf16[16,1536]{1,0:T(8,128)(2,1)S(1)}, u32[]{:S(2)}, u32[]{:S(2)}) collective-permute-start(bf16[16,1536]{1,0:T(8,128)(2,1)S(1)} %get-tuple-element.54), channel_id=1, source_target_pairs={{0,8},{4,12},{8,0},{12,4},{1,9},{5,13},{9,1},{13,5},{2,10},{6,14},... | collective-permute-start | bytes 147464 | tf_op jit(solution)/shard_map/ppermute | solution.py:235
  63.6 6.3 %collective-permute-start.16 = (bf16[16,1536]{1,0:T(8,128)(2,1)S(1)}, bf16[16,1536]{1,0:T(8,128)(2,1)S(1)}, u32[]{:S(2)}, u32[]{:S(2)}) collective-permute-start(bf16[16,1536]{1,0:T(8,128)(2,1)S(1)} %get-tuple-element.55), channel_id=1, source_target_pairs={{0,12},{4,8},{8,4},{12,0},{1,13},{5,9},{9,5},{13,1},{2,14},{6,10},... | collective-permute-start | bytes 147464 | tf_op jit(solution)/shard_map/ppermute | solution.py:235
  65.3 5.1 %collective-permute-start.19 = (bf16[16,1664]{1,0:T(8,128)(2,1)S(1)}, bf16[16,1664]{1,0:T(8,128)(2,1)S(1)}, u32[]{:S(2)}, u32[]{:S(2)}) collective-permute-start(bf16[16,1664]{1,0:T(8,128)(2,1)S(1)} %get-tuple-element.65), channel_id=1, source_target_pairs={{0,4},{4,0},{8,12},{12,8},{1,5},{5,1},{9,13},{13,9},{2,6},{6,2},{1... | collective-permute-start | bytes 159752 | tf_op jit(solution)/shard_map/ppermute | solution.py:235
  65.8 7.1 %collective-permute-start.20 = (bf16[16,1664]{1,0:T(8,128)(2,1)S(1)}, bf16[16,1664]{1,0:T(8,128)(2,1)S(1)}, u32[]{:S(2)}, u32[]{:S(2)}) collective-permute-start(bf16[16,1664]{1,0:T(8,128)(2,1)S(1)} %get-tuple-element.66), channel_id=1, source_target_pairs={{0,8},{4,12},{8,0},{12,4},{1,9},{5,13},{9,1},{13,5},{2,10},{6,14},... | collective-permute-start | bytes 159752 | tf_op jit(solution)/shard_map/ppermute | solution.py:235
  68.2 5.9 %collective-permute-start.21 = (bf16[16,1664]{1,0:T(8,128)(2,1)S(1)}, bf16[16,1664]{1,0:T(8,128)(2,1)S(1)}, u32[]{:S(2)}, u32[]{:S(2)}) collective-permute-start(bf16[16,1664]{1,0:T(8,128)(2,1)S(1)} %get-tuple-element.67), channel_id=1, source_target_pairs={{0,12},{4,8},{8,4},{12,0},{1,13},{5,9},{9,5},{13,1},{2,14},{6,10},... | collective-permute-start | bytes 159752 | tf_op jit(solution)/shard_map/ppermute | solution.py:235

commit v6 on v5

--- a/solution.py
+++ b/solution.py
@@ -274,7 +274,8 @@
         (out,) = call(functools.partial(load_kernel, k), args, [pair_of], specs, sem, grant, cost(0, 0), alias)
         return vmem(out)
 
-    x_column, weights = lax.optimization_barrier((column(tokens), load(0, w_gate)))
+    grad_out, weights = lax.optimization_barrier((grad_out, load(0, w_gate)))
+    x_column, weights = lax.optimization_barrier((column(tokens), weights))
     x_pieces = spread([x_column], bits[:-1])
     x_pieces[-1], weights = lax.optimization_barrier((x_pieces[-1], load(1, w_up, weights)))
     x_pieces = spread(x_pieces, bits[-1:])

time: 75.4 us -> 74.2 us (0.984)
  starting transfers between devices: 29.2 us -> 26.8 us
  waiting for transfers between devices: 14.6 us -> 15.8 us
    ppermute x12, starting transfers between devices: 21.4 us -> 19 us  [along(): return lax.ppermute(x, 'expert', [(i, i ^ shift) for i in range(experts)])]
    ppermute x12, waiting for transfers between devices: 4.17 us -> 5.38 us  [along(): return lax.ppermute(x, 'expert', [(i, i ^ shift) for i in range(experts)])]
where the time goes in v6:
time: 74.2 us; the launch traced here: 74 us
  Pallas kernels  30.4 us (41%)
  starting transfers between devices  26.8 us (36%)
  waiting for transfers between devices  15.8 us (21%)
  between operations  0.82 us (1%)
    pallas_call x11, Pallas kernels, call(): pl.pallas_call(kernel, out_shape=outs, in_specs=specs, out_specs=[VMEM] *...  30.4 us
    ppermute x12, starting transfers between devices, along(): return lax.ppermute(x, 'expert', [(i, i ^ shift) for i in range(experts)])  19 us
    ppermute x10, waiting for transfers between devices, across(): return lax.ppermute(x, 'hidden', [(i, i ^ bit) for i in range(hidden)])  10.4 us
    ppermute x10, starting transfers between devices, across(): return lax.ppermute(x, 'hidden', [(i, i ^ bit) for i in range(hidden)])  7.8 us
    ppermute x12, waiting for transfers between devices, along(): return lax.ppermute(x, 'expert', [(i, i ^ shift) for i in range(experts)])  5.38 us
  transfers between devices with their start and end apart: 22, of which 7 were waited for; matrix products, arithmetic and copies ran while one was open for 0% of the time, Pallas kernels for 28%

profile of v6, /device:TPU:0, one launch (start us, length us, event | category | flops | bytes accessed | tf_op | source)
XLA Modules:
  0.0 74.0 jit_solution(334686178660021758)
XLA Ops:
  0.6 3.1 %collective-permute-start.4 = (bf16[16,3072]{1,0:T(8,128)(2,1)}, bf16[16,3072]{1,0:T(8,128)(2,1)S(1)}, u32[]{:S(2)}, u32[]{:S(2)}) collective-permute-start(bf16[16,3072]{1,0:T(8,128)(2,1)} %tokens), channel_id=1, source_target_pairs={{0,4},{4,0},{8,12},{12,8},{1,5},{5,1},{9,13},{13,9},{2,6},{6,2},{1... | collective-permute-start | bytes 294920 | tf_op jit(solution)/shard_map/ppermute | solution.py:235
  3.7 2.6 %collective-permute-start.5 = (bf16[16,3072]{1,0:T(8,128)(2,1)}, bf16[16,3072]{1,0:T(8,128)(2,1)S(1)}, u32[]{:S(2)}, u32[]{:S(2)}) collective-permute-start(bf16[16,3072]{1,0:T(8,128)(2,1)} %tokens), channel_id=1, source_target_pairs={{0,8},{4,12},{8,0},{12,4},{1,9},{5,13},{9,1},{13,5},{2,10},{6,14},... | collective-permute-start | bytes 294920 | tf_op jit(solution)/shard_map/ppermute | solution.py:235
  6.3 0.0 collective-permute-start.6
  6.3 0.0 copy-start.2
  6.3 0.0 copy-start
  6.3 4.6 %shard_map.86.refs_0_ = bf16[2,3072,2048]{2,1,0:T(8,128)(2,1)S(1)} custom-call(bf16[3072,2048]{1,0:T(8,128)(2,1)} %bitcast.9), custom_call_target="tpu_custom_call" | custom-call | tf_op jit(solution)/shard_map/pallas_call | solution.py:212
  10.9 0.0 copy-done.2
  11.0 1.0 %collective-permute-start = (bf16[16,3072]{1,0:T(8,128)(2,1)S(1)}, bf16[16,3072]{1,0:T(8,128)(2,1)S(1)}, u32[]{:S(2)}, u32[]{:S(2)}) collective-permute-start(bf16[16,3072]{1,0:T(8,128)(2,1)S(1)} %copy-done.2), channel_id=1, source_target_pairs={{0,4},{4,0},{8,12},{12,8},{1,5},{5,1},{9,13},{13,9},{2,6},{6,2},{1... | collective-permute-start | bytes 294920 | tf_op jit(solution)/shard_map/ppermute | solution.py:235
  11.9 3.5 %collective-permute-start.1 = (bf16[16,3072]{1,0:T(8,128)(2,1)S(1)}, bf16[16,3072]{1,0:T(8,128)(2,1)S(1)}, u32[]{:S(2)}, u32[]{:S(2)}) collective-permute-start(bf16[16,3072]{1,0:T(8,128)(2,1)S(1)} %copy-done.2), channel_id=1, source_target_pairs={{0,8},{4,12},{8,0},{12,4},{1,9},{5,13},{9,1},{13,5},{2,10},{6,14},... | collective-permute-start | bytes 294920 | tf_op jit(solution)/shard_map/ppermute | solution.py:235
  15.4 0.0 collective-permute-done.4
  15.4 0.0 collective-permute-start.2
  15.4 0.0 collective-permute-done.5
  15.4 0.0 collective-permute-done.6
  15.4 0.0 copy-done
  15.5 1.8 %collective-permute-start.7 = (bf16[64,3072]{1,0:T(8,128)(2,1)S(1)}, bf16[64,3072]{1,0:T(8,128)(2,1)S(1)}, u32[]{:S(2)}, u32[]{:S(2)}) collective-permute-start(bf16[64,3072]{1,0:T(8,128)(2,1)S(1)} %pad_maximum_fusion.refs_0_), channel_id=1, source_target_pairs={{0,2},{1,3},{2,0},{3,1},{4,6},{5,7},{6,4},{7,5},{8,10},{9,11},{10,... | collective-permute-start | bytes 1179656 | tf_op jit(solution)/shard_map/ppermute | solution.py:238
  17.3 0.1 collective-permute-start.8
  17.3 0.0 collective-permute-done
  17.4 4.6 %shard_map.87.refs_4_ = bf16[2,3072,2048]{2,1,0:T(8,128)(2,1)S(1)} custom-call(bf16[3072,2048]{1,0:T(8,128)(2,1)} %bitcast.10, bf16[2,3072,2048]{2,1,0:T(8,128)(2,1)S(1)} %shard_map.86.refs_0_), custom_call_target="tpu_custom_call", output_to_operand_aliasing={{}: (1, {})} | custom-call | tf_op jit(solution)/shard_map/pallas_call | solution.py:212
  22.0 3.0 %collective-permute-done.7.refs_1_ = bf16[64,3072]{1,0:T(8,128)(2,1)S(1)} collective-permute-done((bf16[64,3072]{1,0:T(8,128)(2,1)S(1)}, bf16[64,3072]{1,0:T(8,128)(2,1)S(1)}, u32[]{:S(2)}, u32[]{:S(2)}) %collective-permute-start.7) | collective-permute-done | bytes 393248 | tf_op jit(solution)/shard_map/ppermute | solution.py:238
  25.0 0.0 collective-permute-start.9
  25.0 0.0 collective-permute-done.1
  25.0 0.0 collective-permute-done.2
  25.0 1.7 %collective-permute-start.3 = (bf16[64,3072]{1,0:T(8,128)(2,1)S(1)}, bf16[64,3072]{1,0:T(8,128)(2,1)S(1)}, u32[]{:S(2)}, u32[]{:S(2)}) collective-permute-start(bf16[64,3072]{1,0:T(8,128)(2,1)S(1)} %constant_dynamic-update-slice_fusion.refs_0_), channel_id=1, source_target_pairs={{0,3},{1,2},{2,1},{3,0},{4,7},{5,6},{6,5},{7,4},{8,11},{9,10},{10,... | collective-permute-start | bytes 1179656 | tf_op jit(solution)/shard_map/ppermute | solution.py:238
  26.7 0.0 collective-permute-start.11
  26.7 0.0 collective-permute-done.8.refs_2_
  26.7 0.0 collective-permute-done.9.refs_3_
  26.8 7.6 %shard_map.88 = (f32[2,256,2048]{2,1,0:T(8,128)S(1)}, bf16[2,3072,2048]{2,1,0:T(8,128)(2,1)S(1)}, bf16[1024,3072]{1,0:T(8,128)(2,1)S(1)}) custom-call(bf16[64,3072]{1,0:T(8,128)(2,1)S(1)} %pad_maximum_fusion.refs_0_, bf16[64,3072]{1,0:T(8,128)(2,1)S(1)} %collective-permute-done.7.refs_1_, ...), custom_call_target="tpu_custom_call", output_to_operand_aliasing={{1}: (4, {})} | custom-call | flops 6442450944 | bytes 25165824 | tf_op jit(solution)/shard_map/pallas_call | solution.py:212
  34.4 1.5 %collective-permute-done.3.refs_3_ = bf16[64,3072]{1,0:T(8,128)(2,1)S(1)} collective-permute-done((bf16[64,3072]{1,0:T(8,128)(2,1)S(1)}, bf16[64,3072]{1,0:T(8,128)(2,1)S(1)}, u32[]{:S(2)}, u32[]{:S(2)}) %collective-permute-start.3) | collective-permute-done | bytes 393248 | tf_op jit(solution)/shard_map/ppermute | solution.py:238
  35.9 0.5 collective-permute-start.10
  36.3 0.0 collective-permute-done.11.refs_2_
  36.3 1.3 %collective-permute-done.10.refs_1_ = bf16[64,3072]{1,0:T(8,128)(2,1)S(1)} collective-permute-done((bf16[64,3072]{1,0:T(8,128)(2,1)S(1)}, bf16[64,3072]{1,0:T(8,128)(2,1)S(1)}, u32[]{:S(2)}, u32[]{:S(2)}) %collective-permute-start.10) | collective-permute-done | bytes 393248 | tf_op jit(solution)/shard_map/ppermute | solution.py:238
  37.7 8.5 %shard_map.89 = (f32[128,1536]{1,0:T(8,128)S(1)}, bf16[128,1536]{1,0:T(8,128)(2,1)S(1)}, bf16[2,256,2048]{2,1,0:T(8,128)(2,1)S(1)}, f32[256,1]{1,0:T(8,128)S(1)}, bf16[2,3072,2048]{2,1,0:T(8,128)(2,1)S(1)}) custom-call(bf16[64,3072]{1,0:T(8,128)(2,1)S(1)} %constant_dynamic-update-slice_fusion.refs_0_, ...), custom_call_target="tpu_custom_call", output_to_operand_aliasing={{4}: (4, {})} | custom-call | flops 6442450944 | bytes 37748736 | tf_op jit(solution)/shard_map/pallas_call | solution.py:212
  46.2 0.4 collective-permute-start.12
  46.6 0.0 copy-start.1
  46.6 0.0 copy-start.3
  46.7 3.4 %shard_map.92 = (f32[128,1664]{1,0:T(8,128)S(1)}, bf16[128,1664]{1,0:T(8,128)(2,1)S(1)}) custom-call(bf16[2,3072,2048]{2,1,0:T(8,128)(2,1)S(1)} %get-tuple-element.60.weights, bf16[2,256,2048]{2,1,0:T(8,128)(2,1)S(1)} %get-tuple-element.61.grads, f32[256,1]{1,0:T(8,128)S(1)} %get-tuple-element.62.score), custom_call_target="tpu_custom_call" | custom-call | flops 3221225472 | bytes 12582912 | tf_op jit(solution)/shard_map/pallas_call | solution.py:212
  50.1 0.2 collective-permute-start.17
  50.3 0.0 collective-permute-done.12.theirs
  50.3 0.1 shard_map.90
  50.4 1.6 %collective-permute-start.13 = (bf16[64,1536]{1,0:T(8,128)(2,1)S(1)}, bf16[64,1536]{1,0:T(8,128)(2,1)S(1)}, u32[]{:S(2)}, u32[]{:S(2)}) collective-permute-start(bf16[64,1536]{1,0:T(8,128)(2,1)S(1)} %get-tuple-element.55), channel_id=1, source_target_pairs={{0,2},{1,3},{2,0},{3,1},{4,6},{5,7},{6,4},{7,5},{8,10},{9,11},{10,... | collective-permute-start | bytes 589832 | tf_op jit(solution)/shard_map/ppermute | solution.py:238
  52.0 0.0 collective-permute-done.17.theirs
  52.0 0.1 shard_map.93
  52.1 1.5 %collective-permute-start.18 = (bf16[64,1664]{1,0:T(8,128)(2,1)S(1)}, bf16[64,1664]{1,0:T(8,128)(2,1)S(1)}, u32[]{:S(2)}, u32[]{:S(2)}) collective-permute-start(bf16[64,1664]{1,0:T(8,128)(2,1)S(1)} %get-tuple-element.67), channel_id=1, source_target_pairs={{0,2},{1,3},{2,0},{3,1},{4,6},{5,7},{6,4},{7,5},{8,10},{9,11},{10,... | collective-permute-start | bytes 638984 | tf_op jit(solution)/shard_map/ppermute | solution.py:238
  53.6 4.5 %collective-permute-done.13.theirs = bf16[64,1536]{1,0:T(8,128)(2,1)S(1)} collective-permute-done((bf16[64,1536]{1,0:T(8,128)(2,1)S(1)}, bf16[64,1536]{1,0:T(8,128)(2,1)S(1)}, u32[]{:S(2)}, u32[]{:S(2)}) %collective-permute-start.13) | collective-permute-done | bytes 196640 | tf_op jit(solution)/shard_map/ppermute | solution.py:238
  58.2 0.9 %collective-permute-start.14 = (bf16[16,1536]{1,0:T(8,128)(2,1)S(1)}, bf16[16,1536]{1,0:T(8,128)(2,1)S(1)}, u32[]{:S(2)}, u32[]{:S(2)}) collective-permute-start(bf16[16,1536]{1,0:T(8,128)(2,1)S(1)} %get-tuple-element.57), channel_id=1, source_target_pairs={{0,4},{4,0},{8,12},{12,8},{1,5},{5,1},{9,13},{13,9},{2,6},{6,2},{1... | collective-permute-start | bytes 147464 | tf_op jit(solution)/shard_map/ppermute | solution.py:235
  59.1 0.0 copy-done.1
  59.1 0.0 copy-done.3
  59.1 0.1 copy.16.routes
  59.2 3.3 %collective-permute-start.15 = (bf16[16,1536]{1,0:T(8,128)(2,1)S(1)}, bf16[16,1536]{1,0:T(8,128)(2,1)S(1)}, u32[]{:S(2)}, u32[]{:S(2)}) collective-permute-start(bf16[16,1536]{1,0:T(8,128)(2,1)S(1)} %get-tuple-element.58), channel_id=1, source_target_pairs={{0,8},{4,12},{8,0},{12,4},{1,9},{5,13},{9,1},{13,5},{2,10},{6,14},... | collective-permute-start | bytes 147464 | tf_op jit(solution)/shard_map/ppermute | solution.py:235
  62.5 0.3 collective-permute-start.16
  62.8 0.0 collective-permute-done.18.theirs
  62.8 0.1 shard_map.94
  62.9 0.4 collective-permute-start.19
  63.3 3.7 %collective-permute-start.20 = (bf16[16,1664]{1,0:T(8,128)(2,1)S(1)}, bf16[16,1664]{1,0:T(8,128)(2,1)S(1)}, u32[]{:S(2)}, u32[]{:S(2)}) collective-permute-start(bf16[16,1664]{1,0:T(8,128)(2,1)S(1)} %get-tuple-element.70), channel_id=1, source_target_pairs={{0,8},{4,12},{8,0},{12,4},{1,9},{5,13},{9,1},{13,5},{2,10},{6,14},... | collective-permute-start | bytes 159752 | tf_op jit(solution)/shard_map/ppermute | solution.py:235
  67.0 0.0 collective-permute-done.14.refs_1_
  67.0 0.3 collective-permute-start.21
  67.3 0.2 shard_map.95
  67.6 0.0 collective-permute-done.15.refs_2_
  67.6 0.8 %collective-permute-done.16.refs_3_ = bf16[16,1536]{1,0:T(8,128)(2,1)S(1)} collective-permute-done((bf16[16,1536]{1,0:T(8,128)(2,1)S(1)}, bf16[16,1536]{1,0:T(8,128)(2,1)S(1)}, u32[]{:S(2)}, u32[]{:S(2)}) %collective-permute-start.16) | collective-permute-done | bytes 49184 | tf_op jit(solution)/shard_map/ppermute | solution.py:235
  68.4 0.0 collective-permute-done.19.refs_5_
  68.4 2.2 %collective-permute-done.20.refs_6_ = bf16[16,1664]{1,0:T(8,128)(2,1)S(1)} collective-permute-done((bf16[16,1664]{1,0:T(8,128)(2,1)S(1)}, bf16[16,1664]{1,0:T(8,128)(2,1)S(1)}, u32[]{:S(2)}, u32[]{:S(2)}) %collective-permute-start.20) | collective-permute-done | bytes 53280 | tf_op jit(solution)/shard_map/ppermute | solution.py:235
  70.6 2.3 %collective-permute-done.21.refs_7_ = bf16[16,1664]{1,0:T(8,128)(2,1)S(1)} collective-permute-done((bf16[16,1664]{1,0:T(8,128)(2,1)S(1)}, bf16[16,1664]{1,0:T(8,128)(2,1)S(1)}, u32[]{:S(2)}, u32[]{:S(2)}) %collective-permute-start.21) | collective-permute-done | bytes 53280 | tf_op jit(solution)/shard_map/ppermute | solution.py:235
  73.0 1.1 %shard_map.96 = (bf16[16,3072]{1,0:T(8,128)(2,1)}, f32[2,16]{1,0:T(2,128)}) custom-call(f32[16,1536]{1,0:T(8,128)S(1)} %get-tuple-element.56.refs_0_, bf16[16,1536]{1,0:T(8,128)(2,1)S(1)} %collective-permute-done.14.refs_1_, bf16[16,1536]{1,0:T(8,128)(2,1)S(1)} %collective-permute-done.15.refs_2_, bf16[16,1536]{1,0:T(8,128)(2,1)S(1)} %collective-permute-done.16.refs_3_, ...), custom_call_target="tpu_custom_call" | custom-call | tf_op jit(solution)/shard_map/pallas_call | solution.py:212
  (8 shorter events, 0.1 us)
Async XLA Ops:
  0.6 14.8 %collective-permute-start.4 = (bf16[16,3072]{1,0:T(8,128)(2,1)}, bf16[16,3072]{1,0:T(8,128)(2,1)S(1)}, u32[]{:S(2)}, u32[]{:S(2)}) collective-permute-start(bf16[16,3072]{1,0:T(8,128)(2,1)} %tokens), channel_id=1, source_target_pairs={{0,4},{4,0},{8,12},{12,8},{1,5},{5,1},{9,13},{13,9},{2,6},{6,2},{1... | collective-permute-start | bytes 294920 | tf_op jit(solution)/shard_map/ppermute | solution.py:235
  3.7 11.7 %collective-permute-start.5 = (bf16[16,3072]{1,0:T(8,128)(2,1)}, bf16[16,3072]{1,0:T(8,128)(2,1)S(1)}, u32[]{:S(2)}, u32[]{:S(2)}) collective-permute-start(bf16[16,3072]{1,0:T(8,128)(2,1)} %tokens), channel_id=1, source_target_pairs={{0,8},{4,12},{8,0},{12,4},{1,9},{5,13},{9,1},{13,5},{2,10},{6,14},... | collective-permute-start | bytes 294920 | tf_op jit(solution)/shard_map/ppermute | solution.py:235
  6.3 9.1 %collective-permute-start.6 = (bf16[16,3072]{1,0:T(8,128)(2,1)}, bf16[16,3072]{1,0:T(8,128)(2,1)S(1)}, u32[]{:S(2)}, u32[]{:S(2)}) collective-permute-start(bf16[16,3072]{1,0:T(8,128)(2,1)} %tokens), channel_id=1, source_target_pairs={{0,12},{4,8},{8,4},{12,0},{1,13},{5,9},{9,5},{13,1},{2,14},{6,10},... | collective-permute-start | bytes 294920 | tf_op jit(solution)/shard_map/ppermute | solution.py:235
  6.3 4.6 %copy-start.2 = (bf16[16,3072]{1,0:T(8,128)(2,1)S(1)}, bf16[16,3072]{1,0:T(8,128)(2,1)}, u32[]{:S(2)}) copy-start(bf16[16,3072]{1,0:T(8,128)(2,1)} %param.8) | copy-start | bytes 294916
  6.3 9.1 %copy-start = (bf16[16,3072]{1,0:T(8,128)(2,1)S(1)}, bf16[16,3072]{1,0:T(8,128)(2,1)}, u32[]{:S(2)}) copy-start(bf16[16,3072]{1,0:T(8,128)(2,1)} %tokens) | copy-start | bytes 294916
  11.0 6.4 %collective-permute-start = (bf16[16,3072]{1,0:T(8,128)(2,1)S(1)}, bf16[16,3072]{1,0:T(8,128)(2,1)S(1)}, u32[]{:S(2)}, u32[]{:S(2)}) collective-permute-start(bf16[16,3072]{1,0:T(8,128)(2,1)S(1)} %copy-done.2), channel_id=1, source_target_pairs={{0,4},{4,0},{8,12},{12,8},{1,5},{5,1},{9,13},{13,9},{2,6},{6,2},{1... | collective-permute-start | bytes 294920 | tf_op jit(solution)/shard_map/ppermute | solution.py:235
  11.9 13.1 %collective-permute-start.1 = (bf16[16,3072]{1,0:T(8,128)(2,1)S(1)}, bf16[16,3072]{1,0:T(8,128)(2,1)S(1)}, u32[]{:S(2)}, u32[]{:S(2)}) collective-permute-start(bf16[16,3072]{1,0:T(8,128)(2,1)S(1)} %copy-done.2), channel_id=1, source_target_pairs={{0,8},{4,12},{8,0},{12,4},{1,9},{5,13},{9,1},{13,5},{2,10},{6,14},... | collective-permute-start | bytes 294920 | tf_op jit(solution)/shard_map/ppermute | solution.py:235
  15.4 9.6 %collective-permute-start.2 = (bf16[16,3072]{1,0:T(8,128)(2,1)S(1)}, bf16[16,3072]{1,0:T(8,128)(2,1)S(1)}, u32[]{:S(2)}, u32[]{:S(2)}) collective-permute-start(bf16[16,3072]{1,0:T(8,128)(2,1)S(1)} %copy-done.2), channel_id=1, source_target_pairs={{0,12},{4,8},{8,4},{12,0},{1,13},{5,9},{9,5},{13,1},{2,14},{6,10},... | collective-permute-start | bytes 294920 | tf_op jit(solution)/shard_map/ppermute | solution.py:235
  15.5 9.5 %collective-permute-start.7 = (bf16[64,3072]{1,0:T(8,128)(2,1)S(1)}, bf16[64,3072]{1,0:T(8,128)(2,1)S(1)}, u32[]{:S(2)}, u32[]{:S(2)}) collective-permute-start(bf16[64,3072]{1,0:T(8,128)(2,1)S(1)} %pad_maximum_fusion.refs_0_), channel_id=1, source_target_pairs={{0,2},{1,3},{2,0},{3,1},{4,6},{5,7},{6,4},{7,5},{8,10},{9,11},{10,... | collective-permute-start | bytes 1179656 | tf_op jit(solution)/shard_map/ppermute | solution.py:238
  17.3 9.5 %collective-permute-start.8 = (bf16[64,3072]{1,0:T(8,128)(2,1)S(1)}, bf16[64,3072]{1,0:T(8,128)(2,1)S(1)}, u32[]{:S(2)}, u32[]{:S(2)}) collective-permute-start(bf16[64,3072]{1,0:T(8,128)(2,1)S(1)} %pad_maximum_fusion.refs_0_), channel_id=1, source_target_pairs={{0,1},{1,0},{2,3},{3,2},{4,5},{5,4},{6,7},{7,6},{8,9},{9,8},{10,11... | collective-permute-start | bytes 1179656 | tf_op jit(solution)/shard_map/ppermute | solution.py:238
  25.0 1.8 %collective-permute-start.9 = (bf16[64,3072]{1,0:T(8,128)(2,1)S(1)}, bf16[64,3072]{1,0:T(8,128)(2,1)S(1)}, u32[]{:S(2)}, u32[]{:S(2)}) collective-permute-start(bf16[64,3072]{1,0:T(8,128)(2,1)S(1)} %collective-permute-done.7.refs_1_), channel_id=1, source_target_pairs={{0,1},{1,0},{2,3},{3,2},{4,5},{5,4},{6,7},{7,6},{8,9},{9,8},{10,11... | collective-permute-start | bytes 1179656 | tf_op jit(solution)/shard_map/ppermute | solution.py:238
  25.0 10.8 %collective-permute-start.3 = (bf16[64,3072]{1,0:T(8,128)(2,1)S(1)}, bf16[64,3072]{1,0:T(8,128)(2,1)S(1)}, u32[]{:S(2)}, u32[]{:S(2)}) collective-permute-start(bf16[64,3072]{1,0:T(8,128)(2,1)S(1)} %constant_dynamic-update-slice_fusion.refs_0_), channel_id=1, source_target_pairs={{0,3},{1,2},{2,1},{3,0},{4,7},{5,6},{6,5},{7,4},{8,11},{9,10},{10,... | collective-permute-start | bytes 1179656 | tf_op jit(solution)/shard_map/ppermute | solution.py:238
  26.7 9.6 %collective-permute-start.11 = (bf16[64,3072]{1,0:T(8,128)(2,1)S(1)}, bf16[64,3072]{1,0:T(8,128)(2,1)S(1)}, u32[]{:S(2)}, u32[]{:S(2)}) collective-permute-start(bf16[64,3072]{1,0:T(8,128)(2,1)S(1)} %constant_dynamic-update-slice_fusion.refs_0_), channel_id=1, source_target_pairs={{0,1},{1,0},{2,3},{3,2},{4,5},{5,4},{6,7},{7,6},{8,9},{9,8},{10,11... | collective-permute-start | bytes 1179656 | tf_op jit(solution)/shard_map/ppermute | solution.py:238
  35.9 1.8 %collective-permute-start.10 = (bf16[64,3072]{1,0:T(8,128)(2,1)S(1)}, bf16[64,3072]{1,0:T(8,128)(2,1)S(1)}, u32[]{:S(2)}, u32[]{:S(2)}) collective-permute-start(bf16[64,3072]{1,0:T(8,128)(2,1)S(1)} %collective-permute-done.3.refs_3_), channel_id=1, source_target_pairs={{0,1},{1,0},{2,3},{3,2},{4,5},{5,4},{6,7},{7,6},{8,9},{9,8},{10,11... | collective-permute-start | bytes 1179656 | tf_op jit(solution)/shard_map/ppermute | solution.py:238
  46.2 4.1 %collective-permute-start.12 = (bf16[128,1536]{1,0:T(8,128)(2,1)S(1)}, bf16[128,1536]{1,0:T(8,128)(2,1)S(1)}, u32[]{:S(2)}, u32[]{:S(2)}) collective-permute-start(bf16[128,1536]{1,0:T(8,128)(2,1)S(1)} %get-tuple-element.53), channel_id=1, source_target_pairs={{0,1},{1,0},{2,3},{3,2},{4,5},{5,4},{6,7},{7,6},{8,9},{9,8},{10,11... | collective-permute-start | bytes 1179656 | tf_op jit(solution)/shard_map/ppermute | solution.py:238
  46.6 12.4 %copy-start.1 = (bf16[3072,4]{0,1:T(4,128)(2,1)S(1)}, bf16[3072,4]{0,1:T(4,128)(2,1)}, u32[]{:S(2)}) copy-start(bf16[3072,4]{0,1:T(4,128)(2,1)} %param.10) | copy-start | bytes 73732
  46.6 12.4 %copy-start.3 = (s32[16,2]{0,1:T(2,128)S(1)}, s32[16,2]{0,1:T(2,128)}, u32[]{:S(2)}) copy-start(s32[16,2]{0,1:T(2,128)} %param.9) | copy-start | bytes 388
  50.1 1.9 %collective-permute-start.17 = (bf16[128,1664]{1,0:T(8,128)(2,1)S(1)}, bf16[128,1664]{1,0:T(8,128)(2,1)S(1)}, u32[]{:S(2)}, u32[]{:S(2)}) collective-permute-start(bf16[128,1664]{1,0:T(8,128)(2,1)S(1)} %get-tuple-element.65), channel_id=1, source_target_pairs={{0,1},{1,0},{2,3},{3,2},{4,5},{5,4},{6,7},{7,6},{8,9},{9,8},{10,11... | collective-permute-start | bytes 1277960 | tf_op jit(solution)/shard_map/ppermute | solution.py:238
  50.4 7.8 %collective-permute-start.13 = (bf16[64,1536]{1,0:T(8,128)(2,1)S(1)}, bf16[64,1536]{1,0:T(8,128)(2,1)S(1)}, u32[]{:S(2)}, u32[]{:S(2)}) collective-permute-start(bf16[64,1536]{1,0:T(8,128)(2,1)S(1)} %get-tuple-element.55), channel_id=1, source_target_pairs={{0,2},{1,3},{2,0},{3,1},{4,6},{5,7},{6,4},{7,5},{8,10},{9,11},{10,... | collective-permute-start | bytes 589832 | tf_op jit(solution)/shard_map/ppermute | solution.py:238
  52.1 10.7 %collective-permute-start.18 = (bf16[64,1664]{1,0:T(8,128)(2,1)S(1)}, bf16[64,1664]{1,0:T(8,128)(2,1)S(1)}, u32[]{:S(2)}, u32[]{:S(2)}) collective-permute-start(bf16[64,1664]{1,0:T(8,128)(2,1)S(1)} %get-tuple-element.67), channel_id=1, source_target_pairs={{0,2},{1,3},{2,0},{3,1},{4,6},{5,7},{6,4},{7,5},{8,10},{9,11},{10,... | collective-permute-start | bytes 638984 | tf_op jit(solution)/shard_map/ppermute | solution.py:238
  58.2 8.8 %collective-permute-start.14 = (bf16[16,1536]{1,0:T(8,128)(2,1)S(1)}, bf16[16,1536]{1,0:T(8,128)(2,1)S(1)}, u32[]{:S(2)}, u32[]{:S(2)}) collective-permute-start(bf16[16,1536]{1,0:T(8,128)(2,1)S(1)} %get-tuple-element.57), channel_id=1, source_target_pairs={{0,4},{4,0},{8,12},{12,8},{1,5},{5,1},{9,13},{13,9},{2,6},{6,2},{1... | collective-permute-start | bytes 147464 | tf_op jit(solution)/shard_map/ppermute | solution.py:235
  59.2 8.4 %collective-permute-start.15 = (bf16[16,1536]{1,0:T(8,128)(2,1)S(1)}, bf16[16,1536]{1,0:T(8,128)(2,1)S(1)}, u32[]{:S(2)}, u32[]{:S(2)}) collective-permute-start(bf16[16,1536]{1,0:T(8,128)(2,1)S(1)} %get-tuple-element.58), channel_id=1, source_target_pairs={{0,8},{4,12},{8,0},{12,4},{1,9},{5,13},{9,1},{13,5},{2,10},{6,14},... | collective-permute-start | bytes 147464 | tf_op jit(solution)/shard_map/ppermute | solution.py:235
  62.5 5.9 %collective-permute-start.16 = (bf16[16,1536]{1,0:T(8,128)(2,1)S(1)}, bf16[16,1536]{1,0:T(8,128)(2,1)S(1)}, u32[]{:S(2)}, u32[]{:S(2)}) collective-permute-start(bf16[16,1536]{1,0:T(8,128)(2,1)S(1)} %get-tuple-element.59), channel_id=1, source_target_pairs={{0,12},{4,8},{8,4},{12,0},{1,13},{5,9},{9,5},{13,1},{2,14},{6,10},... | collective-permute-start | bytes 147464 | tf_op jit(solution)/shard_map/ppermute | solution.py:235
  62.9 5.5 %collective-permute-start.19 = (bf16[16,1664]{1,0:T(8,128)(2,1)S(1)}, bf16[16,1664]{1,0:T(8,128)(2,1)S(1)}, u32[]{:S(2)}, u32[]{:S(2)}) collective-permute-start(bf16[16,1664]{1,0:T(8,128)(2,1)S(1)} %get-tuple-element.69), channel_id=1, source_target_pairs={{0,4},{4,0},{8,12},{12,8},{1,5},{5,1},{9,13},{13,9},{2,6},{6,2},{1... | collective-permute-start | bytes 159752 | tf_op jit(solution)/shard_map/ppermute | solution.py:235
  63.3 7.4 %collective-permute-start.20 = (bf16[16,1664]{1,0:T(8,128)(2,1)S(1)}, bf16[16,1664]{1,0:T(8,128)(2,1)S(1)}, u32[]{:S(2)}, u32[]{:S(2)}) collective-permute-start(bf16[16,1664]{1,0:T(8,128)(2,1)S(1)} %get-tuple-element.70), channel_id=1, source_target_pairs={{0,8},{4,12},{8,0},{12,4},{1,9},{5,13},{9,1},{13,5},{2,10},{6,14},... | collective-permute-start | bytes 159752 | tf_op jit(solution)/shard_map/ppermute | solution.py:235
  67.0 5.9 %collective-permute-start.21 = (bf16[16,1664]{1,0:T(8,128)(2,1)S(1)}, bf16[16,1664]{1,0:T(8,128)(2,1)S(1)}, u32[]{:S(2)}, u32[]{:S(2)}) collective-permute-start(bf16[16,1664]{1,0:T(8,128)(2,1)S(1)} %get-tuple-element.71), channel_id=1, source_target_pairs={{0,12},{4,8},{8,4},{12,0},{1,13},{5,9},{9,5},{13,1},{2,14},{6,10},... | collective-permute-start | bytes 159752 | tf_op jit(solution)/shard_map/ppermute | solution.py:235

commit v7 on v6

--- a/solution.py
+++ b/solution.py
@@ -41,9 +41,16 @@
 
 
 def load_kernel(k, source, *refs):
-    copy = pltpu.make_async_copy(source, refs[-2].at[k], refs[-1])
-    copy.start()
-    copy.wait()
+    half = source.shape[0] // 2
+    parts = [pl.ds(i * half, half) for i in range(2)]
+    copies = [
+        pltpu.make_async_copy(source.at[part], refs[-2].at[k, part], refs[-1].at[i])
+        for i, part in enumerate(parts)
+    ]
+    for copy in copies:
+        copy.start()
+    for copy in copies:
+        copy.wait()
 
 
 def gate_up_kernel(n, *refs):
@@ -270,7 +277,7 @@
     def load(k, *args):
         specs = [ANY, VMEM][: len(args)]
         alias = {1: 0} if k else {}
-        sem = [pltpu.SemaphoreType.DMA]
+        sem = [pltpu.SemaphoreType.DMA((2,))]
         (out,) = call(functools.partial(load_kernel, k), args, [pair_of], specs, sem, grant, cost(0, 0), alias)
         return vmem(out)
 

time: 74.2 us -> 74.2 us (level)
  no operation moved by 1% of the time
where the time goes in v7:
time: 74.2 us; the launch traced here: 74.1 us
  Pallas kernels  30.5 us (41%)
  starting transfers between devices  26.8 us (36%)
  waiting for transfers between devices  15.8 us (21%)
  between operations  0.82 us (1%)
    pallas_call x11, Pallas kernels, call(): pl.pallas_call(kernel, out_shape=outs, in_specs=specs, out_specs=[VMEM] *...  30.5 us
    ppermute x12, starting transfers between devices, along(): return lax.ppermute(x, 'expert', [(i, i ^ shift) for i in range(experts)])  19 us
    ppermute x10, waiting for transfers between devices, across(): return lax.ppermute(x, 'hidden', [(i, i ^ bit) for i in range(hidden)])  10.4 us
    ppermute x10, starting transfers between devices, across(): return lax.ppermute(x, 'hidden', [(i, i ^ bit) for i in range(hidden)])  7.81 us
    ppermute x12, waiting for transfers between devices, along(): return lax.ppermute(x, 'expert', [(i, i ^ shift) for i in range(experts)])  5.39 us
  transfers between devices with their start and end apart: 22, of which 7 were waited for; matrix products, arithmetic and copies ran while one was open for 0% of the time, Pallas kernels for 28%

profile of v7, /device:TPU:0, one launch (start us, length us, event | category | flops | bytes accessed | tf_op | source)
XLA Modules:
  0.0 74.1 jit_solution(874874684669921392)
XLA Ops:
  0.6 3.1 %collective-permute-start.4 = (bf16[16,3072]{1,0:T(8,128)(2,1)}, bf16[16,3072]{1,0:T(8,128)(2,1)S(1)}, u32[]{:S(2)}, u32[]{:S(2)}) collective-permute-start(bf16[16,3072]{1,0:T(8,128)(2,1)} %tokens), channel_id=1, source_target_pairs={{0,4},{4,0},{8,12},{12,8},{1,5},{5,1},{9,13},{13,9},{2,6},{6,2},{1... | collective-permute-start | bytes 294920 | tf_op jit(solution)/shard_map/ppermute | solution.py:242
  3.7 2.6 %collective-permute-start.5 = (bf16[16,3072]{1,0:T(8,128)(2,1)}, bf16[16,3072]{1,0:T(8,128)(2,1)S(1)}, u32[]{:S(2)}, u32[]{:S(2)}) collective-permute-start(bf16[16,3072]{1,0:T(8,128)(2,1)} %tokens), channel_id=1, source_target_pairs={{0,8},{4,12},{8,0},{12,4},{1,9},{5,13},{9,1},{13,5},{2,10},{6,14},... | collective-permute-start | bytes 294920 | tf_op jit(solution)/shard_map/ppermute | solution.py:242
  6.3 0.0 collective-permute-start.6
  6.3 0.0 copy-start.2
  6.3 0.0 copy-start
  6.3 4.7 %shard_map.86.refs_0_ = bf16[2,3072,2048]{2,1,0:T(8,128)(2,1)S(1)} custom-call(bf16[3072,2048]{1,0:T(8,128)(2,1)} %bitcast.9), custom_call_target="tpu_custom_call" | custom-call | tf_op jit(solution)/shard_map/pallas_call | solution.py:219
  11.0 0.0 copy-done.2
  11.0 1.0 %collective-permute-start = (bf16[16,3072]{1,0:T(8,128)(2,1)S(1)}, bf16[16,3072]{1,0:T(8,128)(2,1)S(1)}, u32[]{:S(2)}, u32[]{:S(2)}) collective-permute-start(bf16[16,3072]{1,0:T(8,128)(2,1)S(1)} %copy-done.2), channel_id=1, source_target_pairs={{0,4},{4,0},{8,12},{12,8},{1,5},{5,1},{9,13},{13,9},{2,6},{6,2},{1... | collective-permute-start | bytes 294920 | tf_op jit(solution)/shard_map/ppermute | solution.py:242
  12.0 3.5 %collective-permute-start.1 = (bf16[16,3072]{1,0:T(8,128)(2,1)S(1)}, bf16[16,3072]{1,0:T(8,128)(2,1)S(1)}, u32[]{:S(2)}, u32[]{:S(2)}) collective-permute-start(bf16[16,3072]{1,0:T(8,128)(2,1)S(1)} %copy-done.2), channel_id=1, source_target_pairs={{0,8},{4,12},{8,0},{12,4},{1,9},{5,13},{9,1},{13,5},{2,10},{6,14},... | collective-permute-start | bytes 294920 | tf_op jit(solution)/shard_map/ppermute | solution.py:242
  15.4 0.0 collective-permute-done.4
  15.4 0.0 collective-permute-start.2
  15.4 0.0 collective-permute-done.5
  15.5 0.0 collective-permute-done.6
  15.5 0.0 copy-done
  15.5 1.8 %collective-permute-start.7 = (bf16[64,3072]{1,0:T(8,128)(2,1)S(1)}, bf16[64,3072]{1,0:T(8,128)(2,1)S(1)}, u32[]{:S(2)}, u32[]{:S(2)}) collective-permute-start(bf16[64,3072]{1,0:T(8,128)(2,1)S(1)} %pad_maximum_fusion.refs_0_), channel_id=1, source_target_pairs={{0,2},{1,3},{2,0},{3,1},{4,6},{5,7},{6,4},{7,5},{8,10},{9,11},{10,... | collective-permute-start | bytes 1179656 | tf_op jit(solution)/shard_map/ppermute | solution.py:245
  17.3 0.1 collective-permute-start.8
  17.4 0.0 collective-permute-done
  17.4 4.6 %shard_map.87.refs_4_ = bf16[2,3072,2048]{2,1,0:T(8,128)(2,1)S(1)} custom-call(bf16[3072,2048]{1,0:T(8,128)(2,1)} %bitcast.10, bf16[2,3072,2048]{2,1,0:T(8,128)(2,1)S(1)} %shard_map.86.refs_0_), custom_call_target="tpu_custom_call", output_to_operand_aliasing={{}: (1, {})} | custom-call | tf_op jit(solution)/shard_map/pallas_call | solution.py:219
  22.0 3.0 %collective-permute-done.7.refs_1_ = bf16[64,3072]{1,0:T(8,128)(2,1)S(1)} collective-permute-done((bf16[64,3072]{1,0:T(8,128)(2,1)S(1)}, bf16[64,3072]{1,0:T(8,128)(2,1)S(1)}, u32[]{:S(2)}, u32[]{:S(2)}) %collective-permute-start.7) | collective-permute-done | bytes 393248 | tf_op jit(solution)/shard_map/ppermute | solution.py:245
  25.0 0.0 collective-permute-start.9
  25.0 0.0 collective-permute-done.1
  25.0 0.0 collective-permute-done.2
  25.1 1.7 %collective-permute-start.3 = (bf16[64,3072]{1,0:T(8,128)(2,1)S(1)}, bf16[64,3072]{1,0:T(8,128)(2,1)S(1)}, u32[]{:S(2)}, u32[]{:S(2)}) collective-permute-start(bf16[64,3072]{1,0:T(8,128)(2,1)S(1)} %constant_dynamic-update-slice_fusion.refs_0_), channel_id=1, source_target_pairs={{0,3},{1,2},{2,1},{3,0},{4,7},{5,6},{6,5},{7,4},{8,11},{9,10},{10,... | collective-permute-start | bytes 1179656 | tf_op jit(solution)/shard_map/ppermute | solution.py:245
  26.8 0.0 collective-permute-start.11
  26.8 0.0 collective-permute-done.8.refs_2_
  26.8 0.0 collective-permute-done.9.refs_3_
  26.8 7.6 %shard_map.88 = (f32[2,256,2048]{2,1,0:T(8,128)S(1)}, bf16[2,3072,2048]{2,1,0:T(8,128)(2,1)S(1)}, bf16[1024,3072]{1,0:T(8,128)(2,1)S(1)}) custom-call(bf16[64,3072]{1,0:T(8,128)(2,1)S(1)} %pad_maximum_fusion.refs_0_, bf16[64,3072]{1,0:T(8,128)(2,1)S(1)} %collective-permute-done.7.refs_1_, ...), custom_call_target="tpu_custom_call", output_to_operand_aliasing={{1}: (4, {})} | custom-call | flops 6442450944 | bytes 25165824 | tf_op jit(solution)/shard_map/pallas_call | solution.py:219
  34.4 1.5 %collective-permute-done.3.refs_3_ = bf16[64,3072]{1,0:T(8,128)(2,1)S(1)} collective-permute-done((bf16[64,3072]{1,0:T(8,128)(2,1)S(1)}, bf16[64,3072]{1,0:T(8,128)(2,1)S(1)}, u32[]{:S(2)}, u32[]{:S(2)}) %collective-permute-start.3) | collective-permute-done | bytes 393248 | tf_op jit(solution)/shard_map/ppermute | solution.py:245
  35.9 0.5 collective-permute-start.10
  36.4 0.0 collective-permute-done.11.refs_2_
  36.4 1.3 %collective-permute-done.10.refs_1_ = bf16[64,3072]{1,0:T(8,128)(2,1)S(1)} collective-permute-done((bf16[64,3072]{1,0:T(8,128)(2,1)S(1)}, bf16[64,3072]{1,0:T(8,128)(2,1)S(1)}, u32[]{:S(2)}, u32[]{:S(2)}) %collective-permute-start.10) | collective-permute-done | bytes 393248 | tf_op jit(solution)/shard_map/ppermute | solution.py:245
  37.7 8.5 %shard_map.89 = (f32[128,1536]{1,0:T(8,128)S(1)}, bf16[128,1536]{1,0:T(8,128)(2,1)S(1)}, bf16[2,256,2048]{2,1,0:T(8,128)(2,1)S(1)}, f32[256,1]{1,0:T(8,128)S(1)}, bf16[2,3072,2048]{2,1,0:T(8,128)(2,1)S(1)}) custom-call(bf16[64,3072]{1,0:T(8,128)(2,1)S(1)} %constant_dynamic-update-slice_fusion.refs_0_, ...), custom_call_target="tpu_custom_call", output_to_operand_aliasing={{4}: (4, {})} | custom-call | flops 6442450944 | bytes 37748736 | tf_op jit(solution)/shard_map/pallas_call | solution.py:219
  46.2 0.4 collective-permute-start.12
  46.7 0.0 copy-start.1
  46.7 0.0 copy-start.3
  46.7 3.4 %shard_map.92 = (f32[128,1664]{1,0:T(8,128)S(1)}, bf16[128,1664]{1,0:T(8,128)(2,1)S(1)}) custom-call(bf16[2,3072,2048]{2,1,0:T(8,128)(2,1)S(1)} %get-tuple-element.60.weights, bf16[2,256,2048]{2,1,0:T(8,128)(2,1)S(1)} %get-tuple-element.61.grads, f32[256,1]{1,0:T(8,128)S(1)} %get-tuple-element.62.score), custom_call_target="tpu_custom_call" | custom-call | flops 3221225472 | bytes 12582912 | tf_op jit(solution)/shard_map/pallas_call | solution.py:219
  50.1 0.2 collective-permute-start.17
  50.3 0.0 collective-permute-done.12.theirs
  50.3 0.1 shard_map.90
  50.4 1.6 %collective-permute-start.13 = (bf16[64,1536]{1,0:T(8,128)(2,1)S(1)}, bf16[64,1536]{1,0:T(8,128)(2,1)S(1)}, u32[]{:S(2)}, u32[]{:S(2)}) collective-permute-start(bf16[64,1536]{1,0:T(8,128)(2,1)S(1)} %get-tuple-element.55), channel_id=1, source_target_pairs={{0,2},{1,3},{2,0},{3,1},{4,6},{5,7},{6,4},{7,5},{8,10},{9,11},{10,... | collective-permute-start | bytes 589832 | tf_op jit(solution)/shard_map/ppermute | solution.py:245
  52.0 0.0 collective-permute-done.17.theirs
  52.0 0.1 shard_map.93
  52.1 1.5 %collective-permute-start.18 = (bf16[64,1664]{1,0:T(8,128)(2,1)S(1)}, bf16[64,1664]{1,0:T(8,128)(2,1)S(1)}, u32[]{:S(2)}, u32[]{:S(2)}) collective-permute-start(bf16[64,1664]{1,0:T(8,128)(2,1)S(1)} %get-tuple-element.67), channel_id=1, source_target_pairs={{0,2},{1,3},{2,0},{3,1},{4,6},{5,7},{6,4},{7,5},{8,10},{9,11},{10,... | collective-permute-start | bytes 638984 | tf_op jit(solution)/shard_map/ppermute | solution.py:245
  53.7 4.5 %collective-permute-done.13.theirs = bf16[64,1536]{1,0:T(8,128)(2,1)S(1)} collective-permute-done((bf16[64,1536]{1,0:T(8,128)(2,1)S(1)}, bf16[64,1536]{1,0:T(8,128)(2,1)S(1)}, u32[]{:S(2)}, u32[]{:S(2)}) %collective-permute-start.13) | collective-permute-done | bytes 196640 | tf_op jit(solution)/shard_map/ppermute | solution.py:245
  58.2 0.8 %collective-permute-start.14 = (bf16[16,1536]{1,0:T(8,128)(2,1)S(1)}, bf16[16,1536]{1,0:T(8,128)(2,1)S(1)}, u32[]{:S(2)}, u32[]{:S(2)}) collective-permute-start(bf16[16,1536]{1,0:T(8,128)(2,1)S(1)} %get-tuple-element.57), channel_id=1, source_target_pairs={{0,4},{4,0},{8,12},{12,8},{1,5},{5,1},{9,13},{13,9},{2,6},{6,2},{1... | collective-permute-start | bytes 147464 | tf_op jit(solution)/shard_map/ppermute | solution.py:242
  59.1 0.0 copy-done.1
  59.1 0.0 copy-done.3
  59.1 0.1 copy.16.routes
  59.2 3.3 %collective-permute-start.15 = (bf16[16,1536]{1,0:T(8,128)(2,1)S(1)}, bf16[16,1536]{1,0:T(8,128)(2,1)S(1)}, u32[]{:S(2)}, u32[]{:S(2)}) collective-permute-start(bf16[16,1536]{1,0:T(8,128)(2,1)S(1)} %get-tuple-element.58), channel_id=1, source_target_pairs={{0,8},{4,12},{8,0},{12,4},{1,9},{5,13},{9,1},{13,5},{2,10},{6,14},... | collective-permute-start | bytes 147464 | tf_op jit(solution)/shard_map/ppermute | solution.py:242
  62.5 0.3 collective-permute-start.16
  62.8 0.0 collective-permute-done.18.theirs
  62.8 0.1 shard_map.94
  62.9 0.4 collective-permute-start.19
  63.3 3.7 %collective-permute-start.20 = (bf16[16,1664]{1,0:T(8,128)(2,1)S(1)}, bf16[16,1664]{1,0:T(8,128)(2,1)S(1)}, u32[]{:S(2)}, u32[]{:S(2)}) collective-permute-start(bf16[16,1664]{1,0:T(8,128)(2,1)S(1)} %get-tuple-element.70), channel_id=1, source_target_pairs={{0,8},{4,12},{8,0},{12,4},{1,9},{5,13},{9,1},{13,5},{2,10},{6,14},... | collective-permute-start | bytes 159752 | tf_op jit(solution)/shard_map/ppermute | solution.py:242
  67.1 0.0 collective-permute-done.14.refs_1_
  67.1 0.3 collective-permute-start.21
  67.4 0.2 shard_map.95
  67.6 0.0 collective-permute-done.15.refs_2_
  67.6 0.8 %collective-permute-done.16.refs_3_ = bf16[16,1536]{1,0:T(8,128)(2,1)S(1)} collective-permute-done((bf16[16,1536]{1,0:T(8,128)(2,1)S(1)}, bf16[16,1536]{1,0:T(8,128)(2,1)S(1)}, u32[]{:S(2)}, u32[]{:S(2)}) %collective-permute-start.16) | collective-permute-done | bytes 49184 | tf_op jit(solution)/shard_map/ppermute | solution.py:242
  68.5 0.0 collective-permute-done.19.refs_5_
  68.5 2.2 %collective-permute-done.20.refs_6_ = bf16[16,1664]{1,0:T(8,128)(2,1)S(1)} collective-permute-done((bf16[16,1664]{1,0:T(8,128)(2,1)S(1)}, bf16[16,1664]{1,0:T(8,128)(2,1)S(1)}, u32[]{:S(2)}, u32[]{:S(2)}) %collective-permute-start.20) | collective-permute-done | bytes 53280 | tf_op jit(solution)/shard_map/ppermute | solution.py:242
  70.7 2.3 %collective-permute-done.21.refs_7_ = bf16[16,1664]{1,0:T(8,128)(2,1)S(1)} collective-permute-done((bf16[16,1664]{1,0:T(8,128)(2,1)S(1)}, bf16[16,1664]{1,0:T(8,128)(2,1)S(1)}, u32[]{:S(2)}, u32[]{:S(2)}) %collective-permute-start.21) | collective-permute-done | bytes 53280 | tf_op jit(solution)/shard_map/ppermute | solution.py:242
  73.0 1.1 %shard_map.96 = (bf16[16,3072]{1,0:T(8,128)(2,1)}, f32[2,16]{1,0:T(2,128)}) custom-call(f32[16,1536]{1,0:T(8,128)S(1)} %get-tuple-element.56.refs_0_, bf16[16,1536]{1,0:T(8,128)(2,1)S(1)} %collective-permute-done.14.refs_1_, bf16[16,1536]{1,0:T(8,128)(2,1)S(1)} %collective-permute-done.15.refs_2_, bf16[16,1536]{1,0:T(8,128)(2,1)S(1)} %collective-permute-done.16.refs_3_, ...), custom_call_target="tpu_custom_call" | custom-call | tf_op jit(solution)/shard_map/pallas_call | solution.py:219
  (8 shorter events, 0.1 us)
Async XLA Ops:
  0.6 14.8 %collective-permute-start.4 = (bf16[16,3072]{1,0:T(8,128)(2,1)}, bf16[16,3072]{1,0:T(8,128)(2,1)S(1)}, u32[]{:S(2)}, u32[]{:S(2)}) collective-permute-start(bf16[16,3072]{1,0:T(8,128)(2,1)} %tokens), channel_id=1, source_target_pairs={{0,4},{4,0},{8,12},{12,8},{1,5},{5,1},{9,13},{13,9},{2,6},{6,2},{1... | collective-permute-start | bytes 294920 | tf_op jit(solution)/shard_map/ppermute | solution.py:242
  3.7 11.7 %collective-permute-start.5 = (bf16[16,3072]{1,0:T(8,128)(2,1)}, bf16[16,3072]{1,0:T(8,128)(2,1)S(1)}, u32[]{:S(2)}, u32[]{:S(2)}) collective-permute-start(bf16[16,3072]{1,0:T(8,128)(2,1)} %tokens), channel_id=1, source_target_pairs={{0,8},{4,12},{8,0},{12,4},{1,9},{5,13},{9,1},{13,5},{2,10},{6,14},... | collective-permute-start | bytes 294920 | tf_op jit(solution)/shard_map/ppermute | solution.py:242
  6.3 9.1 %collective-permute-start.6 = (bf16[16,3072]{1,0:T(8,128)(2,1)}, bf16[16,3072]{1,0:T(8,128)(2,1)S(1)}, u32[]{:S(2)}, u32[]{:S(2)}) collective-permute-start(bf16[16,3072]{1,0:T(8,128)(2,1)} %tokens), channel_id=1, source_target_pairs={{0,12},{4,8},{8,4},{12,0},{1,13},{5,9},{9,5},{13,1},{2,14},{6,10},... | collective-permute-start | bytes 294920 | tf_op jit(solution)/shard_map/ppermute | solution.py:242
  6.3 4.7 %copy-start.2 = (bf16[16,3072]{1,0:T(8,128)(2,1)S(1)}, bf16[16,3072]{1,0:T(8,128)(2,1)}, u32[]{:S(2)}) copy-start(bf16[16,3072]{1,0:T(8,128)(2,1)} %param.8) | copy-start | bytes 294916
  6.3 9.2 %copy-start = (bf16[16,3072]{1,0:T(8,128)(2,1)S(1)}, bf16[16,3072]{1,0:T(8,128)(2,1)}, u32[]{:S(2)}) copy-start(bf16[16,3072]{1,0:T(8,128)(2,1)} %tokens) | copy-start | bytes 294916
  11.0 6.4 %collective-permute-start = (bf16[16,3072]{1,0:T(8,128)(2,1)S(1)}, bf16[16,3072]{1,0:T(8,128)(2,1)S(1)}, u32[]{:S(2)}, u32[]{:S(2)}) collective-permute-start(bf16[16,3072]{1,0:T(8,128)(2,1)S(1)} %copy-done.2), channel_id=1, source_target_pairs={{0,4},{4,0},{8,12},{12,8},{1,5},{5,1},{9,13},{13,9},{2,6},{6,2},{1... | collective-permute-start | bytes 294920 | tf_op jit(solution)/shard_map/ppermute | solution.py:242
  12.0 13.1 %collective-permute-start.1 = (bf16[16,3072]{1,0:T(8,128)(2,1)S(1)}, bf16[16,3072]{1,0:T(8,128)(2,1)S(1)}, u32[]{:S(2)}, u32[]{:S(2)}) collective-permute-start(bf16[16,3072]{1,0:T(8,128)(2,1)S(1)} %copy-done.2), channel_id=1, source_target_pairs={{0,8},{4,12},{8,0},{12,4},{1,9},{5,13},{9,1},{13,5},{2,10},{6,14},... | collective-permute-start | bytes 294920 | tf_op jit(solution)/shard_map/ppermute | solution.py:242
  15.4 9.6 %collective-permute-start.2 = (bf16[16,3072]{1,0:T(8,128)(2,1)S(1)}, bf16[16,3072]{1,0:T(8,128)(2,1)S(1)}, u32[]{:S(2)}, u32[]{:S(2)}) collective-permute-start(bf16[16,3072]{1,0:T(8,128)(2,1)S(1)} %copy-done.2), channel_id=1, source_target_pairs={{0,12},{4,8},{8,4},{12,0},{1,13},{5,9},{9,5},{13,1},{2,14},{6,10},... | collective-permute-start | bytes 294920 | tf_op jit(solution)/shard_map/ppermute | solution.py:242
  15.5 9.5 %collective-permute-start.7 = (bf16[64,3072]{1,0:T(8,128)(2,1)S(1)}, bf16[64,3072]{1,0:T(8,128)(2,1)S(1)}, u32[]{:S(2)}, u32[]{:S(2)}) collective-permute-start(bf16[64,3072]{1,0:T(8,128)(2,1)S(1)} %pad_maximum_fusion.refs_0_), channel_id=1, source_target_pairs={{0,2},{1,3},{2,0},{3,1},{4,6},{5,7},{6,4},{7,5},{8,10},{9,11},{10,... | collective-permute-start | bytes 1179656 | tf_op jit(solution)/shard_map/ppermute | solution.py:245
  17.3 9.5 %collective-permute-start.8 = (bf16[64,3072]{1,0:T(8,128)(2,1)S(1)}, bf16[64,3072]{1,0:T(8,128)(2,1)S(1)}, u32[]{:S(2)}, u32[]{:S(2)}) collective-permute-start(bf16[64,3072]{1,0:T(8,128)(2,1)S(1)} %pad_maximum_fusion.refs_0_), channel_id=1, source_target_pairs={{0,1},{1,0},{2,3},{3,2},{4,5},{5,4},{6,7},{7,6},{8,9},{9,8},{10,11... | collective-permute-start | bytes 1179656 | tf_op jit(solution)/shard_map/ppermute | solution.py:245
  25.0 1.8 %collective-permute-start.9 = (bf16[64,3072]{1,0:T(8,128)(2,1)S(1)}, bf16[64,3072]{1,0:T(8,128)(2,1)S(1)}, u32[]{:S(2)}, u32[]{:S(2)}) collective-permute-start(bf16[64,3072]{1,0:T(8,128)(2,1)S(1)} %collective-permute-done.7.refs_1_), channel_id=1, source_target_pairs={{0,1},{1,0},{2,3},{3,2},{4,5},{5,4},{6,7},{7,6},{8,9},{9,8},{10,11... | collective-permute-start | bytes 1179656 | tf_op jit(solution)/shard_map/ppermute | solution.py:245
  25.1 10.8 %collective-permute-start.3 = (bf16[64,3072]{1,0:T(8,128)(2,1)S(1)}, bf16[64,3072]{1,0:T(8,128)(2,1)S(1)}, u32[]{:S(2)}, u32[]{:S(2)}) collective-permute-start(bf16[64,3072]{1,0:T(8,128)(2,1)S(1)} %constant_dynamic-update-slice_fusion.refs_0_), channel_id=1, source_target_pairs={{0,3},{1,2},{2,1},{3,0},{4,7},{5,6},{6,5},{7,4},{8,11},{9,10},{10,... | collective-permute-start | bytes 1179656 | tf_op jit(solution)/shard_map/ppermute | solution.py:245
  26.8 9.6 %collective-permute-start.11 = (bf16[64,3072]{1,0:T(8,128)(2,1)S(1)}, bf16[64,3072]{1,0:T(8,128)(2,1)S(1)}, u32[]{:S(2)}, u32[]{:S(2)}) collective-permute-start(bf16[64,3072]{1,0:T(8,128)(2,1)S(1)} %constant_dynamic-update-slice_fusion.refs_0_), channel_id=1, source_target_pairs={{0,1},{1,0},{2,3},{3,2},{4,5},{5,4},{6,7},{7,6},{8,9},{9,8},{10,11... | collective-permute-start | bytes 1179656 | tf_op jit(solution)/shard_map/ppermute | solution.py:245
  35.9 1.8 %collective-permute-start.10 = (bf16[64,3072]{1,0:T(8,128)(2,1)S(1)}, bf16[64,3072]{1,0:T(8,128)(2,1)S(1)}, u32[]{:S(2)}, u32[]{:S(2)}) collective-permute-start(bf16[64,3072]{1,0:T(8,128)(2,1)S(1)} %collective-permute-done.3.refs_3_), channel_id=1, source_target_pairs={{0,1},{1,0},{2,3},{3,2},{4,5},{5,4},{6,7},{7,6},{8,9},{9,8},{10,11... | collective-permute-start | bytes 1179656 | tf_op jit(solution)/shard_map/ppermute | solution.py:245
  46.2 4.1 %collective-permute-start.12 = (bf16[128,1536]{1,0:T(8,128)(2,1)S(1)}, bf16[128,1536]{1,0:T(8,128)(2,1)S(1)}, u32[]{:S(2)}, u32[]{:S(2)}) collective-permute-start(bf16[128,1536]{1,0:T(8,128)(2,1)S(1)} %get-tuple-element.53), channel_id=1, source_target_pairs={{0,1},{1,0},{2,3},{3,2},{4,5},{5,4},{6,7},{7,6},{8,9},{9,8},{10,11... | collective-permute-start | bytes 1179656 | tf_op jit(solution)/shard_map/ppermute | solution.py:245
  46.7 12.4 %copy-start.1 = (bf16[3072,4]{0,1:T(4,128)(2,1)S(1)}, bf16[3072,4]{0,1:T(4,128)(2,1)}, u32[]{:S(2)}) copy-start(bf16[3072,4]{0,1:T(4,128)(2,1)} %param.10) | copy-start | bytes 73732
  46.7 12.4 %copy-start.3 = (s32[16,2]{0,1:T(2,128)S(1)}, s32[16,2]{0,1:T(2,128)}, u32[]{:S(2)}) copy-start(s32[16,2]{0,1:T(2,128)} %param.9) | copy-start | bytes 388
  50.1 1.9 %collective-permute-start.17 = (bf16[128,1664]{1,0:T(8,128)(2,1)S(1)}, bf16[128,1664]{1,0:T(8,128)(2,1)S(1)}, u32[]{:S(2)}, u32[]{:S(2)}) collective-permute-start(bf16[128,1664]{1,0:T(8,128)(2,1)S(1)} %get-tuple-element.65), channel_id=1, source_target_pairs={{0,1},{1,0},{2,3},{3,2},{4,5},{5,4},{6,7},{7,6},{8,9},{9,8},{10,11... | collective-permute-start | bytes 1277960 | tf_op jit(solution)/shard_map/ppermute | solution.py:245
  50.4 7.8 %collective-permute-start.13 = (bf16[64,1536]{1,0:T(8,128)(2,1)S(1)}, bf16[64,1536]{1,0:T(8,128)(2,1)S(1)}, u32[]{:S(2)}, u32[]{:S(2)}) collective-permute-start(bf16[64,1536]{1,0:T(8,128)(2,1)S(1)} %get-tuple-element.55), channel_id=1, source_target_pairs={{0,2},{1,3},{2,0},{3,1},{4,6},{5,7},{6,4},{7,5},{8,10},{9,11},{10,... | collective-permute-start | bytes 589832 | tf_op jit(solution)/shard_map/ppermute | solution.py:245
  52.1 10.7 %collective-permute-start.18 = (bf16[64,1664]{1,0:T(8,128)(2,1)S(1)}, bf16[64,1664]{1,0:T(8,128)(2,1)S(1)}, u32[]{:S(2)}, u32[]{:S(2)}) collective-permute-start(bf16[64,1664]{1,0:T(8,128)(2,1)S(1)} %get-tuple-element.67), channel_id=1, source_target_pairs={{0,2},{1,3},{2,0},{3,1},{4,6},{5,7},{6,4},{7,5},{8,10},{9,11},{10,... | collective-permute-start | bytes 638984 | tf_op jit(solution)/shard_map/ppermute | solution.py:245
  58.2 8.8 %collective-permute-start.14 = (bf16[16,1536]{1,0:T(8,128)(2,1)S(1)}, bf16[16,1536]{1,0:T(8,128)(2,1)S(1)}, u32[]{:S(2)}, u32[]{:S(2)}) collective-permute-start(bf16[16,1536]{1,0:T(8,128)(2,1)S(1)} %get-tuple-element.57), channel_id=1, source_target_pairs={{0,4},{4,0},{8,12},{12,8},{1,5},{5,1},{9,13},{13,9},{2,6},{6,2},{1... | collective-permute-start | bytes 147464 | tf_op jit(solution)/shard_map/ppermute | solution.py:242
  59.2 8.5 %collective-permute-start.15 = (bf16[16,1536]{1,0:T(8,128)(2,1)S(1)}, bf16[16,1536]{1,0:T(8,128)(2,1)S(1)}, u32[]{:S(2)}, u32[]{:S(2)}) collective-permute-start(bf16[16,1536]{1,0:T(8,128)(2,1)S(1)} %get-tuple-element.58), channel_id=1, source_target_pairs={{0,8},{4,12},{8,0},{12,4},{1,9},{5,13},{9,1},{13,5},{2,10},{6,14},... | collective-permute-start | bytes 147464 | tf_op jit(solution)/shard_map/ppermute | solution.py:242
  62.5 5.9 %collective-permute-start.16 = (bf16[16,1536]{1,0:T(8,128)(2,1)S(1)}, bf16[16,1536]{1,0:T(8,128)(2,1)S(1)}, u32[]{:S(2)}, u32[]{:S(2)}) collective-permute-start(bf16[16,1536]{1,0:T(8,128)(2,1)S(1)} %get-tuple-element.59), channel_id=1, source_target_pairs={{0,12},{4,8},{8,4},{12,0},{1,13},{5,9},{9,5},{13,1},{2,14},{6,10},... | collective-permute-start | bytes 147464 | tf_op jit(solution)/shard_map/ppermute | solution.py:242
  62.9 5.5 %collective-permute-start.19 = (bf16[16,1664]{1,0:T(8,128)(2,1)S(1)}, bf16[16,1664]{1,0:T(8,128)(2,1)S(1)}, u32[]{:S(2)}, u32[]{:S(2)}) collective-permute-start(bf16[16,1664]{1,0:T(8,128)(2,1)S(1)} %get-tuple-element.69), channel_id=1, source_target_pairs={{0,4},{4,0},{8,12},{12,8},{1,5},{5,1},{9,13},{13,9},{2,6},{6,2},{1... | collective-permute-start | bytes 159752 | tf_op jit(solution)/shard_map/ppermute | solution.py:242
  63.3 7.4 %collective-permute-start.20 = (bf16[16,1664]{1,0:T(8,128)(2,1)S(1)}, bf16[16,1664]{1,0:T(8,128)(2,1)S(1)}, u32[]{:S(2)}, u32[]{:S(2)}) collective-permute-start(bf16[16,1664]{1,0:T(8,128)(2,1)S(1)} %get-tuple-element.70), channel_id=1, source_target_pairs={{0,8},{4,12},{8,0},{12,4},{1,9},{5,13},{9,1},{13,5},{2,10},{6,14},... | collective-permute-start | bytes 159752 | tf_op jit(solution)/shard_map/ppermute | solution.py:242
  67.1 5.9 %collective-permute-start.21 = (bf16[16,1664]{1,0:T(8,128)(2,1)S(1)}, bf16[16,1664]{1,0:T(8,128)(2,1)S(1)}, u32[]{:S(2)}, u32[]{:S(2)}) collective-permute-start(bf16[16,1664]{1,0:T(8,128)(2,1)S(1)} %get-tuple-element.71), channel_id=1, source_target_pairs={{0,12},{4,8},{8,4},{12,0},{1,13},{5,9},{9,5},{13,1},{2,14},{6,10},... | collective-permute-start | bytes 159752 | tf_op jit(solution)/shard_map/ppermute | solution.py:242
